TPU v7x, 256 devices: a whole 4x4x8 slice. The times are simulated.
256 devices in a mesh: comp: 32 (over y, x, core), tile: 8 (over z).
Axes of the slice: x: 4, y: 4, z: 8, core: 2. Of those that a mesh axis runs over, the one named last changes fastest.
Arguments:
- spectrum: float32 [864, 256, 512], P('comp', 'tile'), may hold values from 0.1 to 2
- speed: float32 [864], P('comp'), may hold values from 0.2 to 0.7
- depth: float32 [256, 512], P('tile'), may hold values from 0.5 to 1.2
- turn: float32 [256, 512], P('tile'), may hold values from -4 to 4
- sea_mask: int32 [256, 512], P('tile'), may hold values from 0 to 1, as said below
- refraction: float32 [24], replicated, may hold values from 0.1 to 0.6
- growth: float32 [864], replicated, may hold values from 0.1 to 1
- dissipation: float32 [864], replicated, may hold values from 0.1 to 1
- quad_first: bfloat16 [864, 864], replicated, may hold values from -0.21875 to 0.21875
- quad_second: bfloat16 [864, 864], replicated, may hold values from -0.21875 to 0.21875
Outputs:
- updated: float32 [864, 256, 512], P('comp', 'tile')
Inputs may be any that keep to these rules, and one draw needn't show every extreme that they name: `sea_mask`: sea fractions vary from row to row and from tile to tile; a grid row may be wholly sea or wholly land.
All inputs are finite; a program needn't handle non-finite values.
Results may differ from a plain program's by a relative error of at most 0.00088.
Values sent between devices are 32-bit elements; how exact they have to be, the bound alone decides.
No kernel may reach another device: no remote copies, remote signals or barrier semaphores. Data moves between devices by JAX's collectives and lax.ppermute only.
A program may use at most 192 MiB of HBM per device.

v0:
```python
import math

import jax
import jax.numpy as jnp
from jax import lax
from jax.sharding import PartitionSpec as P

NTH = 36


def padded_2(block, sides, width):
    for axis, dim in sides:
        count = lax.axis_size(axis)
        forward = [(i, i + 1) for i in range(count - 1)]
        backward = [(target, source) for source, target in forward]
        low = lax.ppermute(
            lax.slice_in_dim(block, block.shape[dim] - width, None, axis=dim), axis, forward
        )
        high = lax.ppermute(lax.slice_in_dim(block, 0, width, axis=dim), axis, backward)
        block = jnp.concatenate([low, block, high], axis=dim)
    return block


def third(padded, velocity, axis):
    count = padded.shape[axis] - 4
    back_two = lax.slice_in_dim(padded, 0, count, axis=axis)
    back_one = lax.slice_in_dim(padded, 1, count + 1, axis=axis)
    centre = lax.slice_in_dim(padded, 2, count + 2, axis=axis)
    ahead_one = lax.slice_in_dim(padded, 3, count + 3, axis=axis)
    ahead_two = lax.slice_in_dim(padded, 4, count + 4, axis=axis)
    positive = (2.0 * ahead_one + 3.0 * centre - 6.0 * back_one + back_two) / 6.0
    negative = (-ahead_two + 6.0 * ahead_one - 3.0 * centre - 2.0 * back_one) / 6.0
    return jnp.where(velocity >= 0.0, positive, negative)


def sources(flat, turn_flat, mask_flat, refraction, growth, dissipation, quad_first, quad_second):
    nfreq = refraction.shape[0]
    ncomp, npts = flat.shape
    grid = flat.reshape(nfreq, ncomp // nfreq, npts)
    rate = refraction[:, None, None] * turn_flat[None, None, :]
    ahead_one = jnp.roll(grid, -1, axis=1)
    ahead_two = jnp.roll(grid, -2, axis=1)
    back_one = jnp.roll(grid, 1, axis=1)
    back_two = jnp.roll(grid, 2, axis=1)
    positive = (2.0 * ahead_one + 3.0 * grid - 6.0 * back_one + back_two) / 6.0
    negative = (-ahead_two + 6.0 * ahead_one - 3.0 * grid - 2.0 * back_one) / 6.0
    turned = (grid - rate * jnp.where(rate >= 0.0, positive, negative)).reshape(ncomp, npts)
    low = turned.astype(jnp.bfloat16)
    partner = jnp.dot(quad_first, low, preferred_element_type=jnp.float32)
    pair = (turned * partner).astype(jnp.bfloat16)
    nonlinear = jnp.dot(quad_second, pair, preferred_element_type=jnp.float32)
    energy = jnp.mean(turned, axis=0)
    total = growth[:, None] * turned + nonlinear - dissipation[:, None] * turned * energy[None, :]
    return mask_flat[None, :] * (turned + 0.2 * total)


def shards(
    spectrum, speed, depth, turn, sea_mask, refraction, growth, dissipation, quad_first, quad_second
):
    comp_count = lax.axis_size("comp")
    held = spectrum.shape[0]
    tile_rows = spectrum.shape[1]
    global_comp = lax.axis_index("comp") * held + jnp.arange(held, dtype=jnp.int32)
    theta = 2.0 * math.pi / NTH * (global_comp % NTH).astype(jnp.float32)
    vel_x = speed[:, None, None] * jnp.cos(theta)[:, None, None] * depth[None]
    vel_y = speed[:, None, None] * jnp.sin(theta)[:, None, None] * depth[None]
    pad_y = padded_2(spectrum, (("tile", 1),), 2)
    pad_x = jnp.pad(spectrum, ((0, 0), (0, 0), (2, 2)))
    moved = spectrum - vel_x * third(pad_x, vel_x, 2) - vel_y * third(pad_y, vel_y, 1)
    mask_float = sea_mask.astype(jnp.float32)
    points = lax.all_to_all(moved, "comp", split_axis=1, concat_axis=0, tiled=True)
    span = tile_rows // comp_count
    first = lax.axis_index("comp") * span
    turn_here = lax.dynamic_slice_in_dim(turn, first, span, 0)
    mask_here = lax.dynamic_slice_in_dim(mask_float, first, span, 0)
    total_comp = points.shape[0]
    result = sources(
        points.reshape(total_comp, -1),
        turn_here.reshape(-1),
        mask_here.reshape(-1),
        refraction,
        growth,
        dissipation,
        quad_first,
        quad_second,
    ).reshape(points.shape)
    updated = lax.all_to_all(result, "comp", split_axis=0, concat_axis=1, tiled=True)
    return updated


def solution(mesh):
    in_specs = (
        P("comp", "tile", None),
        P("comp"),
        P("tile", None),
        P("tile", None),
        P("tile", None),
        P(),
        P(),
        P(),
        P(),
        P(),
    )
    out_specs = P("comp", "tile", None)
    return jax.shard_map(shards, mesh=mesh, in_specs=in_specs, out_specs=out_specs, check_vma=False)
```

profile of v0, /device:TPU:97, one launch (start us, length us, event | category | flops | bytes accessed | tf_op | source)
XLA Modules:
  0.0 149.8 jit_solution(5304127063780550233)
XLA Ops:
  0.0 2.7 %copy.31 = f32[27,32,512]{2,0,1:T(8,128)S(1)} copy(f32[27,32,512]{2,1,0:T(8,128)} %param.10) | data formatting | bytes 3538944 | tf_op args[0]
  2.7 1.3 copy-done.1
  4.7 4.7 %collective-permute-start.1 = (f32[27,2,512]{2,0,1:T(8,128)}, f32[27,2,512]{2,0,1:T(8,128)}, u32[]{:S(2)}, u32[]{:S(2)}) collective-permute-start(f32[27,2,512]{2,0,1:T(8,128)} %get-tuple-element.5), channel_id=1, source_target_pairs={{0,1},{1,2},{2,3},{3,4},{4,5},{5,6},{6,7},{8,9},{9,10},{10,11},{11... | collective-permute-start | bytes 331784 | tf_op jit(solution)/shard_map/ppermute | solution.py:16
  9.5 1.9 %collective-permute-start = (f32[27,2,512]{2,0,1:T(8,128)}, f32[27,2,512]{2,0,1:T(8,128)S(1)}, u32[]{:S(2)}, u32[]{:S(2)}) collective-permute-start(f32[27,2,512]{2,0,1:T(8,128)} %get-tuple-element.6), channel_id=1, source_target_pairs={{1,0},{2,1},{3,2},{4,3},{5,4},{6,5},{7,6},{9,8},{10,9},{11,10},{12... | collective-permute-start | bytes 331784 | tf_op jit(solution)/shard_map/ppermute | solution.py:19
  12.9 1.0 copy_dynamic-update-slice_fusion.1
  14.0 2.7 %collective-permute-done = f32[27,2,512]{2,0,1:T(8,128)S(1)} collective-permute-done((f32[27,2,512]{2,0,1:T(8,128)}, f32[27,2,512]{2,0,1:T(8,128)S(1)}, u32[]{:S(2)}, u32[]{:S(2)}) %collective-permute-start) | collective-permute-done | bytes 110624 | tf_op jit(solution)/shard_map/ppermute | solution.py:19
  16.7 4.1 %fusion.9 = f32[27,32,512]{2,0,1:T(8,128)} fusion(f32[27,32,512]{2,0,1:T(8,128)S(1)} %copy-done.2, f32[27,34,512]{2,0,1:T(8,128)S(1)} %constant_dynamic-update-slice_fusion, f32[27,34,512]{2,0,1:T(8,128)S(1)} %get-tuple-element.19, f32[27]{0:T(128)S(1)} %get-tuple-element.22, f32[32,512]{1,0:T(8,128)S(1)} %copy-done.5, f32[27]{0:T(128)S(1)} %get-tuple-element.21), kind=kLoop, calls=%fused_computation.17 | loop fusion | flops 16367616 | bytes 10682584 | tf_op jit(solution)/shard_map/sub | solution.py:69
  20.8 9.4 %all-to-all-start = ((f32[27,32,512]{2,0,1:T(8,128)}), f32[27,32,512]{2,0,1:T(8,128)}, u32[]{:S(2)}, u32[]{:S(2)}) async-start(f32[27,32,512]{2,0,1:T(8,128)} %fusion.9), calls=%async_computation | async-start | bytes 4194304 | tf_op jit(solution)/shard_map/all_to_all | solution.py:71
  31.2 1.5 %mul.270 = f32[32,27,1,512]{3,1,0,2:T(8,128)} reshape(f32[24,36,512]{2,1,0:T(8,128)S(1)} %mul.254) | data formatting | bytes 3538944 | tf_op jit(solution)/shard_map/mul | solution.py:47
  32.8 1.4 mul.255
  34.4 1.2 broadcast_in_dim.14
  37.3 20.8 %all-to-all-done = f32[27,32,512]{2,0,1:T(8,128)} async-done(((f32[27,32,512]{2,0,1:T(8,128)}), f32[27,32,512]{2,0,1:T(8,128)}, u32[]{:S(2)}, u32[]{:S(2)}) %all-to-all-start) | async-done | bytes 1769504 | tf_op jit(solution)/shard_map/all_to_all | solution.py:71
  58.1 1.6 %reshape_reshape.6 = f32[24,36,512]{2,1,0:T(8,128)S(1)} reshape(f32[32,27,1,512]{3,1,0,2:T(8,128)} %bitcast.2) | data formatting | bytes 3538944 | tf_op jit(solution)/shard_map/reshape;reshape | solution.py:39
  59.7 1.7 %fusion.43 = (f32[24,34,512]{2,1,0:T(8,128)}, f32[24,34,512]{2,1,0:T(8,128)S(1)}) fusion(f32[24,36,512]{2,1,0:T(8,128)S(1)} %reshape_reshape.6), kind=kLoop, calls=%fused_computation.70 | loop fusion | bytes 6684672 | tf_op jit(solution)/shard_map/jit(_roll_static)/slice | solution.py:44
  62.7 3.4 %fusion.27 = (f32[24,36,512]{2,1,0:T(8,128)}, f32[24,36,512]{2,1,0:T(8,128)S(1)}, f32[24,36,512]{2,1,0:T(8,128)}, f32[24,36,512]{2,1,0:T(8,128)}) fusion(f32[24,35,512]{2,1,0:T(8,128)S(1)} %get-tuple-element.16, f32[24,1,512]{2,1,0:T(1,128)S(1)} %get-tuple-element.18, f32[24,1,512]{2,1,0:T(1,128)S(1)} %get-tuple-element.17, ...), kind=kLoop, calls=%fused_computation.47 | loop fusion | flops 3981312 | bytes 12386304 | tf_op jit(solution)/shard_map/mul | solution.py:45
  66.1 2.8 %add.90 = f32[32,27,1,512]{3,1,0,2:T(8,128)} reshape(f32[24,36,512]{2,1,0:T(8,128)} %get-tuple-element.23) | data formatting | bytes 3538944 | tf_op jit(solution)/shard_map/add | solution.py:46
  68.9 2.6 %add.86 = f32[864,512]{1,0:T(8,128)} reshape(f32[24,36,512]{2,1,0:T(8,128)} %get-tuple-element.23) | data formatting | bytes 3538944 | tf_op jit(solution)/shard_map/add | solution.py:46
  71.5 2.8 %mul.271 = f32[32,27,1,512]{3,1,0,2:T(8,128)} reshape(f32[24,36,512]{2,1,0:T(8,128)} %get-tuple-element.24) | data formatting | bytes 3538944 | tf_op jit(solution)/shard_map/mul | solution.py:45
  74.3 2.6 %mul.257 = f32[864,512]{1,0:T(8,128)} reshape(f32[24,36,512]{2,1,0:T(8,128)} %get-tuple-element.24) | data formatting | bytes 3538944 | tf_op jit(solution)/shard_map/mul | solution.py:45
  76.9 2.8 %mul.273 = f32[32,27,1,512]{3,1,0,2:T(8,128)} reshape(f32[24,36,512]{2,1,0:T(8,128)} %get-tuple-element.9) | data formatting | bytes 3538944 | tf_op jit(solution)/shard_map/mul | solution.py:45
  79.7 2.6 %mul.260 = f32[864,512]{1,0:T(8,128)} reshape(f32[24,36,512]{2,1,0:T(8,128)} %get-tuple-element.9) | data formatting | bytes 3538944 | tf_op jit(solution)/shard_map/mul | solution.py:45
  82.3 1.6 %mul.274 = f32[32,27,1,512]{3,1,0,2:T(8,128)} reshape(f32[24,36,512]{2,1,0:T(8,128)S(1)} %get-tuple-element.10) | data formatting | bytes 3538944 | tf_op jit(solution)/shard_map/mul | solution.py:46
  83.9 1.4 mul.263
  85.3 1.9 %pad_maximum_fusion.2 = f32[24,36,512]{2,1,0:T(8,128)S(1)} fusion(f32[24,34,512]{2,1,0:T(8,128)} %get-tuple-element.13, f32[24,2,512]{2,1,0:T(2,128)} %get-tuple-element.11), kind=kLoop, calls=%fused_computation.33 | loop fusion | flops 442368 | bytes 3538944 | tf_op jit(solution)/shard_map/jit(_roll_static)/concatenate | solution.py:44
  87.2 1.6 %concatenate.36 = f32[32,27,1,512]{3,1,0,2:T(8,128)} reshape(f32[24,36,512]{2,1,0:T(8,128)S(1)} %pad_maximum_fusion.2) | data formatting | bytes 3538944 | tf_op jit(solution)/shard_map/jit(_roll_static)/concatenate | solution.py:44
  88.8 1.5 concatenate.34
  90.3 2.8 %reshape_reshape.5 = f32[864,512]{1,0:T(8,128)} reshape(f32[32,27,1,512]{3,1,0,2:T(8,128)} %bitcast.2) | data formatting | bytes 3538944 | tf_op jit(solution)/shard_map/reshape;reshape | solution.py:39
  93.1 7.3 %subtract_reduce_fusion = f32[512]{0:T(512)S(1)} fusion(f32[32,27,1,512]{3,1,0,2:T(8,128)} %mul.270, pred[32,27,1,512]{3,1,0,2:T(8,128)(4,1)S(1)} %copy-done.4, f32[32,27,1,512]{3,1,0,2:T(8,128)} %mul.274, f32[32,27,1,512]{3,1,0,2:T(8,128)} %add.90, f32[32,27,1,512]{3,1,0,2:T(8,128)} %concatenate.36, f32[32,27,1,512]{3,1,0,2:T(8,128)} %mul.273, ...), kind=kLoop, calls=%fused_computation.30 | loop fusion | flops 5307904 | bytes 12830720 | tf_op jit(solution)/shard_map/reduce_sum | solution.py:52
  100.4 16.2 %fusion.24 = f32[864,1,512]{2,0,1:T(8,128)S(1)} fusion(bf16[864,864]{1,0:T(8,128)(2,1)S(1)} %copy-done, bf16[864,864]{1,0:T(8,128)(2,1)} %param.18, f32[512]{0:T(512)S(1)} %broadcast_multiply_fusion.1, f32[864]{0:T(1024)S(1)} %copy-done.8, f32[864,512]{1,0:T(8,128)} %reshape_reshape.5, f32[864,512]{1,0:T(8,128)} %mul.255, ...), kind=kOutput, calls=%fused_computation.41 | convolution fusion | flops 1548288000 | bytes 17595136 | tf_op jit(solution)/shard_map/dot_general | solution.py:51
  116.7 1.8 %copy.36 = f32[864,1,512]{2,1,0:T(1,128)S(1)} copy(f32[864,1,512]{2,0,1:T(8,128)S(1)} %fusion.24) | data formatting | bytes 3538944 | tf_op jit(solution)/shard_map/reshape | solution.py:86
  118.5 29.9 %all_to_all.33 = f32[864,1,512]{2,1,0:T(1,128)S(1)} all-to-all(f32[864,1,512]{2,1,0:T(1,128)S(1)} %copy.36), channel_id=1, replica_groups=mesh['comp'=32,'tile'=8] {'comp'}, dimensions={0} | all-to-all | bytes 3538944 | tf_op jit(solution)/shard_map/all_to_all | solution.py:87
  148.4 1.4 copy.41
  (35 shorter events, 6.4 us)
Async XLA Ops:
  0.0 100.4 %copy-start = (bf16[864,864]{1,0:T(8,128)(2,1)S(1)}, bf16[864,864]{1,0:T(8,128)(2,1)}, u32[]{:S(2)}) copy-start(bf16[864,864]{1,0:T(8,128)(2,1)} %param.19) | copy-start | bytes 4478980
  0.0 12.9 %copy-start.3 = (f32[27,32,512]{2,1,0:T(8,128)S(1)}, f32[27,32,512]{2,1,0:T(8,128)}, u32[]{:S(2)}) copy-start(f32[27,32,512]{2,1,0:T(8,128)} %param.10) | copy-start | bytes 5308420
  0.0 11.4 %copy-start.7 = (f32[27]{0:T(128)S(1)}, f32[27]{0:T(128)}, u32[]{:S(2)}) copy-start(f32[27]{0:T(128)} %param.11) | copy-start | bytes 328
  2.7 1.3 copy-start.1
  4.7 7.2 %collective-permute-start.1 = (f32[27,2,512]{2,0,1:T(8,128)}, f32[27,2,512]{2,0,1:T(8,128)}, u32[]{:S(2)}, u32[]{:S(2)}) collective-permute-start(f32[27,2,512]{2,0,1:T(8,128)} %get-tuple-element.5), channel_id=1, source_target_pairs={{0,1},{1,2},{2,3},{3,4},{4,5},{5,6},{6,7},{8,9},{9,10},{10,11},{11... | collective-permute-start | bytes 331784 | tf_op jit(solution)/shard_map/ppermute | solution.py:16
  9.5 7.1 %collective-permute-start = (f32[27,2,512]{2,0,1:T(8,128)}, f32[27,2,512]{2,0,1:T(8,128)S(1)}, u32[]{:S(2)}, u32[]{:S(2)}) collective-permute-start(f32[27,2,512]{2,0,1:T(8,128)} %get-tuple-element.6), channel_id=1, source_target_pairs={{1,0},{2,1},{3,2},{4,3},{5,4},{6,5},{7,6},{9,8},{10,9},{11,10},{12... | collective-permute-start | bytes 331784 | tf_op jit(solution)/shard_map/ppermute | solution.py:19
  12.9 3.8 %copy-start.2 = (f32[27,32,512]{2,0,1:T(8,128)S(1)}, f32[27,32,512]{2,0,1:T(8,128)}, u32[]{:S(2)}) copy-start(f32[27,32,512]{2,0,1:T(8,128)} %copy-done.1) | copy-start | bytes 5308420
  12.9 3.8 %copy-start.5 = (f32[32,512]{1,0:T(8,128)S(1)}, f32[32,512]{1,0:T(8,128)}, u32[]{:S(2)}) copy-start(f32[32,512]{1,0:T(8,128)} %param.12) | copy-start | bytes 196612
  20.8 10.1 %copy-start.6 = (f32[24]{0:T(128)S(1)}, f32[24]{0:T(128)}, u32[]{:S(2)}) copy-start(f32[24]{0:T(128)} %param.15) | copy-start | bytes 292
  20.8 37.3 %all-to-all-start = ((f32[27,32,512]{2,0,1:T(8,128)}), f32[27,32,512]{2,0,1:T(8,128)}, u32[]{:S(2)}, u32[]{:S(2)}) async-start(f32[27,32,512]{2,0,1:T(8,128)} %fusion.9), calls=%async_computation | async-start | bytes 4194304 | tf_op jit(solution)/shard_map/all_to_all | solution.py:71
  90.3 2.9 %copy-start.4 = (pred[32,27,1,512]{3,1,0,2:T(8,128)(4,1)S(1)}, pred[32,27,1,512]{3,1,0,2:T(8,128)(4,1)}, u32[]{:S(2)}) copy-start(pred[32,27,1,512]{3,1,0,2:T(8,128)(4,1)} %broadcast_in_dim.14) | copy-start | bytes 1327108
  93.1 7.3 %copy-start.8 = (f32[864]{0:T(1024)S(1)}, f32[864]{0:T(1024)}, u32[]{:S(2)}) copy-start(f32[864]{0:T(1024)} %param.17) | copy-start | bytes 10372
  93.1 7.3 %copy-start.9 = (f32[864]{0:T(1024)S(1)}, f32[864]{0:T(1024)}, u32[]{:S(2)}) copy-start(f32[864]{0:T(1024)} %param.16) | copy-start | bytes 10372
where the time goes:
time: 151 us; the launch traced here: 150 us
  local copies, waits for them, and re-layouts  45.9 us (30%)
  blocking collectives  29.9 us (20%)
  waiting for transfers between devices  23.9 us (16%)
  other arithmetic  17.6 us (12%)
  matrix products  16.2 us (11%)
  starting transfers between devices  16 us (11%)
    all_to_all x1, blocking collectives, shards(): lax.all_to_all(result, 'comp', split_axis=0, concat_axis=1, tiled=True)  29.9 us
    all_to_all x1, waiting for transfers between devices, shards(): lax.all_to_all(moved, 'comp', split_axis=1, concat_axis=0, tiled=True)  20.8 us
    dot_general x1, matrix products, sources(): nonlinear = jnp.dot(quad_second, pair, preferred_element_type=jnp.float32)  16.2 us
    mul x4, local copies, waits for them, and re-layouts, sources(): positive = (2.0 * ahead_one + 3.0 * grid - 6.0 * back_one + back_two) / 6.0  10.8 us
    all_to_all x1, starting transfers between devices, shards(): lax.all_to_all(moved, 'comp', split_axis=1, concat_axis=0, tiled=True)  9.38 us
    reduce_sum x1, other arithmetic, sources(): energy = jnp.mean(turned, axis=0)  7.27 us
    add x2, local copies, waits for them, and re-layouts, sources(): -ahead_two + 6.0 * ahead_one - 3.0 * grid - 2.0 * back_one  5.4 us
    unnamed x22, local copies, waits for them, and re-layouts  4.96 us
  transfers between devices with their start and end apart: 3, of which 3 were waited for; matrix products, arithmetic and copies ran while one was open for 6% of the time, Pallas kernels for 0%

commit v1 on v0

v1 whole, which is shorter than its diff:
```python
import functools
import math

import jax
import jax.numpy as jnp
from jax import lax
from jax.experimental import pallas as pl
from jax.experimental.pallas import tpu as pltpu
from jax.sharding import PartitionSpec as P

NTH = 36
HELD = 27
PAD = 32
ROWS = 32
COLS = 512
OWNERS = 32
LANES = 128
TILES = COLS // LANES
VMEM = pl.BlockSpec(memory_space=pltpu.VMEM)
SMEM = pl.BlockSpec(memory_space=pltpu.SMEM)
PARAMS = pltpu.CompilerParams(vmem_limit_bytes=24 * 2**20)


def iota(shape, dim):
    return lax.broadcasted_iota(jnp.int32, shape, dim)


def lane_gather(values, index):
    return jnp.take_along_axis(values, index, axis=1, mode="promise_in_bounds")


def wide(coef):
    return jnp.concatenate([coef] * TILES, axis=1)


def butterfly(rows, lane):
    for step, bit in ((1, 16), (2, 32), (4, 64)):
        swap = (lane & bit) != 0
        rows = [jnp.where(swap, rows[j ^ step], rows[j]) for j in range(8)]
    return rows


def mixed_plane(plane):
    lane = iota((ROWS, LANES), 1)
    row = iota((ROWS, LANES), 0)
    pieces = []
    for t in range(TILES):
        block = plane[:, t * LANES : (t + 1) * LANES]
        block = jnp.concatenate([block[(g ^ t) * 8 : (g ^ t) * 8 + 8] for g in range(4)], axis=0)
        for step, bit in ((1, 16), (2, 32), (4, 64)):
            swapped = jnp.where(
                (row & step) != 0,
                pltpu.roll(block, step, axis=0),
                pltpu.roll(block, ROWS - step, axis=0),
            )
            block = jnp.where((lane & bit) != 0, swapped, block)
        pieces.append(block)
    return jnp.concatenate(pieces, axis=1)


def propagate_kernel(
    spec, depth, turn, mask, speed, moved, halo_coef, pick, rank, turn_own, most, grid
):
    me = lax.axis_index("comp")
    sub = iota((PAD, LANES), 0)
    speeds = jnp.zeros((PAD, LANES), jnp.float32)
    for k in range(HELD):
        speeds = jnp.where(sub == k, speed[k], speeds)
    theta = (2.0 * math.pi / NTH) * lax.rem(me * HELD + sub, NTH).astype(jnp.float32)

    def taps(velocity):
        up = velocity >= 0.0
        sixth = velocity / 6.0
        return (
            sixth * jnp.where(up, 3.0, -3.0),
            sixth * jnp.where(up, 2.0, 6.0),
            sixth * jnp.where(up, -6.0, -2.0),
            jnp.where(up, sixth, 0.0),
            jnp.where(up, 0.0, -sixth),
        )

    x_centre, x_ahead, x_back, x_back_two, x_ahead_two = taps(speeds * jnp.cos(theta))
    y_centre, y_ahead, y_back, y_back_two, y_ahead_two = taps(speeds * jnp.sin(theta))
    halo_coef[0] = y_back
    halo_coef[1] = y_back_two
    halo_coef[2] = y_ahead
    halo_coef[3] = y_ahead_two

    for r in (0, 1, ROWS + 2, ROWS + 3):
        grid[r] = jnp.zeros((PAD, COLS), jnp.float32)
    for cb in range(4):
        size = min(8, HELD - cb * 8)
        for rb in range(4):
            block = spec[cb * 8 : cb * 8 + size, rb * 8 : rb * 8 + 8, :]
            if size < 8:
                block = jnp.concatenate(
                    [block, jnp.zeros((8 - size, 8, COLS), jnp.float32)], axis=0
                )
            grid[2 + rb * 8 : 10 + rb * 8, cb * 8 : cb * 8 + 8, :] = jnp.swapaxes(block, 0, 1)

    lane = iota((8, COLS), 1)
    for cb in range(4):
        part = slice(cb * 8, cb * 8 + 8)
        coefs = [
            wide(c[part])
            for c in (
                x_centre + y_centre, x_ahead, x_back, x_back_two, x_ahead_two,
                y_ahead, y_back, y_back_two, y_ahead_two,
            )
        ]

        def row_group(rb, carry):
            depths = depth[pl.ds(pl.multiple_of(rb * 8, 8), 8), :]
            for i in range(8):
                row_step(rb * 8 + i, depths[i : i + 1, :])
            return carry

        def row_step(r, depth_row):
            centre = grid[r + 2, part, :]
            total = coefs[0] * centre
            total += coefs[1] * jnp.where(lane < COLS - 1, pltpu.roll(centre, COLS - 1, axis=1), 0.0)
            total += coefs[2] * jnp.where(lane >= 1, pltpu.roll(centre, 1, axis=1), 0.0)
            total += coefs[3] * jnp.where(lane >= 2, pltpu.roll(centre, 2, axis=1), 0.0)
            total += coefs[4] * jnp.where(lane < COLS - 2, pltpu.roll(centre, COLS - 2, axis=1), 0.0)
            total += coefs[5] * grid[r + 3, part, :]
            total += coefs[6] * grid[r + 1, part, :]
            total += coefs[7] * grid[r, part, :]
            total += coefs[8] * grid[r + 4, part, :]
            moved[r, part, :] = centre - depth_row * total

        lax.fori_loop(0, ROWS // 8, row_group, 0)

    sea = mixed_plane(mask[...])
    column = iota((ROWS, COLS), 1)
    count = sea
    step = 1
    while step < COLS:
        count = count + jnp.where(column >= step, pltpu.roll(count, step, axis=1), 0)
        step *= 2
    most[0] = jnp.max(count)
    place = count - 1
    rank[...] = jnp.where(sea > 0, place, -1)
    entry = jnp.where(sea > 0, column * COLS + (column - place), -1)
    step = 1
    while step < COLS:
        other = pltpu.roll(entry, COLS - step, axis=1)
        arrives = (other >= 0) & ((other & step) != 0)
        stays = (entry >= 0) & ((entry & step) == 0)
        entry = jnp.where(arrives, other, jnp.where(stays, entry, -1))
        step *= 2
    entry = jnp.where(entry >= 0, entry >> 9, 0)
    pick[...] = entry

    mine = iota((ROWS, COLS), 0) == me
    own_turn = jnp.sum(jnp.where(mine, mixed_plane(turn[...]), 0.0), axis=0, keepdims=True)
    own_pick = jnp.sum(jnp.where(mine, entry, 0), axis=0, keepdims=True)
    for t in range(TILES):
        index = jnp.broadcast_to(own_pick[:, t * LANES : (t + 1) * LANES], (8, LANES))
        total = jnp.zeros((8, LANES), jnp.float32)
        for source in range(TILES):
            own = jnp.broadcast_to(own_turn[:, source * LANES : (source + 1) * LANES], (8, LANES))
            value = lane_gather(own, index & (LANES - 1))
            total = jnp.where(index >> 7 == source, value, total)
        turn_own[:, t * LANES : (t + 1) * LANES] = total


def propagate(spectrum, depth, turn, mask, speed):
    plane = jax.ShapeDtypeStruct((ROWS, COLS), jnp.int32)
    return pl.pallas_call(
        propagate_kernel,
        out_shape=[
            jax.ShapeDtypeStruct((ROWS, PAD, COLS), jnp.float32),
            jax.ShapeDtypeStruct((4, PAD, LANES), jnp.float32),
            plane,
            plane,
            jax.ShapeDtypeStruct((8, COLS), jnp.float32),
            jax.ShapeDtypeStruct((1,), jnp.int32),
        ],
        in_specs=[VMEM, VMEM, VMEM, VMEM, SMEM],
        out_specs=[VMEM, VMEM, VMEM, VMEM, VMEM, SMEM],
        scratch_shapes=[
            pltpu.VMEM((ROWS + 4, PAD, COLS), jnp.float32),
        ],
        compiler_params=PARAMS,
        cost_estimate=pl.CostEstimate(flops=20000000, bytes_accessed=5000000, transcendentals=0),
        name="propagate",
    )(spectrum, depth, turn, mask, speed)


def block_rows(tiles):
    return (HELD * tiles + 7) // 8 * 8


def compact_kernel(tiles, moved, low, high, depth, halo_coef, pick, out, mixed, edge):
    lane = iota((8, LANES), 1)
    back, back_two, ahead, ahead_two = [wide(halo_coef[i, 0:HELD, :]) for i in range(4)]
    terms = {
        0: back * low[1] + back_two * low[0],
        1: back_two * low[1],
        ROWS - 2: ahead_two * high[0],
        ROWS - 1: ahead * high[0] + ahead_two * high[1],
    }
    edge_of = {}
    for r, term in terms.items():
        edge_of[r] = len(edge_of)
        edge[edge_of[r], 0:HELD, :] = moved[r, 0:HELD, :] - depth[r : r + 1, :] * term

    def load(r, cb, t):
        rows, lanes = slice(cb * 8, cb * 8 + 8), slice(t * LANES, (t + 1) * LANES)
        return edge[edge_of[r], rows, lanes] if r in edge_of else moved[r, rows, lanes]

    for cb in range(4):
        for g in range(4):
            for t in range(TILES):
                rows = [load((g ^ t) * 8 + j, cb, t) for j in range(8)]
                for j, value in enumerate(butterfly(rows, lane)):
                    mixed[g * 8 + j, cb * 8 : cb * 8 + 8, t * LANES : (t + 1) * LANES] = value

    def owner_group(g, carry):
        picks = pick[pl.ds(pl.multiple_of(g * 8, 8), 8), :]
        for i in range(8):
            owner_step(g * 8 + i, picks[i : i + 1, :])
        return carry

    def owner_step(d, pick_row):
        for slot in range(tiles):
            index = jnp.broadcast_to(pick_row[:, slot * LANES : (slot + 1) * LANES], (8, LANES))
            tile_of = index >> 7
            index = index & (LANES - 1)
            for cb in range(4):
                total = lane_gather(
                    mixed[d, cb * 8 : cb * 8 + 8, slot * LANES : (slot + 1) * LANES], index
                )
                for source in range(slot + 1, TILES):
                    value = mixed[d, cb * 8 : cb * 8 + 8, source * LANES : (source + 1) * LANES]
                    total = jnp.where(tile_of == source, lane_gather(value, index), total)
                if cb < 3:
                    out[d, slot * 24 + cb * 8 : slot * 24 + cb * 8 + 8, :] = total
                else:
                    first = 24 * tiles + 3 * slot
                    out[d, first : first + 3, :] = total[0:3]

    lax.fori_loop(0, OWNERS // 8, owner_group, 0)


def compact(tiles, moved, low, high, depth, halo_coef, pick):
    return pl.pallas_call(
        functools.partial(compact_kernel, tiles),
        out_shape=jax.ShapeDtypeStruct((OWNERS, block_rows(tiles), LANES), jnp.float32),
        in_specs=[VMEM] * 6,
        out_specs=VMEM,
        scratch_shapes=[
            pltpu.VMEM((OWNERS, PAD, COLS), jnp.float32),
            pltpu.VMEM((4, PAD, COLS), jnp.float32),
        ],
        compiler_params=PARAMS,
        cost_estimate=pl.CostEstimate(flops=5000000, bytes_accessed=4000000, transcendentals=0),
        name="compact",
    )(moved, low, high, depth, halo_coef, pick)


def runs():
    found = []
    for s in range(OWNERS):
        k = 0
        while k < HELD:
            c = s * HELD + k
            end = min(24 if k < 24 else HELD, k + NTH - c % NTH)
            found.append((s, k, end - k, c))
            k = end
    return found


def block_row(tiles, slot, k):
    return slot * 24 + k if k < 24 else 24 * tiles + 3 * slot + k - 24


def source_kernel(
    tiles, points, turn_own, refraction, keep, lose, first, second, out, grid, turned, low, pair
):
    ncomp = turned.shape[0]
    nfreq = ncomp // NTH
    width = NTH + 4
    for slot in range(tiles):
        lanes = slice(slot * LANES, (slot + 1) * LANES)
        for s, k, size, c in runs():
            row = block_row(tiles, slot, k)
            to = c // NTH * width + 2 + c % NTH
            grid[to : to + size, lanes] = points[s, row : row + size, :]
        for f in range(nfreq):
            base = f * width
            grid[base : base + 2, lanes] = grid[base + NTH : base + NTH + 2, lanes]
            grid[base + NTH + 2 : base + NTH + 4, lanes] = grid[base + 2 : base + 4, lanes]
        for f in range(nfreq):
            base = f * width
            rate = refraction[f] * turn_own[0:1, lanes]
            up = rate >= 0.0
            sixth = rate / 6.0
            centre = grid[base : base + width, lanes]
            total = (sixth * jnp.where(up, 3.0, -3.0)) * centre
            total += (sixth * jnp.where(up, 2.0, 6.0)) * pltpu.roll(centre, width - 1, axis=0)
            total += (sixth * jnp.where(up, -6.0, -2.0)) * pltpu.roll(centre, 1, axis=0)
            total += jnp.where(up, sixth, 0.0) * pltpu.roll(centre, 2, axis=0)
            total += jnp.where(up, 0.0, -sixth) * pltpu.roll(centre, width - 2, axis=0)
            result = centre - total
            turned[f * NTH : (f + 1) * NTH, lanes] = result[2 : NTH + 2]

    chunk = ncomp // 3
    energy = jnp.zeros((1, tiles * LANES), jnp.float32)
    for m in range(0, ncomp, chunk):
        value = turned[m : m + chunk, :]
        low[m : m + chunk, :] = value.astype(jnp.bfloat16)
        energy += jnp.sum(value, axis=0, keepdims=True)
    energy = energy / ncomp
    for m in range(0, ncomp, chunk):
        partner = jnp.dot(
            first[m : m + chunk, :], low[...], preferred_element_type=jnp.float32
        )
        pair[m : m + chunk, :] = (turned[m : m + chunk, :] * partner).astype(jnp.bfloat16)
    for m in range(0, ncomp, chunk):
        nonlinear = jnp.dot(
            second[m : m + chunk, :], pair[...], preferred_element_type=jnp.float32
        )
        for slot in range(tiles):
            lanes = slice(slot * LANES, (slot + 1) * LANES)
            scale = keep[m : m + chunk, :] - lose[m : m + chunk, :] * energy[:, lanes]
            turned[m : m + chunk, lanes] = (
                turned[m : m + chunk, lanes] * scale + 0.2 * nonlinear[:, lanes]
            )
    for s in range(OWNERS):
        for slot in range(tiles):
            lanes = slice(slot * LANES, (slot + 1) * LANES)
            out[s, slot * 24 : slot * 24 + 24, :] = turned[s * HELD : s * HELD + 24, lanes]
            row = 24 * tiles + 3 * slot
            out[s, row : row + 3, :] = turned[s * HELD + 24 : s * HELD + HELD, lanes]


def sources(tiles, points, turn_own, refraction, keep, lose, first, second):
    ncomp = first.shape[0]
    lanes = tiles * LANES
    return pl.pallas_call(
        functools.partial(source_kernel, tiles),
        out_shape=jax.ShapeDtypeStruct(points.shape, jnp.float32),
        in_specs=[VMEM, VMEM, SMEM, VMEM, VMEM, VMEM, VMEM],
        out_specs=VMEM,
        scratch_shapes=[
            pltpu.VMEM((ncomp // NTH * (NTH + 4), lanes), jnp.float32),
            pltpu.VMEM((ncomp, lanes), jnp.float32),
            pltpu.VMEM((ncomp, lanes), jnp.bfloat16),
            pltpu.VMEM((ncomp, lanes), jnp.bfloat16),
        ],
        compiler_params=PARAMS,
        cost_estimate=pl.CostEstimate(
            flops=4 * ncomp * ncomp * lanes, bytes_accessed=6000000, transcendentals=0
        ),
        name="sources",
    )(points, turn_own, refraction, keep, lose, first, second)


def expand_kernel(tiles, result, rank, out, mixed):
    lane = iota((8, LANES), 1)

    def owner_group(g, carry):
        ranks = rank[pl.ds(pl.multiple_of(g * 8, 8), 8), :]
        for i in range(8):
            owner_step(g * 8 + i, ranks[i : i + 1, :])
        return carry

    def owner_step(d, rank_row):
        tail = result[d, 24 * tiles : 24 * tiles + 16, :]
        for t in range(TILES):
            index = jnp.broadcast_to(rank_row[:, t * LANES : (t + 1) * LANES], (8, LANES))
            slot_of = index >> 7
            land = index < 0
            index = index & (LANES - 1)
            for cb in range(4):
                total = jnp.zeros((8, LANES), jnp.float32)
                for slot in range(min(t + 1, tiles)):
                    if cb < 3:
                        row = slot * 24 + cb * 8
                        value = result[d, row : row + 8, :]
                    else:
                        value = pltpu.roll(tail, (16 - 3 * slot) % 16, axis=0)[0:8]
                    value = lane_gather(value, index)
                    total = value if slot == 0 else jnp.where(slot_of == slot, value, total)
                mixed[d, cb * 8 : cb * 8 + 8, t * LANES : (t + 1) * LANES] = jnp.where(
                    land, 0.0, total
                )

    lax.fori_loop(0, OWNERS // 8, owner_group, 0)
    for cb in range(4):
        size = min(8, HELD - cb * 8)
        for g in range(4):
            for t in range(TILES):
                rows = [
                    mixed[(g ^ t) * 8 + j, cb * 8 : cb * 8 + 8, t * LANES : (t + 1) * LANES]
                    for j in range(8)
                ]
                block = jnp.swapaxes(jnp.stack(butterfly(rows, lane)), 0, 1)
                out[cb * 8 : cb * 8 + size, g * 8 : g * 8 + 8, t * LANES : (t + 1) * LANES] = block[
                    0:size
                ]


def expand(tiles, result, rank):
    return pl.pallas_call(
        functools.partial(expand_kernel, tiles),
        out_shape=jax.ShapeDtypeStruct((HELD, ROWS, COLS), jnp.float32),
        in_specs=[VMEM] * 2,
        out_specs=VMEM,
        scratch_shapes=[pltpu.VMEM((OWNERS, PAD, COLS), jnp.float32)],
        compiler_params=PARAMS,
        cost_estimate=pl.CostEstimate(flops=5000000, bytes_accessed=4000000, transcendentals=0),
        name="expand",
    )(result, rank)


def exchange(blocks):
    return lax.all_to_all(blocks, "comp", split_axis=0, concat_axis=0, tiled=True)


def shards(
    spectrum, speed, depth, turn, sea_mask, refraction, growth, dissipation, quad_first, quad_second
):
    count = lax.axis_size("tile")
    forward = [(i, i + 1) for i in range(count - 1)]
    backward = [(i + 1, i) for i in range(count - 1)]
    low = lax.ppermute(jnp.swapaxes(spectrum[:, ROWS - 2 :, :], 0, 1), "tile", forward)
    high = lax.ppermute(jnp.swapaxes(spectrum[:, :2, :], 0, 1), "tile", backward)
    moved, halo_coef, pick, rank, turn_own, most = propagate(
        spectrum, depth, turn, sea_mask, speed
    )
    ncomp = growth.shape[0]
    keep = jnp.broadcast_to((1.0 + 0.2 * growth)[:, None], (ncomp, LANES))
    lose = jnp.broadcast_to((0.2 * dissipation)[:, None], (ncomp, LANES))

    def rest(tiles):
        def run(moved, low, high):
            sent = compact(tiles, moved, low, high, depth, halo_coef, pick)
            points = exchange(sent)
            result = sources(
                tiles, points, turn_own, refraction, keep, lose, quad_first, quad_second
            )
            return expand(tiles, exchange(result), rank)

        return run

    return lax.cond(most[0] <= 3 * LANES, rest(3), rest(4), moved, low, high)


def solution(mesh):
    in_specs = (
        P("comp", "tile", None),
        P("comp"),
        P("tile", None),
        P("tile", None),
        P("tile", None),
        P(),
        P(),
        P(),
        P(),
        P(),
    )
    out_specs = P("comp", "tile", None)
    return jax.shard_map(shards, mesh=mesh, in_specs=in_specs, out_specs=out_specs, check_vma=False)
```

time: 151 us -> 87 us (0.58)
  local copies, waits for them, and re-layouts: 45.9 us -> 6.71 us
  other arithmetic: 17.6 us -> 0.01 us
  Pallas kernels: 0 us -> 17.2 us
  matrix products: 16.2 us -> 0 us
  blocking collectives: 29.9 us -> 26.2 us
  waiting for transfers between devices: 23.9 us -> 20.6 us
    pallas_call x0 -> x4, Pallas kernels: none -> 17.2 us  [the longest x1 6.62 us: propagate(): pl.pallas_call(propagate_kernel, out_shape=[jax.ShapeDtypeStruct((ROWS, P...]
    mul x9 -> x0, local copies, waits for them, and re-layouts: 17 us -> none  [the longest x4 10.8 us: sources(): positive = (2.0 * ahead_one + 3.0 * grid - 6.0 * back_one + back_two) / 6.0]
    dot_general x1 -> x0, matrix products: 16.2 us -> none  [sources(): nonlinear = jnp.dot(quad_second, pair, preferred_element_type=jnp.float32)]
    reduce_sum x1 -> x0, other arithmetic: 7.27 us -> none  [sources(): energy = jnp.mean(turned, axis=0)]
    add x2 -> x0, local copies, waits for them, and re-layouts: 5.4 us -> none  [sources(): -ahead_two + 6.0 * ahead_one - 3.0 * grid - 2.0 * back_one]
    another operation x2 -> x0, local copies, waits for them, and re-layouts: 4.48 us -> none  [sources(): grid = flat.reshape(nfreq, ncomp // nfreq, npts)]
    sub x1 -> x0, other arithmetic: 4.15 us -> none  [shards(): spectrum - vel_x * third(pad_x, vel_x, 2) - vel_y * third(pad_y, vel_y, 1)]
    concatenate x4 -> x0, local copies, waits for them, and re-layouts: 4.11 us -> none  [the longest x2 3.06 us: sources(): back_two = jnp.roll(grid, 2, axis=1)]
  transfers between devices with their start and end apart: 3 -> 3, of which waited for: 3 -> 1; matrix products, arithmetic and copies ran while one was open for 6% -> 0% of each run, Pallas kernels for 0% -> 8%
where the time goes in v1:
time: 87 us; the launch traced here: 86.5 us
  blocking collectives  26.2 us (30%)
  waiting for transfers between devices  20.6 us (24%)
  Pallas kernels  17.2 us (20%)
  starting transfers between devices  14.7 us (17%)
  local copies, waits for them, and re-layouts  6.71 us (8%)
    all_to_all x1, blocking collectives, exchange(): lax.all_to_all(blocks, 'comp', split_axis=0, concat_axis=0, tiled=True)  26.2 us
    all_to_all x1, waiting for transfers between devices, exchange(): lax.all_to_all(blocks, 'comp', split_axis=0, concat_axis=0, tiled=True)  20.6 us
    all_to_all x1, starting transfers between devices, exchange(): lax.all_to_all(blocks, 'comp', split_axis=0, concat_axis=0, tiled=True)  8.05 us
    pallas_call x1, Pallas kernels, propagate(): pl.pallas_call(propagate_kernel, out_shape=[jax.ShapeDtypeStruct((ROWS, P...  6.62 us
    unnamed x22, local copies, waits for them, and re-layouts  5.07 us
    pallas_call x1, Pallas kernels, sources(): pl.pallas_call(functools.partial(source_kernel, tiles), out_shape=jax.Sha...  4.94 us
    ppermute x1, starting transfers between devices, shards(): lax.ppermute(jnp.swapaxes(spectrum[:, ROWS - 2:, :], 0, 1), 'tile', forward)  4.76 us
    pallas_call x1, Pallas kernels, compact(): pl.pallas_call(functools.partial(compact_kernel, tiles), out_shape=jax.Sh...  3.19 us
  transfers between devices with their start and end apart: 3, of which 1 were waited for; matrix products, arithmetic and copies ran while one was open for 0% of the time, Pallas kernels for 8%

profile of v1, /device:TPU:97, one launch (start us, length us, event | category | flops | bytes accessed | tf_op | source)
XLA Modules:
  0.0 86.5 jit_solution(16076201754741017304)
XLA Ops:
  0.0 0.0 copy-start.6
  0.0 0.0 copy-start.8
  0.0 0.0 copy-start.7
  0.0 0.0 copy-start.9
  0.0 1.3 %fusion = (f32[27,2,512]{2,1,0:T(2,128)S(1)}, f32[27,2,512]{2,1,0:T(2,128)S(1)}) fusion(f32[27,32,512]{2,1,0:T(8,128)} %spec.1), kind=kLoop, calls=%fused_computation.6 | loop fusion | bytes 442368 | tf_op jit(solution)/shard_map/slice | solution.py:429
  1.4 4.8 %collective-permute-start = (f32[2,27,512]{2,1,0:T(8,128)S(1)}, f32[2,27,512]{2,1,0:T(8,128)S(1)}, u32[]{:S(2)}, u32[]{:S(2)}) collective-permute-start(f32[2,27,512]{2,1,0:T(8,128)S(1)} %bitcast.7), channel_id=1, source_target_pairs={{0,1},{1,2},{2,3},{3,4},{4,5},{5,6},{6,7},{8,9},{9,10},{10,11},{11... | collective-permute-start | bytes 331784 | tf_op jit(solution)/shard_map/ppermute | solution.py:428
  6.1 1.9 %collective-permute-start.1 = (f32[2,27,512]{2,1,0:T(8,128)S(1)}, f32[2,27,512]{2,1,0:T(8,128)S(1)}, u32[]{:S(2)}, u32[]{:S(2)}) collective-permute-start(f32[2,27,512]{2,1,0:T(8,128)S(1)} %bitcast.8), channel_id=1, source_target_pairs={{1,0},{2,1},{3,2},{4,3},{5,4},{6,5},{7,6},{9,8},{10,9},{11,10},{12... | collective-permute-start | bytes 331784 | tf_op jit(solution)/shard_map/ppermute | solution.py:429
  8.1 0.0 copy-start
  8.1 1.5 %copy-done = f32[27,32,512]{2,1,0:T(8,128)S(1)} copy-done((f32[27,32,512]{2,1,0:T(8,128)S(1)}, f32[27,32,512]{2,1,0:T(8,128)}, u32[]{:S(2)}) %copy-start) | copy-done | bytes 1769496
  9.6 0.0 copy-start.1
  9.6 0.8 copy-done.1
  10.4 0.8 copy-done.2
  11.2 0.7 copy-done.3
  11.9 6.6 %propagate.1 = (f32[32,32,512]{2,1,0:T(8,128)S(1)}, f32[4,32,128]{2,1,0:T(8,128)S(1)}, s32[32,512]{1,0:T(8,128)S(1)}, s32[32,512]{1,0:T(8,128)S(1)}, f32[8,512]{1,0:T(8,128)S(1)}, /*index=5*/s32[1]{0:T(128)}) custom-call(f32[27,32,512]{2,1,0:T(8,128)S(1)} %copy-done, f32[32,512]{1,0:T(8,128)} %depth.1, f32[32,512]{1,0:T(8,128)S(1)} %copy-done.1, ...), custom_call_target="tpu_custom_call" | custom-call | flops 20000000 | bytes 5000000 | tf_op jit(solution)/shard_map/propagate/pallas_call | solution.py:169
  19.2 0.0 collective-permute-done
  19.2 0.0 collective-permute-done.1
  19.2 0.0 copy-done.6
  19.2 0.0 copy-done.8
  19.2 0.0 copy-done.7
  19.2 0.0 copy-done.9
  19.2 0.0 copy-done.4
  19.2 66.0 %conditional.1 = (f32[27,32,512]{2,1,0:T(8,128)S(1)}) conditional(s32[]{:T(128)} %bitcast, (f32[32,32,512]{2,1,0:T(8,128)S(1)}, f32[2,27,512]{2,1,0:T(8,128)S(1)}, f32[2,27,512]{2,1,0:T(8,128)S(1)}, f32[32,512]{1,0:T(8,128)S(1)}, f32[4,32,128]{2,1,0:T(8,128)S(1)}, /*index=5*/s32[32,512]{1,0:T(8,128)S(1)}, f32[8,512]{1,0:T(8,128)S(1)}, ...), branch_computations={%region_0.0_spmd, %region_1.0_spmd} | conditional | flops 1538826496 | bytes 24080552 | solution.py:448
  19.3 3.2 %compact.3 = f32[32,88,128]{2,1,0:T(8,128)} custom-call(f32[32,32,512]{2,1,0:T(8,128)S(1)} %get-tuple-element.73.moved, f32[2,27,512]{2,1,0:T(8,128)S(1)} %get-tuple-element.74.low, f32[2,27,512]{2,1,0:T(8,128)S(1)} %get-tuple-element.75.high, f32[32,512]{1,0:T(8,128)S(1)} %get-tuple-element.76.depth, f32[4,32,128]{2,1,0:T(8,128)S(1)} %get-tuple-element.77.halo_coef, ...), custom_call_target="tpu_custom_call" | custom-call | flops 5000000 | bytes 4000000 | tf_op jit(solution)/shard_map/cond/branch_1_fun/compact/pallas_call | solution.py:247
  22.5 8.0 %all-to-all-start.2 = ((f32[32,88,128]{2,1,0:T(8,128)}), f32[32,88,128]{2,1,0:T(8,128)S(1)}, u32[]{:S(2)}, u32[]{:S(2)}) async-start(f32[32,88,128]{2,1,0:T(8,128)} %compact.3), calls=%async_computation.2 | async-start | bytes 2883584 | tf_op jit(solution)/shard_map/cond/branch_1_fun/all_to_all | solution.py:419
  30.5 20.6 %all-to-all-done.2.points = f32[32,88,128]{2,1,0:T(8,128)S(1)} async-done(((f32[32,88,128]{2,1,0:T(8,128)}), f32[32,88,128]{2,1,0:T(8,128)S(1)}, u32[]{:S(2)}, u32[]{:S(2)}) %all-to-all-start.2) | async-done | bytes 1441824 | tf_op jit(solution)/shard_map/cond/branch_1_fun/all_to_all | solution.py:419
  51.1 0.2 broadcast_in_dim.7.keep
  51.3 0.2 broadcast_in_dim.17.lose
  51.5 4.9 %sources.3 = f32[32,88,128]{2,1,0:T(8,128)S(1)} custom-call(f32[32,88,128]{2,1,0:T(8,128)S(1)} %all-to-all-done.2.points, f32[8,512]{1,0:T(8,128)S(1)} %get-tuple-element.79.turn_own, f32[24]{0:T(128)S(1)} %get-tuple-element.110.refraction, f32[864,128]{1,0:T(8,128)S(1)} %broadcast_in_dim.7.keep, f32[864,128]{1,0:T(8,128)S(1)} %broadcast_in_dim.17.lose, ...), custom_call_target="tpu_custom_call" | custom-call | flops 1146617856 | bytes 6000000 | tf_op jit(solution)/shard_map/cond/branch_1_fun/sources/pallas_call | solution.py:341
  56.4 26.2 %all_to_all.17.result = f32[32,88,128]{2,1,0:T(8,128)S(1)} all-to-all(f32[32,88,128]{2,1,0:T(8,128)S(1)} %sources.3), channel_id=1, replica_groups=mesh['comp'=32,'tile'=8] {'comp'}, dimensions={0} | all-to-all | bytes 2883584 | tf_op jit(solution)/shard_map/cond/branch_1_fun/all_to_all | solution.py:419
  82.6 2.4 %expand.3 = f32[27,32,512]{2,1,0:T(8,128)S(1)} custom-call(f32[32,88,128]{2,1,0:T(8,128)S(1)} %all_to_all.17.result, s32[32,512]{1,0:T(8,128)S(1)} %get-tuple-element.85.rank), custom_call_target="tpu_custom_call" | custom-call | flops 5000000 | bytes 4000000 | tf_op jit(solution)/shard_map/cond/branch_1_fun/expand/pallas_call | solution.py:406
  85.3 0.0 copy-start.5
  85.3 1.2 %copy-done.5 = f32[27,32,512]{2,1,0:T(8,128)} copy-done((f32[27,32,512]{2,1,0:T(8,128)}, f32[27,32,512]{2,1,0:T(8,128)S(1)}, u32[]{:S(2)}) %copy-start.5) | copy-done | bytes 1769496
  (6 shorter events, 0.1 us)
Async XLA Ops:
  0.0 19.2 %copy-start.6 = (f32[32,512]{1,0:T(8,128)S(1)}, f32[32,512]{1,0:T(8,128)}, u32[]{:S(2)}) copy-start(f32[32,512]{1,0:T(8,128)} %depth.1) | copy-start | bytes 196612
  0.0 19.2 %copy-start.8 = (f32[864]{0:T(1024)S(1)}, f32[864]{0:T(1024)}, u32[]{:S(2)}) copy-start(f32[864]{0:T(1024)} %param.19) | copy-start | bytes 10372
  0.0 19.2 %copy-start.7 = (f32[864]{0:T(1024)S(1)}, f32[864]{0:T(1024)}, u32[]{:S(2)}) copy-start(f32[864]{0:T(1024)} %param.18) | copy-start | bytes 10372
  0.0 19.2 %copy-start.9 = (f32[24]{0:T(128)S(1)}, f32[24]{0:T(128)}, u32[]{:S(2)}) copy-start(f32[24]{0:T(128)} %param.17) | copy-start | bytes 292
  1.4 17.8 %collective-permute-start = (f32[2,27,512]{2,1,0:T(8,128)S(1)}, f32[2,27,512]{2,1,0:T(8,128)S(1)}, u32[]{:S(2)}, u32[]{:S(2)}) collective-permute-start(f32[2,27,512]{2,1,0:T(8,128)S(1)} %bitcast.7), channel_id=1, source_target_pairs={{0,1},{1,2},{2,3},{3,4},{4,5},{5,6},{6,7},{8,9},{9,10},{10,11},{11... | collective-permute-start | bytes 331784 | tf_op jit(solution)/shard_map/ppermute | solution.py:428
  6.1 13.0 %collective-permute-start.1 = (f32[2,27,512]{2,1,0:T(8,128)S(1)}, f32[2,27,512]{2,1,0:T(8,128)S(1)}, u32[]{:S(2)}, u32[]{:S(2)}) collective-permute-start(f32[2,27,512]{2,1,0:T(8,128)S(1)} %bitcast.8), channel_id=1, source_target_pairs={{1,0},{2,1},{3,2},{4,3},{5,4},{6,5},{7,6},{9,8},{10,9},{11,10},{12... | collective-permute-start | bytes 331784 | tf_op jit(solution)/shard_map/ppermute | solution.py:429
  8.1 1.5 %copy-start = (f32[27,32,512]{2,1,0:T(8,128)S(1)}, f32[27,32,512]{2,1,0:T(8,128)}, u32[]{:S(2)}) copy-start(f32[27,32,512]{2,1,0:T(8,128)} %spec.1) | copy-start | bytes 5308420
  9.6 0.8 copy-start.1
  10.4 0.8 copy-start.2
  11.2 0.7 copy-start.3
  11.9 7.3 %copy-start.4 = (bf16[864,864]{1,0:T(8,128)(2,1)S(1)}, bf16[864,864]{1,0:T(8,128)(2,1)}, u32[]{:S(2)}) copy-start(bf16[864,864]{1,0:T(8,128)(2,1)} %param.20) | copy-start | bytes 4478980
  22.5 28.7 %all-to-all-start.2 = ((f32[32,88,128]{2,1,0:T(8,128)}), f32[32,88,128]{2,1,0:T(8,128)S(1)}, u32[]{:S(2)}, u32[]{:S(2)}) async-start(f32[32,88,128]{2,1,0:T(8,128)} %compact.3), calls=%async_computation.2 | async-start | bytes 2883584 | tf_op jit(solution)/shard_map/cond/branch_1_fun/all_to_all | solution.py:419
  85.3 1.2 %copy-start.5 = (f32[27,32,512]{2,1,0:T(8,128)}, f32[27,32,512]{2,1,0:T(8,128)S(1)}, u32[]{:S(2)}) copy-start(f32[27,32,512]{2,1,0:T(8,128)S(1)} %get-tuple-element.149) | copy-start | bytes 5308420

commit v2 on v1

--- a/solution.py
+++ b/solution.py
@@ -58,78 +58,21 @@
     return jnp.concatenate(pieces, axis=1)
 
 
-def propagate_kernel(
-    spec, depth, turn, mask, speed, moved, halo_coef, pick, rank, turn_own, most, grid
+def prepare_kernel(
+    spec, turn, mask, grid, low, high, pick, rank, turn_own, most, arrived, arriving
 ):
+    copies = [
+        pltpu.make_async_copy(
+            spec.at[cb * 8 : min(cb * 8 + 8, HELD)],
+            arrived.at[cb * 8 : min(cb * 8 + 8, HELD)],
+            arriving.at[cb],
+        )
+        for cb in range(4)
+    ]
+    for copy in copies:
+        copy.start()
+
     me = lax.axis_index("comp")
-    sub = iota((PAD, LANES), 0)
-    speeds = jnp.zeros((PAD, LANES), jnp.float32)
-    for k in range(HELD):
-        speeds = jnp.where(sub == k, speed[k], speeds)
-    theta = (2.0 * math.pi / NTH) * lax.rem(me * HELD + sub, NTH).astype(jnp.float32)
-
-    def taps(velocity):
-        up = velocity >= 0.0
-        sixth = velocity / 6.0
-        return (
-            sixth * jnp.where(up, 3.0, -3.0),
-            sixth * jnp.where(up, 2.0, 6.0),
-            sixth * jnp.where(up, -6.0, -2.0),
-            jnp.where(up, sixth, 0.0),
-            jnp.where(up, 0.0, -sixth),
-        )
-
-    x_centre, x_ahead, x_back, x_back_two, x_ahead_two = taps(speeds * jnp.cos(theta))
-    y_centre, y_ahead, y_back, y_back_two, y_ahead_two = taps(speeds * jnp.sin(theta))
-    halo_coef[0] = y_back
-    halo_coef[1] = y_back_two
-    halo_coef[2] = y_ahead
-    halo_coef[3] = y_ahead_two
-
-    for r in (0, 1, ROWS + 2, ROWS + 3):
-        grid[r] = jnp.zeros((PAD, COLS), jnp.float32)
-    for cb in range(4):
-        size = min(8, HELD - cb * 8)
-        for rb in range(4):
-            block = spec[cb * 8 : cb * 8 + size, rb * 8 : rb * 8 + 8, :]
-            if size < 8:
-                block = jnp.concatenate(
-                    [block, jnp.zeros((8 - size, 8, COLS), jnp.float32)], axis=0
-                )
-            grid[2 + rb * 8 : 10 + rb * 8, cb * 8 : cb * 8 + 8, :] = jnp.swapaxes(block, 0, 1)
-
-    lane = iota((8, COLS), 1)
-    for cb in range(4):
-        part = slice(cb * 8, cb * 8 + 8)
-        coefs = [
-            wide(c[part])
-            for c in (
-                x_centre + y_centre, x_ahead, x_back, x_back_two, x_ahead_two,
-                y_ahead, y_back, y_back_two, y_ahead_two,
-            )
-        ]
-
-        def row_group(rb, carry):
-            depths = depth[pl.ds(pl.multiple_of(rb * 8, 8), 8), :]
-            for i in range(8):
-                row_step(rb * 8 + i, depths[i : i + 1, :])
-            return carry
-
-        def row_step(r, depth_row):
-            centre = grid[r + 2, part, :]
-            total = coefs[0] * centre
-            total += coefs[1] * jnp.where(lane < COLS - 1, pltpu.roll(centre, COLS - 1, axis=1), 0.0)
-            total += coefs[2] * jnp.where(lane >= 1, pltpu.roll(centre, 1, axis=1), 0.0)
-            total += coefs[3] * jnp.where(lane >= 2, pltpu.roll(centre, 2, axis=1), 0.0)
-            total += coefs[4] * jnp.where(lane < COLS - 2, pltpu.roll(centre, COLS - 2, axis=1), 0.0)
-            total += coefs[5] * grid[r + 3, part, :]
-            total += coefs[6] * grid[r + 1, part, :]
-            total += coefs[7] * grid[r, part, :]
-            total += coefs[8] * grid[r + 4, part, :]
-            moved[r, part, :] = centre - depth_row * total
-
-        lax.fori_loop(0, ROWS // 8, row_group, 0)
-
     sea = mixed_plane(mask[...])
     column = iota((ROWS, COLS), 1)
     count = sea
@@ -163,28 +106,144 @@
             total = jnp.where(index >> 7 == source, value, total)
         turn_own[:, t * LANES : (t + 1) * LANES] = total
 
-
-def propagate(spectrum, depth, turn, mask, speed):
+    for cb in range(4):
+        copies[cb].wait()
+        part = slice(cb * 8, cb * 8 + 8)
+        size = min(8, HELD - cb * 8)
+        for rb in range(4):
+            block = arrived[cb * 8 : cb * 8 + size, rb * 8 : rb * 8 + 8, :]
+            if size < 8:
+                block = jnp.concatenate(
+                    [block, jnp.zeros((8 - size, 8, COLS), jnp.float32)], axis=0
+                )
+            block = jnp.swapaxes(block, 0, 1)
+            grid[rb * 8 : rb * 8 + 8, part, :] = block
+            if rb == 0:
+                low[:, part, :] = block[0:2]
+            if rb == 3:
+                high[:, part, :] = block[6:8]
+
+
+def prepare(spectrum, turn, mask):
     plane = jax.ShapeDtypeStruct((ROWS, COLS), jnp.int32)
+    edge = jax.ShapeDtypeStruct((2, PAD, COLS), jnp.float32)
+    return pl.pallas_call(
+        prepare_kernel,
+        out_shape=[
+            jax.ShapeDtypeStruct((ROWS, PAD, COLS), jnp.float32),
+            edge,
+            edge,
+            plane,
+            plane,
+            jax.ShapeDtypeStruct((8, COLS), jnp.float32),
+            jax.ShapeDtypeStruct((1,), jnp.int32),
+        ],
+        in_specs=[pl.BlockSpec(memory_space=pl.ANY), VMEM, VMEM],
+        out_specs=[VMEM] * 6 + [SMEM],
+        scratch_shapes=[
+            pltpu.VMEM((PAD, ROWS, COLS), jnp.float32),
+            pltpu.SemaphoreType.DMA((4,)),
+        ],
+        compiler_params=PARAMS,
+        cost_estimate=pl.CostEstimate(flops=2000000, bytes_accessed=4000000, transcendentals=0),
+        name="prepare",
+    )(spectrum, turn, mask)
+
+
+def shifted(tiles, lane):
+    ahead = [pltpu.roll(v, LANES - 1, axis=1) for v in tiles] + [0.0]
+    back = [0.0] + [pltpu.roll(v, 1, axis=1) for v in tiles]
+    ahead_two = [pltpu.roll(v, LANES - 2, axis=1) for v in tiles] + [0.0]
+    back_two = [0.0] + [pltpu.roll(v, 2, axis=1) for v in tiles]
+    return [
+        (
+            jnp.where(lane < LANES - 1, ahead[t], ahead[t + 1]),
+            jnp.where(lane >= 1, back[t + 1], back[t]),
+            jnp.where(lane < LANES - 2, ahead_two[t], ahead_two[t + 1]),
+            jnp.where(lane >= 2, back_two[t + 1], back_two[t]),
+        )
+        for t in range(TILES)
+    ]
+
+
+def propagate_kernel(grid, depth, speed, moved, halo_coef):
+    me = lax.axis_index("comp")
+    sub = iota((PAD, LANES), 0)
+    speeds = jnp.zeros((PAD, LANES), jnp.float32)
+    for k in range(HELD):
+        speeds = jnp.where(sub == k, speed[k], speeds)
+    theta = (2.0 * math.pi / NTH) * lax.rem(me * HELD + sub, NTH).astype(jnp.float32)
+
+    def taps(velocity):
+        up = velocity >= 0.0
+        sixth = velocity / 6.0
+        return (
+            sixth * jnp.where(up, 3.0, -3.0),
+            sixth * jnp.where(up, 2.0, 6.0),
+            sixth * jnp.where(up, -6.0, -2.0),
+            jnp.where(up, sixth, -sixth),
+            up,
+        )
+
+    x_centre, x_ahead, x_back, x_far, x_up = taps(speeds * jnp.cos(theta))
+    y_centre, y_ahead, y_back, y_far, y_up = taps(speeds * jnp.sin(theta))
+    halo_coef[0] = y_back
+    halo_coef[1] = jnp.where(y_up, y_far, 0.0)
+    halo_coef[2] = y_ahead
+    halo_coef[3] = jnp.where(y_up, 0.0, y_far)
+    centre_coef = x_centre + y_centre
+
+    lane = iota((8, LANES), 1)
+    for cb in range(4):
+        part = slice(cb * 8, cb * 8 + 8)
+        c0, xa, xb, xf, xu, ya, yb, yf, yu = [
+            c[part]
+            for c in (centre_coef, x_ahead, x_back, x_far, x_up, y_ahead, y_back, y_far, y_up)
+        ]
+
+        def row_step(r, rows, depth_row):
+            centre = [grid[r, part, t * LANES : (t + 1) * LANES] for t in range(TILES)]
+
+            def near(i, t):
+                if not 0 <= rows + i < ROWS:
+                    return jnp.zeros((8, LANES), jnp.float32)
+                return grid[r + i, part, t * LANES : (t + 1) * LANES]
+
+            for t, (ahead, back, ahead_two, back_two) in enumerate(shifted(centre, lane)):
+                total = c0 * centre[t] + xa * ahead + xb * back
+                total += xf * jnp.where(xu, back_two, ahead_two)
+                total += ya * near(1, t) + yb * near(-1, t)
+                total += yf * jnp.where(yu, near(-2, t), near(2, t))
+                lanes = slice(t * LANES, (t + 1) * LANES)
+                moved[r, part, lanes] = centre[t] - depth_row[:, lanes] * total
+
+        def group(rb, first):
+            depths = depth[pl.ds(pl.multiple_of(rb * 8, 8), 8), :]
+            for i in range(8):
+                row_step(rb * 8 + i, first + i, depths[i : i + 1, :])
+
+        group(0, 0)
+
+        @pl.loop(1, 3)
+        def _(rb):
+            group(rb, 8)
+
+        group(3, 24)
+
+
+def propagate(grid, depth, speed):
     return pl.pallas_call(
         propagate_kernel,
         out_shape=[
             jax.ShapeDtypeStruct((ROWS, PAD, COLS), jnp.float32),
             jax.ShapeDtypeStruct((4, PAD, LANES), jnp.float32),
-            plane,
-            plane,
-            jax.ShapeDtypeStruct((8, COLS), jnp.float32),
-            jax.ShapeDtypeStruct((1,), jnp.int32),
         ],
-        in_specs=[VMEM, VMEM, VMEM, VMEM, SMEM],
-        out_specs=[VMEM, VMEM, VMEM, VMEM, VMEM, SMEM],
-        scratch_shapes=[
-            pltpu.VMEM((ROWS + 4, PAD, COLS), jnp.float32),
-        ],
+        in_specs=[VMEM, VMEM, SMEM],
+        out_specs=[VMEM, VMEM],
         compiler_params=PARAMS,
-        cost_estimate=pl.CostEstimate(flops=20000000, bytes_accessed=5000000, transcendentals=0),
+        cost_estimate=pl.CostEstimate(flops=20000000, bytes_accessed=4000000, transcendentals=0),
         name="propagate",
-    )(spectrum, depth, turn, mask, speed)
+    )(grid, depth, speed)
 
 
 def block_rows(tiles):
@@ -193,7 +252,7 @@
 
 def compact_kernel(tiles, moved, low, high, depth, halo_coef, pick, out, mixed, edge):
     lane = iota((8, LANES), 1)
-    back, back_two, ahead, ahead_two = [wide(halo_coef[i, 0:HELD, :]) for i in range(4)]
+    back, back_two, ahead, ahead_two = [wide(halo_coef[i]) for i in range(4)]
     terms = {
         0: back * low[1] + back_two * low[0],
         1: back_two * low[1],
@@ -203,7 +262,7 @@
     edge_of = {}
     for r, term in terms.items():
         edge_of[r] = len(edge_of)
-        edge[edge_of[r], 0:HELD, :] = moved[r, 0:HELD, :] - depth[r : r + 1, :] * term
+        edge[edge_of[r]] = moved[r] - depth[r : r + 1, :] * term
 
     def load(r, cb, t):
         rows, lanes = slice(cb * 8, cb * 8 + 8), slice(t * LANES, (t + 1) * LANES)
@@ -425,11 +484,10 @@
     count = lax.axis_size("tile")
     forward = [(i, i + 1) for i in range(count - 1)]
     backward = [(i + 1, i) for i in range(count - 1)]
-    low = lax.ppermute(jnp.swapaxes(spectrum[:, ROWS - 2 :, :], 0, 1), "tile", forward)
-    high = lax.ppermute(jnp.swapaxes(spectrum[:, :2, :], 0, 1), "tile", backward)
-    moved, halo_coef, pick, rank, turn_own, most = propagate(
-        spectrum, depth, turn, sea_mask, speed
-    )
+    grid, first, last, pick, rank, turn_own, most = prepare(spectrum, turn, sea_mask)
+    low = lax.ppermute(last, "tile", forward)
+    high = lax.ppermute(first, "tile", backward)
+    moved, halo_coef = propagate(grid, depth, speed)
     ncomp = growth.shape[0]
     keep = jnp.broadcast_to((1.0 + 0.2 * growth)[:, None], (ncomp, LANES))
     lose = jnp.broadcast_to((0.2 * dissipation)[:, None], (ncomp, LANES))

time: 87 us -> 86.5 us (level)
  local copies, waits for them, and re-layouts: 6.71 us -> 4.72 us
  starting transfers between devices: 14.7 us -> 15.9 us
    pallas_call x1, Pallas kernels: 6.62 us -> 3.7 us  [propagate(): pl.pallas_call(propagate_kernel, out_shape=[jax.ShapeDtypeStruct((ROWS, P...]
    pallas_call x0 -> x1, Pallas kernels: none -> 2.65 us  [prepare(): pl.pallas_call(prepare_kernel, out_shape=[jax.ShapeDtypeStruct((ROWS, PAD...]
    slice x1 -> x0, local copies, waits for them, and re-layouts: 1.3 us -> none  [shards(): spectrum[:, :2, :]]
    all_to_all x1, starting transfers between devices: 8.05 us -> 9.19 us  [exchange(): lax.all_to_all(blocks, 'comp', split_axis=0, concat_axis=0, tiled=True)]
    unnamed x22 -> x20, local copies, waits for them, and re-layouts: 5.07 us -> 4.38 us
  transfers between devices with their start and end apart: 3 -> 3, of which waited for: 1 -> 2; matrix products, arithmetic and copies ran while one was open for 0% -> 0% of each run, Pallas kernels for 8% -> 4%
where the time goes in v2:
time: 86.5 us; the launch traced here: 86.1 us
  blocking collectives  26.3 us (30%)
  waiting for transfers between devices  21.2 us (25%)
  Pallas kernels  16.9 us (20%)
  starting transfers between devices  15.9 us (18%)
  local copies, waits for them, and re-layouts  4.72 us (5%)
    all_to_all x1, blocking collectives, exchange(): lax.all_to_all(blocks, 'comp', split_axis=0, concat_axis=0, tiled=True)  26.3 us
    all_to_all x1, waiting for transfers between devices, exchange(): lax.all_to_all(blocks, 'comp', split_axis=0, concat_axis=0, tiled=True)  20.6 us
    all_to_all x1, starting transfers between devices, exchange(): lax.all_to_all(blocks, 'comp', split_axis=0, concat_axis=0, tiled=True)  9.19 us
    pallas_call x1, Pallas kernels, sources(): pl.pallas_call(functools.partial(source_kernel, tiles), out_shape=jax.Sha...  4.94 us
    ppermute x1, starting transfers between devices, shards(): low = lax.ppermute(last, 'tile', forward)  4.76 us
    unnamed x20, local copies, waits for them, and re-layouts  4.38 us
    pallas_call x1, Pallas kernels, propagate(): pl.pallas_call(propagate_kernel, out_shape=[jax.ShapeDtypeStruct((ROWS, P...  3.7 us
    pallas_call x1, Pallas kernels, compact(): pl.pallas_call(functools.partial(compact_kernel, tiles), out_shape=jax.Sh...  3.2 us
  transfers between devices with their start and end apart: 3, of which 2 were waited for; matrix products, arithmetic and copies ran while one was open for 0% of the time, Pallas kernels for 4%

profile of v2, /device:TPU:97, one launch (start us, length us, event | category | flops | bytes accessed | tf_op | source)
XLA Modules:
  0.0 86.1 jit_solution(10566741499821873416)
XLA Ops:
  0.0 0.0 copy-start
  0.0 1.5 %copy-done = f32[27,32,512]{2,1,0:T(8,128)S(1)} copy-done((f32[27,32,512]{2,1,0:T(8,128)S(1)}, f32[27,32,512]{2,1,0:T(8,128)}, u32[]{:S(2)}) %copy-start) | copy-done | bytes 1769496
  1.5 0.0 copy-start.1
  1.5 0.8 copy-done.1
  2.3 0.8 copy-done.2
  3.2 0.0 copy-start.10
  3.2 0.0 copy-start.11
  3.2 2.6 %prepare.1 = (f32[32,32,512]{2,1,0:T(8,128)S(1)}, f32[2,32,512]{2,1,0:T(8,128)S(1)}, f32[2,32,512]{2,1,0:T(8,128)S(1)}, s32[32,512]{1,0:T(8,128)S(1)}, s32[32,51...) custom-call(f32[27,32,512]{2,1,0:T(8,128)S(1)} %copy-done, f32[32,512]{1,0:T(8,128)S(1)} %copy-done.1, ...), custom_call_target="tpu_custom_call" | custom-call | flops 2000000 | bytes 4000000 | tf_op jit(solution)/shard_map/prepare/pallas_call | solution.py:130
  5.8 4.8 %collective-permute-start = (f32[2,32,512]{2,1,0:T(8,128)S(1)}, f32[2,32,512]{2,1,0:T(8,128)S(1)}, u32[]{:S(2)}, u32[]{:S(2)}) collective-permute-start(f32[2,32,512]{2,1,0:T(8,128)S(1)} %get-tuple-element.98), channel_id=1, source_target_pairs={{0,1},{1,2},{2,3},{3,4},{4,5},{5,6},{6,7},{8,9},{9,10},{10,11},{11... | collective-permute-start | bytes 393224 | tf_op jit(solution)/shard_map/ppermute | solution.py:488
  10.6 1.9 %collective-permute-start.1 = (f32[2,32,512]{2,1,0:T(8,128)S(1)}, f32[2,32,512]{2,1,0:T(8,128)S(1)}, u32[]{:S(2)}, u32[]{:S(2)}) collective-permute-start(f32[2,32,512]{2,1,0:T(8,128)S(1)} %get-tuple-element.99), channel_id=1, source_target_pairs={{1,0},{2,1},{3,2},{4,3},{5,4},{6,5},{7,6},{9,8},{10,9},{11,10},{12... | collective-permute-start | bytes 393224 | tf_op jit(solution)/shard_map/ppermute | solution.py:489
  13.2 0.0 copy-done.3
  13.2 0.0 copy-done.6
  13.2 3.7 %propagate.1 = (f32[32,32,512]{2,1,0:T(8,128)S(1)}, f32[4,32,128]{2,1,0:T(8,128)S(1)}) custom-call(f32[32,32,512]{2,1,0:T(8,128)S(1)} %get-tuple-element.96.grid, f32[32,512]{1,0:T(8,128)S(1)} %copy-done.6, f32[27]{0:T(128)S(1)} %copy-done.3), custom_call_target="tpu_custom_call" | custom-call | flops 20000000 | bytes 4000000 | tf_op jit(solution)/shard_map/propagate/pallas_call | solution.py:235
  16.9 0.0 collective-permute-done
  16.9 0.6 collective-permute-done.1
  17.5 0.0 copy-done.4
  17.5 0.0 copy-done.9
  17.5 0.0 copy-done.10
  17.5 0.0 copy-done.11
  17.6 67.3 %conditional.1 = (f32[27,32,512]{2,1,0:T(8,128)S(1)}) conditional(s32[]{:T(128)} %bitcast, (f32[32,32,512]{2,1,0:T(8,128)S(1)}, f32[2,32,512]{2,1,0:T(8,128)S(1)}, f32[2,32,512]{2,1,0:T(8,128)S(1)}, f32[32,512]{1,0:T(8,128)S(1)}, f32[4,32,128]{2,1,0:T(8,128)S(1)}, /*index=5*/s32[32,512]{1,0:T(8,128)S(1)}, f32[8,512]{1,0:T(8,128)S(1)}, ...), branch_computations={%region_0.0_spmd, %region_1.0_spmd} | conditional | flops 1538826496 | bytes 24342724 | solution.py:506
  17.6 3.2 %compact.3 = f32[32,88,128]{2,1,0:T(8,128)} custom-call(f32[32,32,512]{2,1,0:T(8,128)S(1)} %get-tuple-element.73.moved, f32[2,32,512]{2,1,0:T(8,128)S(1)} %get-tuple-element.74.low, f32[2,32,512]{2,1,0:T(8,128)S(1)} %get-tuple-element.75.high, f32[32,512]{1,0:T(8,128)S(1)} %get-tuple-element.76.depth, f32[4,32,128]{2,1,0:T(8,128)S(1)} %get-tuple-element.77.halo_coef, ...), custom_call_target="tpu_custom_call" | custom-call | flops 5000000 | bytes 4000000 | tf_op jit(solution)/shard_map/cond/branch_1_fun/compact/pallas_call | solution.py:306
  20.8 9.2 %all-to-all-start.2 = ((f32[32,88,128]{2,1,0:T(8,128)}), f32[32,88,128]{2,1,0:T(8,128)S(1)}, u32[]{:S(2)}, u32[]{:S(2)}) async-start(f32[32,88,128]{2,1,0:T(8,128)} %compact.3), calls=%async_computation.2 | async-start | bytes 2883584 | tf_op jit(solution)/shard_map/cond/branch_1_fun/all_to_all | solution.py:478
  30.0 20.6 %all-to-all-done.2.points = f32[32,88,128]{2,1,0:T(8,128)S(1)} async-done(((f32[32,88,128]{2,1,0:T(8,128)}), f32[32,88,128]{2,1,0:T(8,128)S(1)}, u32[]{:S(2)}, u32[]{:S(2)}) %all-to-all-start.2) | async-done | bytes 1441824 | tf_op jit(solution)/shard_map/cond/branch_1_fun/all_to_all | solution.py:478
  50.6 0.2 broadcast_in_dim.7.keep
  50.8 0.2 broadcast_in_dim.17.lose
  51.0 4.9 %sources.3 = f32[32,88,128]{2,1,0:T(8,128)S(1)} custom-call(f32[32,88,128]{2,1,0:T(8,128)S(1)} %all-to-all-done.2.points, f32[8,512]{1,0:T(8,128)S(1)} %get-tuple-element.79.turn_own, f32[24]{0:T(128)S(1)} %get-tuple-element.116.refraction, f32[864,128]{1,0:T(8,128)S(1)} %broadcast_in_dim.7.keep, f32[864,128]{1,0:T(8,128)S(1)} %broadcast_in_dim.17.lose, ...), custom_call_target="tpu_custom_call" | custom-call | flops 1146617856 | bytes 6000000 | tf_op jit(solution)/shard_map/cond/branch_1_fun/sources/pallas_call | solution.py:400
  55.9 0.0 copy-start.8
  55.9 26.3 %all_to_all.17.result = f32[32,88,128]{2,1,0:T(8,128)S(1)} all-to-all(f32[32,88,128]{2,1,0:T(8,128)S(1)} %sources.3), channel_id=1, replica_groups=mesh['comp'=32,'tile'=8] {'comp'}, dimensions={0} | all-to-all | bytes 2883584 | tf_op jit(solution)/shard_map/cond/branch_1_fun/all_to_all | solution.py:478
  82.2 0.0 copy-done.8
  82.2 2.4 %expand.3 = f32[27,32,512]{2,1,0:T(8,128)S(1)} custom-call(f32[32,88,128]{2,1,0:T(8,128)S(1)} %all_to_all.17.result, s32[32,512]{1,0:T(8,128)S(1)} %copy-done.8), custom_call_target="tpu_custom_call" | custom-call | flops 5000000 | bytes 4000000 | tf_op jit(solution)/shard_map/cond/branch_1_fun/expand/pallas_call | solution.py:465
  84.9 0.0 copy-start.5
  84.9 1.2 %copy-done.5 = f32[27,32,512]{2,1,0:T(8,128)} copy-done((f32[27,32,512]{2,1,0:T(8,128)}, f32[27,32,512]{2,1,0:T(8,128)S(1)}, u32[]{:S(2)}) %copy-start.5) | copy-done | bytes 1769496
  (6 shorter events, 0.0 us)
Async XLA Ops:
  0.0 1.5 %copy-start = (f32[27,32,512]{2,1,0:T(8,128)S(1)}, f32[27,32,512]{2,1,0:T(8,128)}, u32[]{:S(2)}) copy-start(f32[27,32,512]{2,1,0:T(8,128)} %spec.1) | copy-start | bytes 5308420
  1.5 0.8 copy-start.1
  2.3 0.8 copy-start.2
  3.2 10.0 %copy-start.3 = (f32[27]{0:T(128)S(1)}, f32[27]{0:T(128)}, u32[]{:S(2)}) copy-start(f32[27]{0:T(128)} %speed.1) | copy-start | bytes 328
  3.2 10.0 %copy-start.6 = (f32[32,512]{1,0:T(8,128)S(1)}, f32[32,512]{1,0:T(8,128)}, u32[]{:S(2)}) copy-start(f32[32,512]{1,0:T(8,128)} %depth.1) | copy-start | bytes 196612
  3.2 14.4 %copy-start.4 = (bf16[864,864]{1,0:T(8,128)(2,1)S(1)}, bf16[864,864]{1,0:T(8,128)(2,1)}, u32[]{:S(2)}) copy-start(bf16[864,864]{1,0:T(8,128)(2,1)} %param.20) | copy-start | bytes 4478980
  3.2 14.4 %copy-start.9 = (f32[864]{0:T(1024)S(1)}, f32[864]{0:T(1024)}, u32[]{:S(2)}) copy-start(f32[864]{0:T(1024)} %param.18) | copy-start | bytes 10372
  3.2 14.4 %copy-start.10 = (f32[864]{0:T(1024)S(1)}, f32[864]{0:T(1024)}, u32[]{:S(2)}) copy-start(f32[864]{0:T(1024)} %param.19) | copy-start | bytes 10372
  3.2 14.4 %copy-start.11 = (f32[24]{0:T(128)S(1)}, f32[24]{0:T(128)}, u32[]{:S(2)}) copy-start(f32[24]{0:T(128)} %param.17) | copy-start | bytes 292
  5.8 11.1 %collective-permute-start = (f32[2,32,512]{2,1,0:T(8,128)S(1)}, f32[2,32,512]{2,1,0:T(8,128)S(1)}, u32[]{:S(2)}, u32[]{:S(2)}) collective-permute-start(f32[2,32,512]{2,1,0:T(8,128)S(1)} %get-tuple-element.98), channel_id=1, source_target_pairs={{0,1},{1,2},{2,3},{3,4},{4,5},{5,6},{6,7},{8,9},{9,10},{10,11},{11... | collective-permute-start | bytes 393224 | tf_op jit(solution)/shard_map/ppermute | solution.py:488
  10.6 6.9 %collective-permute-start.1 = (f32[2,32,512]{2,1,0:T(8,128)S(1)}, f32[2,32,512]{2,1,0:T(8,128)S(1)}, u32[]{:S(2)}, u32[]{:S(2)}) collective-permute-start(f32[2,32,512]{2,1,0:T(8,128)S(1)} %get-tuple-element.99), channel_id=1, source_target_pairs={{1,0},{2,1},{3,2},{4,3},{5,4},{6,5},{7,6},{9,8},{10,9},{11,10},{12... | collective-permute-start | bytes 393224 | tf_op jit(solution)/shard_map/ppermute | solution.py:489
  20.8 29.8 %all-to-all-start.2 = ((f32[32,88,128]{2,1,0:T(8,128)}), f32[32,88,128]{2,1,0:T(8,128)S(1)}, u32[]{:S(2)}, u32[]{:S(2)}) async-start(f32[32,88,128]{2,1,0:T(8,128)} %compact.3), calls=%async_computation.2 | async-start | bytes 2883584 | tf_op jit(solution)/shard_map/cond/branch_1_fun/all_to_all | solution.py:478
  55.9 26.3 %copy-start.8 = (s32[32,512]{1,0:T(8,128)S(1)}, s32[32,512]{1,0:T(8,128)}, u32[]{:S(2)}) copy-start(s32[32,512]{1,0:T(8,128)} %get-tuple-element.85.rank) | copy-start | bytes 196612 | tf_op jit(solution)/shard_map/cond
  84.9 1.2 %copy-start.5 = (f32[27,32,512]{2,1,0:T(8,128)}, f32[27,32,512]{2,1,0:T(8,128)S(1)}, u32[]{:S(2)}) copy-start(f32[27,32,512]{2,1,0:T(8,128)S(1)} %get-tuple-element.155) | copy-start | bytes 5308420

commit v3 on v2

--- a/solution.py
+++ b/solution.py
@@ -18,6 +18,7 @@
 TILES = COLS // LANES
 VMEM = pl.BlockSpec(memory_space=pltpu.VMEM)
 SMEM = pl.BlockSpec(memory_space=pltpu.SMEM)
+ANY = pl.BlockSpec(memory_space=pl.ANY)
 PARAMS = pltpu.CompilerParams(vmem_limit_bytes=24 * 2**20)
 
 
@@ -58,20 +59,38 @@
     return jnp.concatenate(pieces, axis=1)
 
 
-def prepare_kernel(
-    spec, turn, mask, grid, low, high, pick, rank, turn_own, most, arrived, arriving
-):
-    copies = [
-        pltpu.make_async_copy(
-            spec.at[cb * 8 : min(cb * 8 + 8, HELD)],
-            arrived.at[cb * 8 : min(cb * 8 + 8, HELD)],
-            arriving.at[cb],
-        )
-        for cb in range(4)
-    ]
-    for copy in copies:
-        copy.start()
-
+def prepare_kernel(spec, grid, low, high):
+    for cb in range(4):
+        part = slice(cb * 8, cb * 8 + 8)
+        size = min(8, HELD - cb * 8)
+        for rb in range(4):
+            block = spec[cb * 8 : cb * 8 + size, rb * 8 : rb * 8 + 8, :]
+            if size < 8:
+                block = jnp.concatenate(
+                    [block, jnp.zeros((8 - size, 8, COLS), jnp.float32)], axis=0
+                )
+            block = jnp.swapaxes(block, 0, 1)
+            grid[rb * 8 : rb * 8 + 8, part, :] = block
+            if rb == 0:
+                low[:, part, :] = block[0:2]
+            if rb == 3:
+                high[:, part, :] = block[6:8]
+
+
+def prepare(spectrum):
+    edge = jax.ShapeDtypeStruct((2, PAD, COLS), jnp.float32)
+    return pl.pallas_call(
+        prepare_kernel,
+        out_shape=[jax.ShapeDtypeStruct((ROWS, PAD, COLS), jnp.float32), edge, edge],
+        in_specs=[VMEM],
+        out_specs=[VMEM] * 3,
+        compiler_params=PARAMS,
+        cost_estimate=pl.CostEstimate(flops=2000000, bytes_accessed=4000000, transcendentals=0),
+        name="prepare",
+    )(spectrum)
+
+
+def index_kernel(turn, mask, after, pick, rank, turn_own, most):
     me = lax.axis_index("comp")
     sea = mixed_plane(mask[...])
     column = iota((ROWS, COLS), 1)
@@ -106,48 +125,23 @@
             total = jnp.where(index >> 7 == source, value, total)
         turn_own[:, t * LANES : (t + 1) * LANES] = total
 
-    for cb in range(4):
-        copies[cb].wait()
-        part = slice(cb * 8, cb * 8 + 8)
-        size = min(8, HELD - cb * 8)
-        for rb in range(4):
-            block = arrived[cb * 8 : cb * 8 + size, rb * 8 : rb * 8 + 8, :]
-            if size < 8:
-                block = jnp.concatenate(
-                    [block, jnp.zeros((8 - size, 8, COLS), jnp.float32)], axis=0
-                )
-            block = jnp.swapaxes(block, 0, 1)
-            grid[rb * 8 : rb * 8 + 8, part, :] = block
-            if rb == 0:
-                low[:, part, :] = block[0:2]
-            if rb == 3:
-                high[:, part, :] = block[6:8]
-
-
-def prepare(spectrum, turn, mask):
+
+def make_index(turn, mask, after):
     plane = jax.ShapeDtypeStruct((ROWS, COLS), jnp.int32)
-    edge = jax.ShapeDtypeStruct((2, PAD, COLS), jnp.float32)
-    return pl.pallas_call(
-        prepare_kernel,
+    return pl.pallas_call(
+        index_kernel,
         out_shape=[
-            jax.ShapeDtypeStruct((ROWS, PAD, COLS), jnp.float32),
-            edge,
-            edge,
             plane,
             plane,
             jax.ShapeDtypeStruct((8, COLS), jnp.float32),
             jax.ShapeDtypeStruct((1,), jnp.int32),
         ],
-        in_specs=[pl.BlockSpec(memory_space=pl.ANY), VMEM, VMEM],
-        out_specs=[VMEM] * 6 + [SMEM],
-        scratch_shapes=[
-            pltpu.VMEM((PAD, ROWS, COLS), jnp.float32),
-            pltpu.SemaphoreType.DMA((4,)),
-        ],
-        compiler_params=PARAMS,
-        cost_estimate=pl.CostEstimate(flops=2000000, bytes_accessed=4000000, transcendentals=0),
-        name="prepare",
-    )(spectrum, turn, mask)
+        in_specs=[VMEM, VMEM, ANY],
+        out_specs=[VMEM] * 3 + [SMEM],
+        compiler_params=PARAMS,
+        cost_estimate=pl.CostEstimate(flops=2000000, bytes_accessed=200000, transcendentals=0),
+        name="index",
+    )(turn, mask, after)
 
 
 def shifted(tiles, lane):
@@ -335,8 +329,13 @@
 
 
 def source_kernel(
-    tiles, points, turn_own, refraction, keep, lose, first, second, out, grid, turned, low, pair
+    tiles, points, turn_own, refraction, keep, lose, first_far, second_far, out,
+    grid, turned, low, pair, first, second, arriving,
 ):
+    first_copy = pltpu.make_async_copy(first_far, first, arriving.at[0])
+    first_copy.start()
+    second_copy = pltpu.make_async_copy(second_far, second, arriving.at[1])
+    second_copy.start()
     ncomp = turned.shape[0]
     nfreq = ncomp // NTH
     width = NTH + 4
@@ -371,21 +370,15 @@
         low[m : m + chunk, :] = value.astype(jnp.bfloat16)
         energy += jnp.sum(value, axis=0, keepdims=True)
     energy = energy / ncomp
-    for m in range(0, ncomp, chunk):
-        partner = jnp.dot(
-            first[m : m + chunk, :], low[...], preferred_element_type=jnp.float32
-        )
-        pair[m : m + chunk, :] = (turned[m : m + chunk, :] * partner).astype(jnp.bfloat16)
-    for m in range(0, ncomp, chunk):
-        nonlinear = jnp.dot(
-            second[m : m + chunk, :], pair[...], preferred_element_type=jnp.float32
-        )
-        for slot in range(tiles):
-            lanes = slice(slot * LANES, (slot + 1) * LANES)
-            scale = keep[m : m + chunk, :] - lose[m : m + chunk, :] * energy[:, lanes]
-            turned[m : m + chunk, lanes] = (
-                turned[m : m + chunk, lanes] * scale + 0.2 * nonlinear[:, lanes]
-            )
+    first_copy.wait()
+    partner = jnp.dot(first[...], low[...], preferred_element_type=jnp.float32)
+    pair[...] = (turned[...] * partner).astype(jnp.bfloat16)
+    second_copy.wait()
+    nonlinear = jnp.dot(second[...], pair[...], preferred_element_type=jnp.float32)
+    for slot in range(tiles):
+        lanes = slice(slot * LANES, (slot + 1) * LANES)
+        scale = keep[...] - lose[...] * energy[:, lanes]
+        turned[:, lanes] = turned[:, lanes] * scale + 0.2 * nonlinear[:, lanes]
     for s in range(OWNERS):
         for slot in range(tiles):
             lanes = slice(slot * LANES, (slot + 1) * LANES)
@@ -400,13 +393,16 @@
     return pl.pallas_call(
         functools.partial(source_kernel, tiles),
         out_shape=jax.ShapeDtypeStruct(points.shape, jnp.float32),
-        in_specs=[VMEM, VMEM, SMEM, VMEM, VMEM, VMEM, VMEM],
+        in_specs=[VMEM, VMEM, SMEM, VMEM, VMEM, ANY, ANY],
         out_specs=VMEM,
         scratch_shapes=[
             pltpu.VMEM((ncomp // NTH * (NTH + 4), lanes), jnp.float32),
             pltpu.VMEM((ncomp, lanes), jnp.float32),
             pltpu.VMEM((ncomp, lanes), jnp.bfloat16),
             pltpu.VMEM((ncomp, lanes), jnp.bfloat16),
+            pltpu.VMEM((ncomp, ncomp), jnp.bfloat16),
+            pltpu.VMEM((ncomp, ncomp), jnp.bfloat16),
+            pltpu.SemaphoreType.DMA((2,)),
         ],
         compiler_params=PARAMS,
         cost_estimate=pl.CostEstimate(
@@ -416,9 +412,7 @@
     )(points, turn_own, refraction, keep, lose, first, second)
 
 
-def expand_kernel(tiles, result, rank, out, mixed):
-    lane = iota((8, LANES), 1)
-
+def expand_kernel(tiles, result, rank, mixed):
     def owner_group(g, carry):
         ranks = rank[pl.ds(pl.multiple_of(g * 8, 8), 8), :]
         for i in range(8):
@@ -447,31 +441,52 @@
                 )
 
     lax.fori_loop(0, OWNERS // 8, owner_group, 0)
+
+
+def expand(tiles, result, rank):
+    return pl.pallas_call(
+        functools.partial(expand_kernel, tiles),
+        out_shape=jax.ShapeDtypeStruct((OWNERS, PAD, COLS), jnp.float32),
+        in_specs=[VMEM] * 2,
+        out_specs=VMEM,
+        compiler_params=PARAMS,
+        cost_estimate=pl.CostEstimate(flops=5000000, bytes_accessed=4000000, transcendentals=0),
+        name="expand",
+    )(result, rank)
+
+
+def finish_kernel(mixed, out, done, leaving):
+    lane = iota((8, LANES), 1)
+    copies = []
     for cb in range(4):
         size = min(8, HELD - cb * 8)
         for g in range(4):
             for t in range(TILES):
-                rows = [
-                    mixed[(g ^ t) * 8 + j, cb * 8 : cb * 8 + 8, t * LANES : (t + 1) * LANES]
-                    for j in range(8)
-                ]
+                lanes = slice(t * LANES, (t + 1) * LANES)
+                rows = [mixed[(g ^ t) * 8 + j, cb * 8 : cb * 8 + 8, lanes] for j in range(8)]
                 block = jnp.swapaxes(jnp.stack(butterfly(rows, lane)), 0, 1)
-                out[cb * 8 : cb * 8 + size, g * 8 : g * 8 + 8, t * LANES : (t + 1) * LANES] = block[
-                    0:size
-                ]
-
-
-def expand(tiles, result, rank):
-    return pl.pallas_call(
-        functools.partial(expand_kernel, tiles),
+                done[cb * 8 : cb * 8 + size, g * 8 : g * 8 + 8, lanes] = block[0:size]
+        part = slice(cb * 8, cb * 8 + size)
+        copies.append(pltpu.make_async_copy(done.at[part], out.at[part], leaving.at[cb]))
+        copies[cb].start()
+    for copy in copies:
+        copy.wait()
+
+
+def finish(mixed):
+    return pl.pallas_call(
+        finish_kernel,
         out_shape=jax.ShapeDtypeStruct((HELD, ROWS, COLS), jnp.float32),
-        in_specs=[VMEM] * 2,
-        out_specs=VMEM,
-        scratch_shapes=[pltpu.VMEM((OWNERS, PAD, COLS), jnp.float32)],
+        in_specs=[VMEM],
+        out_specs=ANY,
+        scratch_shapes=[
+            pltpu.VMEM((HELD, ROWS, COLS), jnp.float32),
+            pltpu.SemaphoreType.DMA((4,)),
+        ],
         compiler_params=PARAMS,
         cost_estimate=pl.CostEstimate(flops=5000000, bytes_accessed=4000000, transcendentals=0),
-        name="expand",
-    )(result, rank)
+        name="finish",
+    )(mixed)
 
 
 def exchange(blocks):
@@ -484,13 +499,16 @@
     count = lax.axis_size("tile")
     forward = [(i, i + 1) for i in range(count - 1)]
     backward = [(i + 1, i) for i in range(count - 1)]
-    grid, first, last, pick, rank, turn_own, most = prepare(spectrum, turn, sea_mask)
+    grid, first, last = prepare(spectrum)
     low = lax.ppermute(last, "tile", forward)
     high = lax.ppermute(first, "tile", backward)
     moved, halo_coef = propagate(grid, depth, speed)
+    pick, rank, turn_own, most = make_index(turn, sea_mask, halo_coef)
     ncomp = growth.shape[0]
     keep = jnp.broadcast_to((1.0 + 0.2 * growth)[:, None], (ncomp, LANES))
     lose = jnp.broadcast_to((0.2 * dissipation)[:, None], (ncomp, LANES))
+
+    keep, lose = lax.optimization_barrier((keep, lose))
 
     def rest(tiles):
         def run(moved, low, high):
@@ -503,7 +521,7 @@
 
         return run
 
-    return lax.cond(most[0] <= 3 * LANES, rest(3), rest(4), moved, low, high)
+    return finish(lax.cond(most[0] <= 3 * LANES, rest(3), rest(4), moved, low, high))
 
 
 def solution(mesh):

time: 86.5 us -> 82.3 us (0.951)
  blocking collectives: 26.3 us -> 54.3 us
  waiting for transfers between devices: 21.2 us -> 0.01 us
  starting transfers between devices: 15.9 us -> 6.94 us
  local copies, waits for them, and re-layouts: 4.72 us -> 1.86 us
  other arithmetic: 0.01 us -> 1.38 us
    all_to_all x1 -> x2, blocking collectives: 26.3 us -> 54.3 us  [exchange(): lax.all_to_all(blocks, 'comp', split_axis=0, concat_axis=0, tiled=True)]
    all_to_all x1 -> x0, waiting for transfers between devices: 20.6 us -> none  [exchange(): lax.all_to_all(blocks, 'comp', split_axis=0, concat_axis=0, tiled=True)]
    all_to_all x1 -> x0, starting transfers between devices: 9.19 us -> none  [exchange(): lax.all_to_all(blocks, 'comp', split_axis=0, concat_axis=0, tiled=True)]
    pallas_call x0 -> x2, Pallas kernels: none -> 3.14 us  [the longest x1 1.76 us: make_index(): pl.pallas_call(index_kernel, out_shape=[plane, plane, jax.ShapeDtypeStruc...]
    unnamed x20 -> x16, local copies, waits for them, and re-layouts: 4.38 us -> 1.51 us
    pallas_call x1, Pallas kernels: 2.65 us -> 0.34 us  [prepare(): pl.pallas_call(prepare_kernel, out_shape=[jax.ShapeDtypeStruct((ROWS, PAD...]
    pallas_call x1, Pallas kernels: 3.2 us -> 2.07 us  [compact(): pl.pallas_call(functools.partial(compact_kernel, tiles), out_shape=jax.Sh...]
  transfers between devices with their start and end apart: 3 -> 2, of which waited for: 2 -> 0; matrix products, arithmetic and copies ran while one was open for 0% -> 2% of each run, Pallas kernels for 4% -> 7%
where the time goes in v3:
time: 82.3 us; the launch traced here: 81.9 us
  blocking collectives  54.3 us (66%)
  Pallas kernels  16.2 us (20%)
  starting transfers between devices  6.94 us (8%)
  local copies, waits for them, and re-layouts  1.86 us (2%)
  other arithmetic  1.38 us (2%)
  between operations  1 us (1%)
    all_to_all x2, blocking collectives, exchange(): lax.all_to_all(blocks, 'comp', split_axis=0, concat_axis=0, tiled=True)  54.3 us
    pallas_call x1, Pallas kernels, sources(): pl.pallas_call(functools.partial(source_kernel, tiles), out_shape=jax.Sha...  5.08 us
    ppermute x1, starting transfers between devices, shards(): low = lax.ppermute(last, 'tile', forward)  5.02 us
    pallas_call x1, Pallas kernels, propagate(): pl.pallas_call(propagate_kernel, out_shape=[jax.ShapeDtypeStruct((ROWS, P...  3.66 us
    pallas_call x1, Pallas kernels, compact(): pl.pallas_call(functools.partial(compact_kernel, tiles), out_shape=jax.Sh...  2.07 us
    ppermute x1, starting transfers between devices, shards(): high = lax.ppermute(first, 'tile', backward)  1.92 us
    pallas_call x1, Pallas kernels, expand(): pl.pallas_call(functools.partial(expand_kernel, tiles), out_shape=jax.Sha...  1.91 us
    pallas_call x1, Pallas kernels, make_index(): pl.pallas_call(index_kernel, out_shape=[plane, plane, jax.ShapeDtypeStruc...  1.76 us
  transfers between devices with their start and end apart: 2, of which 0 were waited for; matrix products, arithmetic and copies ran while one was open for 2% of the time, Pallas kernels for 7%

profile of v3, /device:TPU:97, one launch (start us, length us, event | category | flops | bytes accessed | tf_op | source)
XLA Modules:
  0.0 81.9 jit_solution(15636221236350758792)
XLA Ops:
  0.0 0.0 copy-start
  0.0 1.5 %copy-done = f32[27,32,512]{2,1,0:T(8,128)S(1)} copy-done((f32[27,32,512]{2,1,0:T(8,128)S(1)}, f32[27,32,512]{2,1,0:T(8,128)}, u32[]{:S(2)}) %copy-start) | copy-done | bytes 1769496
  1.5 0.3 prepare.1
  1.8 0.0 copy-start.1
  1.8 0.0 copy-start.2
  1.9 0.0 copy-start.4
  1.9 0.0 copy-start.5
  1.9 0.0 copy-start.7
  1.9 5.0 %collective-permute-start = (f32[2,32,512]{2,1,0:T(8,128)S(1)}, f32[2,32,512]{2,1,0:T(8,128)S(1)}, u32[]{:S(2)}, u32[]{:S(2)}) collective-permute-start(f32[2,32,512]{2,1,0:T(8,128)S(1)} %get-tuple-element.101), channel_id=1, source_target_pairs={{0,1},{1,2},{2,3},{3,4},{4,5},{5,6},{6,7},{8,9},{9,10},{10,11},{11... | collective-permute-start | bytes 393224 | tf_op jit(solution)/shard_map/ppermute | solution.py:503
  6.9 1.9 %collective-permute-start.1 = (f32[2,32,512]{2,1,0:T(8,128)S(1)}, f32[2,32,512]{2,1,0:T(8,128)S(1)}, u32[]{:S(2)}, u32[]{:S(2)}) collective-permute-start(f32[2,32,512]{2,1,0:T(8,128)S(1)} %get-tuple-element.102), channel_id=1, source_target_pairs={{1,0},{2,1},{3,2},{4,3},{5,4},{6,5},{7,6},{9,8},{10,9},{11,10},{12... | collective-permute-start | bytes 393224 | tf_op jit(solution)/shard_map/ppermute | solution.py:504
  8.8 0.7 multiply_add_fusion
  9.5 0.7 broadcast_multiply_fusion
  10.2 0.2 broadcast_in_dim.5
  10.4 0.2 broadcast_in_dim.4
  10.6 0.0 copy-done.3
  10.6 0.0 copy-done.6
  10.6 3.7 %propagate.1 = (f32[32,32,512]{2,1,0:T(8,128)S(1)}, f32[4,32,128]{2,1,0:T(8,128)S(1)}) custom-call(f32[32,32,512]{2,1,0:T(8,128)S(1)} %get-tuple-element.97.grid, f32[32,512]{1,0:T(8,128)S(1)} %copy-done.6, f32[27]{0:T(128)S(1)} %copy-done.3), custom_call_target="tpu_custom_call" | custom-call | flops 20000000 | bytes 4000000 | tf_op jit(solution)/shard_map/propagate/pallas_call | solution.py:229
  14.3 0.0 copy-done.1
  14.3 0.0 copy-done.2
  14.3 1.8 %index.1 = (s32[32,512]{1,0:T(8,128)S(1)}, s32[32,512]{1,0:T(8,128)S(1)}, f32[8,512]{1,0:T(8,128)S(1)}, s32[1]{0:T(128)}) custom-call(f32[32,512]{1,0:T(8,128)S(1)} %copy-done.1, s32[32,512]{1,0:T(8,128)S(1)} %copy-done.2, f32[4,32,128]{2,1,0:T(8,128)S(1)} %get-tuple-element.98.after), custom_call_target="tpu_custom_call" | custom-call | flops 2000000 | bytes 200000 | tf_op jit(solution)/shard_map/index/pallas_call | solution.py:131
  16.7 0.0 collective-permute-done
  16.7 0.0 collective-permute-done.1
  16.7 0.0 copy-done.4
  16.7 0.0 copy-done.5
  16.8 0.0 copy-done.7
  16.8 63.6 %conditional.1 = (f32[32,32,512]{2,1,0:T(8,128)S(1)}) conditional(s32[]{:T(128)} %bitcast, (f32[32,32,512]{2,1,0:T(8,128)S(1)}, f32[2,32,512]{2,1,0:T(8,128)S(1)}, f32[2,32,512]{2,1,0:T(8,128)S(1)}, f32[32,512]{1,0:T(8,128)S(1)}, f32[4,32,128]{2,1,0:T(8,128)S(1)}, /*index=5*/s32[32,512]{1,0:T(8,128)S(1)}, f32[8,512]{1,0:T(8,128)S(1)}, ...), branch_computations={%region_0.0_spmd, %region_1.0_spmd} | conditional | flops 1538823680 | bytes 21340040 | solution.py:524
  16.8 2.1 %compact.3 = f32[32,88,128]{2,1,0:T(8,128)S(1)} custom-call(f32[32,32,512]{2,1,0:T(8,128)S(1)} %get-tuple-element.73.moved, f32[2,32,512]{2,1,0:T(8,128)S(1)} %get-tuple-element.74.low, f32[2,32,512]{2,1,0:T(8,128)S(1)} %get-tuple-element.75.high, f32[32,512]{1,0:T(8,128)S(1)} %get-tuple-element.76.depth, f32[4,32,128]{2,1,0:T(8,128)S(1)} %get-tuple-element.77.halo_coef, ...), custom_call_target="tpu_custom_call" | custom-call | flops 5000000 | bytes 4000000 | tf_op jit(solution)/shard_map/cond/branch_1_fun/compact/pallas_call | solution.py:300
  18.9 29.3 %all_to_all.18.points = f32[32,88,128]{2,1,0:T(8,128)S(1)} all-to-all(f32[32,88,128]{2,1,0:T(8,128)S(1)} %compact.3), channel_id=1, replica_groups=mesh['comp'=32,'tile'=8] {'comp'}, dimensions={0} | all-to-all | bytes 2883584 | tf_op jit(solution)/shard_map/cond/branch_1_fun/all_to_all | solution.py:493
  48.2 5.1 %sources.3 = f32[32,88,128]{2,1,0:T(8,128)S(1)} custom-call(f32[32,88,128]{2,1,0:T(8,128)S(1)} %all_to_all.18.points, f32[8,512]{1,0:T(8,128)S(1)} %get-tuple-element.79.turn_own, f32[24]{0:T(128)S(1)} %get-tuple-element.80.refraction, f32[864,128]{1,0:T(8,128)S(1)} %get-tuple-element.81.keep, f32[864,128]{1,0:T(8,128)S(1)} %get-tuple-element.82.lose, ...), custom_call_target="tpu_custom_call" | custom-call | flops 1146617856 | bytes 6000000 | tf_op jit(solution)/shard_map/cond/branch_1_fun/sources/pallas_call | solution.py:393
  53.2 25.0 %all_to_all.19.result = f32[32,88,128]{2,1,0:T(8,128)S(1)} all-to-all(f32[32,88,128]{2,1,0:T(8,128)S(1)} %sources.3), channel_id=1, replica_groups=mesh['comp'=32,'tile'=8] {'comp'}, dimensions={0} | all-to-all | bytes 2883584 | tf_op jit(solution)/shard_map/cond/branch_1_fun/all_to_all | solution.py:493
  78.2 1.9 %expand.3 = f32[32,32,512]{2,1,0:T(8,128)S(1)} custom-call(f32[32,88,128]{2,1,0:T(8,128)S(1)} %all_to_all.19.result, s32[32,512]{1,0:T(8,128)S(1)} %get-tuple-element.85.rank), custom_call_target="tpu_custom_call" | custom-call | flops 5000000 | bytes 4000000 | tf_op jit(solution)/shard_map/cond/branch_1_fun/expand/pallas_call | solution.py:447
  80.3 1.4 %finish.1 = f32[27,32,512]{2,1,0:T(8,128)} custom-call(f32[32,32,512]{2,1,0:T(8,128)S(1)} %get-tuple-element.108.mixed), custom_call_target="tpu_custom_call" | custom-call | flops 5000000 | bytes 4000000 | tf_op jit(solution)/shard_map/finish/pallas_call | solution.py:477
  (2 shorter events, 0.0 us)
Async XLA Ops:
  0.0 1.5 %copy-start = (f32[27,32,512]{2,1,0:T(8,128)S(1)}, f32[27,32,512]{2,1,0:T(8,128)}, u32[]{:S(2)}) copy-start(f32[27,32,512]{2,1,0:T(8,128)} %spec.1) | copy-start | bytes 5308420
  1.5 9.1 %copy-start.3 = (f32[27]{0:T(128)S(1)}, f32[27]{0:T(128)}, u32[]{:S(2)}) copy-start(f32[27]{0:T(128)} %speed.1) | copy-start | bytes 328
  1.5 9.1 %copy-start.6 = (f32[32,512]{1,0:T(8,128)S(1)}, f32[32,512]{1,0:T(8,128)}, u32[]{:S(2)}) copy-start(f32[32,512]{1,0:T(8,128)} %depth.1) | copy-start | bytes 196612
  1.8 12.4 %copy-start.1 = (f32[32,512]{1,0:T(8,128)S(1)}, f32[32,512]{1,0:T(8,128)}, u32[]{:S(2)}) copy-start(f32[32,512]{1,0:T(8,128)} %turn.1) | copy-start | bytes 196612
  1.8 12.4 %copy-start.2 = (s32[32,512]{1,0:T(8,128)S(1)}, s32[32,512]{1,0:T(8,128)}, u32[]{:S(2)}) copy-start(s32[32,512]{1,0:T(8,128)} %mask.1) | copy-start | bytes 196612
  1.9 14.9 %copy-start.4 = (bf16[864,864]{1,0:T(8,128)(2,1)S(1)}, bf16[864,864]{1,0:T(8,128)(2,1)}, u32[]{:S(2)}) copy-start(bf16[864,864]{1,0:T(8,128)(2,1)} %param.20) | copy-start | bytes 4478980
  1.9 14.9 %copy-start.5 = (bf16[864,864]{1,0:T(8,128)(2,1)S(1)}, bf16[864,864]{1,0:T(8,128)(2,1)}, u32[]{:S(2)}) copy-start(bf16[864,864]{1,0:T(8,128)(2,1)} %param.21) | copy-start | bytes 4478980
  1.9 14.9 %copy-start.7 = (f32[24]{0:T(128)S(1)}, f32[24]{0:T(128)}, u32[]{:S(2)}) copy-start(f32[24]{0:T(128)} %param.17) | copy-start | bytes 292
  1.9 14.8 %collective-permute-start = (f32[2,32,512]{2,1,0:T(8,128)S(1)}, f32[2,32,512]{2,1,0:T(8,128)S(1)}, u32[]{:S(2)}, u32[]{:S(2)}) collective-permute-start(f32[2,32,512]{2,1,0:T(8,128)S(1)} %get-tuple-element.101), channel_id=1, source_target_pairs={{0,1},{1,2},{2,3},{3,4},{4,5},{5,6},{6,7},{8,9},{9,10},{10,11},{11... | collective-permute-start | bytes 393224 | tf_op jit(solution)/shard_map/ppermute | solution.py:503
  6.9 9.8 %collective-permute-start.1 = (f32[2,32,512]{2,1,0:T(8,128)S(1)}, f32[2,32,512]{2,1,0:T(8,128)S(1)}, u32[]{:S(2)}, u32[]{:S(2)}) collective-permute-start(f32[2,32,512]{2,1,0:T(8,128)S(1)} %get-tuple-element.102), channel_id=1, source_target_pairs={{1,0},{2,1},{3,2},{4,3},{5,4},{6,5},{7,6},{9,8},{10,9},{11,10},{12... | collective-permute-start | bytes 393224 | tf_op jit(solution)/shard_map/ppermute | solution.py:504

commit v4 on v3

--- a/solution.py
+++ b/solution.py
@@ -240,11 +240,33 @@
     )(grid, depth, speed)
 
 
-def block_rows(tiles):
-    return (HELD * tiles + 7) // 8 * 8
-
-
-def compact_kernel(tiles, moved, low, high, depth, halo_coef, pick, out, mixed, edge):
+SHORT = 112
+KINDS = ((2, SHORT), (3, 0), (4, 0))
+
+
+def slots_of(kind):
+    return kind[0] + (kind[1] > 0)
+
+
+def block_rows(kind):
+    return (24 * slots_of(kind) + 3 * kind[0] + 7) // 8 * 8
+
+
+def tuck(row):
+    spare = iota((8, LANES), 0) * 16 + (iota((8, LANES), 1) & 15)
+    return lane_gather(jnp.broadcast_to(row, (8, LANES)), spare)
+
+
+def untuck(rows):
+    lane = iota((8, LANES), 1)
+    value = lane_gather(rows, SHORT + (lane & 15))
+    value = jnp.where(iota((8, LANES), 0) == lane >> 4, value, 0.0)
+    for step in (4, 2, 1):
+        value = value + pltpu.roll(value, step, axis=0)
+    return value
+
+
+def compact_kernel(kind, moved, low, high, depth, halo_coef, pick, out, mixed, edge):
     lane = iota((8, LANES), 1)
     back, back_two, ahead, ahead_two = [wide(halo_coef[i]) for i in range(4)]
     terms = {
@@ -275,11 +297,14 @@
             owner_step(g * 8 + i, picks[i : i + 1, :])
         return carry
 
+    whole, short = kind
+
     def owner_step(d, pick_row):
-        for slot in range(tiles):
+        for slot in range(slots_of(kind)):
             index = jnp.broadcast_to(pick_row[:, slot * LANES : (slot + 1) * LANES], (8, LANES))
             tile_of = index >> 7
             index = index & (LANES - 1)
+            values = []
             for cb in range(4):
                 total = lane_gather(
                     mixed[d, cb * 8 : cb * 8 + 8, slot * LANES : (slot + 1) * LANES], index
@@ -287,19 +312,23 @@
                 for source in range(slot + 1, TILES):
                     value = mixed[d, cb * 8 : cb * 8 + 8, source * LANES : (source + 1) * LANES]
                     total = jnp.where(tile_of == source, lane_gather(value, index), total)
-                if cb < 3:
-                    out[d, slot * 24 + cb * 8 : slot * 24 + cb * 8 + 8, :] = total
-                else:
-                    first = 24 * tiles + 3 * slot
-                    out[d, first : first + 3, :] = total[0:3]
+                values.append(total)
+            for cb in range(3):
+                value = values[cb]
+                if slot >= whole:
+                    value = jnp.where(lane < SHORT, value, tuck(values[3][cb : cb + 1]))
+                out[d, slot * 24 + cb * 8 : slot * 24 + cb * 8 + 8, :] = value
+            if slot < whole:
+                row = 24 * slots_of(kind) + 3 * slot
+                out[d, row : row + 3, :] = values[3][0:3]
 
     lax.fori_loop(0, OWNERS // 8, owner_group, 0)
 
 
-def compact(tiles, moved, low, high, depth, halo_coef, pick):
+def compact(kind, moved, low, high, depth, halo_coef, pick):
     return pl.pallas_call(
-        functools.partial(compact_kernel, tiles),
-        out_shape=jax.ShapeDtypeStruct((OWNERS, block_rows(tiles), LANES), jnp.float32),
+        functools.partial(compact_kernel, kind),
+        out_shape=jax.ShapeDtypeStruct((OWNERS, block_rows(kind), LANES), jnp.float32),
         in_specs=[VMEM] * 6,
         out_specs=VMEM,
         scratch_shapes=[
@@ -324,95 +353,132 @@
     return found
 
 
-def block_row(tiles, slot, k):
-    return slot * 24 + k if k < 24 else 24 * tiles + 3 * slot + k - 24
+def columns(vector):
+    pieces = []
+    for begin in range(0, vector.shape[0], LANES):
+        size = min(LANES, vector.shape[0] - begin)
+        row = jnp.broadcast_to(vector[begin : begin + size][None, :], (8, size))
+        if size < LANES:
+            row = jnp.concatenate([row, jnp.zeros((8, LANES - size), jnp.float32)], axis=1)
+        column = jnp.transpose(row)[:size, 0:1]
+        pieces.append(jnp.broadcast_to(column, (size, LANES)))
+    return pieces
 
 
 def source_kernel(
-    tiles, points, turn_own, refraction, keep, lose, first_far, second_far, out,
-    grid, turned, low, pair, first, second, arriving,
+    kind, points, turn_own, refraction, growth, dissipation, first_far, second_far, out,
+    grid, turned, low, pair,
 ):
-    first_copy = pltpu.make_async_copy(first_far, first, arriving.at[0])
-    first_copy.start()
-    second_copy = pltpu.make_async_copy(second_far, second, arriving.at[1])
-    second_copy.start()
-    ncomp = turned.shape[0]
+    first, second = first_far, second_far
+    whole = kind[0]
+    tiles = slots_of(kind)
+    ncomp = low.shape[0]
     nfreq = ncomp // NTH
     width = NTH + 4
     for slot in range(tiles):
         lanes = slice(slot * LANES, (slot + 1) * LANES)
         for s, k, size, c in runs():
-            row = block_row(tiles, slot, k)
             to = c // NTH * width + 2 + c % NTH
-            grid[to : to + size, lanes] = points[s, row : row + size, :]
+            if k >= 24 and slot >= whole:
+                for i in range(k - 24, k - 24 + size):
+                    row = slot * 24 + i * 8
+                    grid[slot, to : to + 1, :] = untuck(points[s, row : row + 8, :])[0:1]
+                    to += 1
+                continue
+            row = slot * 24 + k if k < 24 else 24 * tiles + 3 * slot + k - 24
+            grid[slot, to : to + size, :] = points[s, row : row + size, :]
         for f in range(nfreq):
             base = f * width
-            grid[base : base + 2, lanes] = grid[base + NTH : base + NTH + 2, lanes]
-            grid[base + NTH + 2 : base + NTH + 4, lanes] = grid[base + 2 : base + 4, lanes]
+            grid[slot, base : base + 2, :] = grid[slot, base + NTH : base + NTH + 2, :]
+            grid[slot, base + NTH + 2 : base + NTH + 4, :] = grid[slot, base + 2 : base + 4, :]
+        turn_row = jnp.broadcast_to(turn_own[0:1, lanes], (8, LANES))
+        up = turn_row >= 0.0
+        sixth = turn_row / 6.0
+        by_turn = [
+            sixth * jnp.where(up, 3.0, -3.0),
+            sixth * jnp.where(up, 2.0, 6.0),
+            sixth * jnp.where(up, -6.0, -2.0),
+            jnp.where(up, sixth, -sixth),
+        ]
         for f in range(nfreq):
             base = f * width
-            rate = refraction[f] * turn_own[0:1, lanes]
-            up = rate >= 0.0
-            sixth = rate / 6.0
-            centre = grid[base : base + width, lanes]
-            total = (sixth * jnp.where(up, 3.0, -3.0)) * centre
-            total += (sixth * jnp.where(up, 2.0, 6.0)) * pltpu.roll(centre, width - 1, axis=0)
-            total += (sixth * jnp.where(up, -6.0, -2.0)) * pltpu.roll(centre, 1, axis=0)
-            total += jnp.where(up, sixth, 0.0) * pltpu.roll(centre, 2, axis=0)
-            total += jnp.where(up, 0.0, -sixth) * pltpu.roll(centre, width - 2, axis=0)
-            result = centre - total
-            turned[f * NTH : (f + 1) * NTH, lanes] = result[2 : NTH + 2]
-
-    chunk = ncomp // 3
-    energy = jnp.zeros((1, tiles * LANES), jnp.float32)
-    for m in range(0, ncomp, chunk):
-        value = turned[m : m + chunk, :]
-        low[m : m + chunk, :] = value.astype(jnp.bfloat16)
-        energy += jnp.sum(value, axis=0, keepdims=True)
-    energy = energy / ncomp
-    first_copy.wait()
+            c0, ca, cb, cf = [c * refraction[f] for c in by_turn]
+            for begin in range(0, NTH, 8):
+                size = min(8, NTH - begin)
+                at = base + 2 + begin
+
+                def near(step):
+                    return grid[slot, at + step : at + step + size, :]
+
+                centre = near(0)
+                total = c0[:size] * centre + ca[:size] * near(1) + cb[:size] * near(-1)
+                total += cf[:size] * jnp.where(up[:size], near(-2), near(2))
+                to = f * NTH + begin
+                turned[slot, to : to + size, :] = centre - total
+
+    energy = []
+    for slot in range(tiles):
+        value = turned[slot]
+        low[:, slot * LANES : (slot + 1) * LANES] = value.astype(jnp.bfloat16)
+        energy.append(jnp.sum(value, axis=0, keepdims=True) / ncomp)
+    keep = [1.0 + 0.2 * column for column in columns(growth)]
+    lose = [0.2 * column for column in columns(dissipation)]
     partner = jnp.dot(first[...], low[...], preferred_element_type=jnp.float32)
-    pair[...] = (turned[...] * partner).astype(jnp.bfloat16)
-    second_copy.wait()
+    for slot in range(tiles):
+        lanes = slice(slot * LANES, (slot + 1) * LANES)
+        pair[:, lanes] = (turned[slot] * partner[:, lanes]).astype(jnp.bfloat16)
     nonlinear = jnp.dot(second[...], pair[...], preferred_element_type=jnp.float32)
     for slot in range(tiles):
         lanes = slice(slot * LANES, (slot + 1) * LANES)
-        scale = keep[...] - lose[...] * energy[:, lanes]
-        turned[:, lanes] = turned[:, lanes] * scale + 0.2 * nonlinear[:, lanes]
+        for begin in range(0, ncomp, LANES):
+            part = slice(begin, min(begin + LANES, ncomp))
+            scale = keep[begin // LANES] - lose[begin // LANES] * energy[slot]
+            turned[slot, part, :] = turned[slot, part, :] * scale + 0.2 * nonlinear[part, lanes]
+    lane = iota((8, LANES), 1)
     for s in range(OWNERS):
         for slot in range(tiles):
-            lanes = slice(slot * LANES, (slot + 1) * LANES)
-            out[s, slot * 24 : slot * 24 + 24, :] = turned[s * HELD : s * HELD + 24, lanes]
-            row = 24 * tiles + 3 * slot
-            out[s, row : row + 3, :] = turned[s * HELD + 24 : s * HELD + HELD, lanes]
-
-
-def sources(tiles, points, turn_own, refraction, keep, lose, first, second):
+            c = s * HELD
+            if slot < whole:
+                out[s, slot * 24 : slot * 24 + 24, :] = turned[slot, c : c + 24, :]
+                row = 24 * tiles + 3 * slot
+                out[s, row : row + 3, :] = turned[slot, c + 24 : c + HELD, :]
+                continue
+            for cb in range(3):
+                value = turned[slot, c + cb * 8 : c + cb * 8 + 8, :]
+                spare = tuck(turned[slot, c + 24 + cb : c + 25 + cb, :])
+                row = slot * 24 + cb * 8
+                out[s, row : row + 8, :] = jnp.where(lane < SHORT, value, spare)
+
+
+def sources(kind, points, turn_own, refraction, growth, dissipation, first, second):
     ncomp = first.shape[0]
+    tiles = slots_of(kind)
     lanes = tiles * LANES
     return pl.pallas_call(
-        functools.partial(source_kernel, tiles),
+        functools.partial(source_kernel, kind),
         out_shape=jax.ShapeDtypeStruct(points.shape, jnp.float32),
-        in_specs=[VMEM, VMEM, SMEM, VMEM, VMEM, ANY, ANY],
+        in_specs=[VMEM, VMEM, SMEM, VMEM, VMEM, VMEM, VMEM],
         out_specs=VMEM,
         scratch_shapes=[
-            pltpu.VMEM((ncomp // NTH * (NTH + 4), lanes), jnp.float32),
-            pltpu.VMEM((ncomp, lanes), jnp.float32),
+            pltpu.VMEM((tiles, ncomp // NTH * (NTH + 4), LANES), jnp.float32),
+            pltpu.VMEM((tiles, ncomp, LANES), jnp.float32),
             pltpu.VMEM((ncomp, lanes), jnp.bfloat16),
             pltpu.VMEM((ncomp, lanes), jnp.bfloat16),
-            pltpu.VMEM((ncomp, ncomp), jnp.bfloat16),
-            pltpu.VMEM((ncomp, ncomp), jnp.bfloat16),
-            pltpu.SemaphoreType.DMA((2,)),
         ],
         compiler_params=PARAMS,
         cost_estimate=pl.CostEstimate(
             flops=4 * ncomp * ncomp * lanes, bytes_accessed=6000000, transcendentals=0
         ),
         name="sources",
-    )(points, turn_own, refraction, keep, lose, first, second)
-
-
-def expand_kernel(tiles, result, rank, mixed):
+    )(points, turn_own, refraction, growth, dissipation, first, second)
+
+
+def expand_kernel(kind, result, rank, mixed):
+    whole, short = kind
+    slots = slots_of(kind)
+    tail_rows = (3 * whole + 7) // 8 * 8
+    row_at = iota((8, LANES), 0)
+
     def owner_group(g, carry):
         ranks = rank[pl.ds(pl.multiple_of(g * 8, 8), 8), :]
         for i in range(8):
@@ -420,22 +486,25 @@
         return carry
 
     def owner_step(d, rank_row):
-        tail = result[d, 24 * tiles : 24 * tiles + 16, :]
+        tail = result[d, 24 * slots : 24 * slots + tail_rows, :]
+        values = []
+        for slot in range(slots):
+            parts = [result[d, slot * 24 + cb * 8 : slot * 24 + cb * 8 + 8, :] for cb in range(3)]
+            if slot < whole:
+                last = pltpu.roll(tail, (tail_rows - 3 * slot) % tail_rows, axis=0)[0:8]
+            else:
+                last = jnp.where(row_at == 1, untuck(parts[1]), untuck(parts[0]))
+                last = jnp.where(row_at == 2, untuck(parts[2]), last)
+            values.append(parts + [last])
         for t in range(TILES):
             index = jnp.broadcast_to(rank_row[:, t * LANES : (t + 1) * LANES], (8, LANES))
             slot_of = index >> 7
             land = index < 0
             index = index & (LANES - 1)
             for cb in range(4):
-                total = jnp.zeros((8, LANES), jnp.float32)
-                for slot in range(min(t + 1, tiles)):
-                    if cb < 3:
-                        row = slot * 24 + cb * 8
-                        value = result[d, row : row + 8, :]
-                    else:
-                        value = pltpu.roll(tail, (16 - 3 * slot) % 16, axis=0)[0:8]
-                    value = lane_gather(value, index)
-                    total = value if slot == 0 else jnp.where(slot_of == slot, value, total)
+                total = lane_gather(values[0][cb], index)
+                for slot in range(1, min(t + 1, slots)):
+                    total = jnp.where(slot_of == slot, lane_gather(values[slot][cb], index), total)
                 mixed[d, cb * 8 : cb * 8 + 8, t * LANES : (t + 1) * LANES] = jnp.where(
                     land, 0.0, total
                 )
@@ -443,9 +512,9 @@
     lax.fori_loop(0, OWNERS // 8, owner_group, 0)
 
 
-def expand(tiles, result, rank):
+def expand(kind, result, rank):
     return pl.pallas_call(
-        functools.partial(expand_kernel, tiles),
+        functools.partial(expand_kernel, kind),
         out_shape=jax.ShapeDtypeStruct((OWNERS, PAD, COLS), jnp.float32),
         in_specs=[VMEM] * 2,
         out_specs=VMEM,
@@ -504,24 +573,21 @@
     high = lax.ppermute(first, "tile", backward)
     moved, halo_coef = propagate(grid, depth, speed)
     pick, rank, turn_own, most = make_index(turn, sea_mask, halo_coef)
-    ncomp = growth.shape[0]
-    keep = jnp.broadcast_to((1.0 + 0.2 * growth)[:, None], (ncomp, LANES))
-    lose = jnp.broadcast_to((0.2 * dissipation)[:, None], (ncomp, LANES))
-
-    keep, lose = lax.optimization_barrier((keep, lose))
-
-    def rest(tiles):
+
+    def rest(kind):
         def run(moved, low, high):
-            sent = compact(tiles, moved, low, high, depth, halo_coef, pick)
+            sent = compact(kind, moved, low, high, depth, halo_coef, pick)
             points = exchange(sent)
             result = sources(
-                tiles, points, turn_own, refraction, keep, lose, quad_first, quad_second
+                kind, points, turn_own, refraction, growth, dissipation, quad_first, quad_second
             )
-            return expand(tiles, exchange(result), rank)
+            return expand(kind, exchange(result), rank)
 
         return run
 
-    return finish(lax.cond(most[0] <= 3 * LANES, rest(3), rest(4), moved, low, high))
+    limits = [whole * LANES + short for whole, short in KINDS[:-1]]
+    chosen = sum((most[0] > limit).astype(jnp.int32) for limit in limits)
+    return finish(lax.switch(chosen, [rest(kind) for kind in KINDS], moved, low, high))
 
 
 def solution(mesh):

time: 82.3 us -> 80.4 us (0.977)
  blocking collectives: 54.3 us -> 51.7 us
  Pallas kernels: 16.2 us -> 18 us
  other arithmetic: 1.38 us -> 0 us
    all_to_all x2, blocking collectives: 54.3 us -> 51.7 us  [exchange(): lax.all_to_all(blocks, 'comp', split_axis=0, concat_axis=0, tiled=True)]
    pallas_call x3, Pallas kernels: 9.06 us -> 10.6 us  [the longest x1 4.05 us: compact(): pl.pallas_call(functools.partial(compact_kernel, kind), out_shape=jax.Sha...]
  transfers between devices with their start and end apart: 2 -> 2, of which waited for: 0 -> 0; matrix products, arithmetic and copies ran while one was open for 2% -> 0% of each run, Pallas kernels for 7% -> 7%
where the time goes in v4:
time: 80.4 us; the launch traced here: 80 us
  blocking collectives  51.7 us (64%)
  Pallas kernels  18 us (22%)
  starting transfers between devices  6.81 us (8%)
  between operations  1.66 us (2%)
  local copies, waits for them, and re-layouts  1.51 us (2%)
    all_to_all x2, blocking collectives, exchange(): lax.all_to_all(blocks, 'comp', split_axis=0, concat_axis=0, tiled=True)  51.7 us
    ppermute x1, starting transfers between devices, shards(): low = lax.ppermute(last, 'tile', forward)  4.89 us
    pallas_call x1, Pallas kernels, compact(): pl.pallas_call(functools.partial(compact_kernel, kind), out_shape=jax.Sha...  4.05 us
    pallas_call x1, Pallas kernels, propagate(): pl.pallas_call(propagate_kernel, out_shape=[jax.ShapeDtypeStruct((ROWS, P...  3.97 us
    pallas_call x1, Pallas kernels, sources(): pl.pallas_call(functools.partial(source_kernel, kind), out_shape=jax.Shap...  3.4 us
    pallas_call x1, Pallas kernels, expand(): pl.pallas_call(functools.partial(expand_kernel, kind), out_shape=jax.Shap...  3.14 us
    ppermute x1, starting transfers between devices, shards(): high = lax.ppermute(first, 'tile', backward)  1.92 us
    pallas_call x1, Pallas kernels, make_index(): pl.pallas_call(index_kernel, out_shape=[plane, plane, jax.ShapeDtypeStruc...  1.76 us
  transfers between devices with their start and end apart: 2, of which 0 were waited for; matrix products, arithmetic and copies ran while one was open for 0% of the time, Pallas kernels for 7%

profile of v4, /device:TPU:97, one launch (start us, length us, event | category | flops | bytes accessed | tf_op | source)
XLA Modules:
  0.0 80.0 jit_solution(7951372892683199502)
XLA Ops:
  0.0 0.0 copy-start
  0.0 1.5 %copy-done = f32[27,32,512]{2,1,0:T(8,128)S(1)} copy-done((f32[27,32,512]{2,1,0:T(8,128)S(1)}, f32[27,32,512]{2,1,0:T(8,128)}, u32[]{:S(2)}) %copy-start) | copy-done | bytes 1769496
  1.5 0.0 copy-start.3
  1.5 0.0 copy-start.1
  1.5 0.0 copy-start.5
  1.5 0.0 copy-start.6
  1.5 0.0 copy-start.7
  1.5 0.0 copy-start.8
  1.5 0.0 copy-start.9
  1.5 0.3 prepare.1
  1.9 4.9 %collective-permute-start = (f32[2,32,512]{2,1,0:T(8,128)S(1)}, f32[2,32,512]{2,1,0:T(8,128)S(1)}, u32[]{:S(2)}, u32[]{:S(2)}) collective-permute-start(f32[2,32,512]{2,1,0:T(8,128)S(1)} %get-tuple-element.139), channel_id=1, source_target_pairs={{0,1},{1,2},{2,3},{3,4},{4,5},{5,6},{6,7},{8,9},{9,10},{10,11},{11... | collective-permute-start | bytes 393224 | tf_op jit(solution)/shard_map/ppermute | solution.py:572
  6.8 1.9 %collective-permute-start.1 = (f32[2,32,512]{2,1,0:T(8,128)S(1)}, f32[2,32,512]{2,1,0:T(8,128)S(1)}, u32[]{:S(2)}, u32[]{:S(2)}) collective-permute-start(f32[2,32,512]{2,1,0:T(8,128)S(1)} %get-tuple-element.140), channel_id=1, source_target_pairs={{1,0},{2,1},{3,2},{4,3},{5,4},{6,5},{7,6},{9,8},{10,9},{11,10},{12... | collective-permute-start | bytes 393224 | tf_op jit(solution)/shard_map/ppermute | solution.py:573
  8.7 0.0 copy-done.3
  8.7 4.0 %propagate.1 = (f32[32,32,512]{2,1,0:T(8,128)S(1)}, f32[4,32,128]{2,1,0:T(8,128)S(1)}) custom-call(f32[32,32,512]{2,1,0:T(8,128)S(1)} %get-tuple-element.135.grid, f32[32,512]{1,0:T(8,128)} %depth.1, f32[27]{0:T(128)S(1)} %copy-done.3), custom_call_target="tpu_custom_call" | custom-call | flops 20000000 | bytes 4000000 | tf_op jit(solution)/shard_map/propagate/pallas_call | solution.py:229
  12.7 0.0 copy-done.1
  12.7 0.0 copy-done.2
  12.7 1.8 %index.1 = (s32[32,512]{1,0:T(8,128)S(1)}, s32[32,512]{1,0:T(8,128)S(1)}, f32[8,512]{1,0:T(8,128)S(1)}, s32[1]{0:T(128)}) custom-call(f32[32,512]{1,0:T(8,128)S(1)} %copy-done.1, s32[32,512]{1,0:T(8,128)S(1)} %copy-done.2, f32[4,32,128]{2,1,0:T(8,128)S(1)} %get-tuple-element.136.after), custom_call_target="tpu_custom_call" | custom-call | flops 2000000 | bytes 200000 | tf_op jit(solution)/shard_map/index/pallas_call | solution.py:131
  15.8 0.0 collective-permute-done
  15.8 0.0 collective-permute-done.1
  15.8 0.0 copy-done.4
  15.8 0.0 copy-done.5
  15.8 0.0 copy-done.6
  15.8 0.0 copy-done.7
  15.9 0.0 copy-done.8
  15.9 0.0 copy-done.9
  15.9 62.6 %conditional.1 = (f32[32,32,512]{2,1,0:T(8,128)S(1)}) conditional(s32[]{:T(128)} %bitcast, (f32[32,32,512]{2,1,0:T(8,128)S(1)}, f32[2,32,512]{2,1,0:T(8,128)S(1)}, f32[2,32,512]{2,1,0:T(8,128)S(1)}, f32[32,512]{1,0:T(8,128)S(1)}, f32[4,32,128]{2,1,0:T(8,128)S(1)}, /*index=5*/s32[32,512]{1,0:T(8,128)S(1)}, f32[8,512]{1,0:T(8,128)S(1)}, ...), branch_computations={%region_0.0_spmd, %region_1.0_spmd, %region_2.0_spmd} | conditional | flops 1538823680 | bytes 21340040 | solution.py:590
  15.9 4.0 %compact.3 = f32[32,80,128]{2,1,0:T(8,128)S(1)} custom-call(f32[32,32,512]{2,1,0:T(8,128)S(1)} %get-tuple-element.86.moved, f32[2,32,512]{2,1,0:T(8,128)S(1)} %get-tuple-element.88.low, f32[2,32,512]{2,1,0:T(8,128)S(1)} %get-tuple-element.89.high, f32[32,512]{1,0:T(8,128)S(1)} %get-tuple-element.90.depth, f32[4,32,128]{2,1,0:T(8,128)S(1)} %get-tuple-element.91.halo_coef, ...), custom_call_target="tpu_custom_call" | custom-call | flops 5000000 | bytes 4000000 | tf_op jit(solution)/shard_map/cond/branch_0_fun/compact/pallas_call | solution.py:329
  19.9 28.0 %all_to_all.24.points = f32[32,80,128]{2,1,0:T(8,128)S(1)} all-to-all(f32[32,80,128]{2,1,0:T(8,128)S(1)} %compact.3), channel_id=1, replica_groups=mesh['comp'=32,'tile'=8] {'comp'}, dimensions={0} | all-to-all | bytes 2621440 | tf_op jit(solution)/shard_map/cond/branch_0_fun/all_to_all | solution.py:562
  48.0 3.4 %sources.3 = f32[32,80,128]{2,1,0:T(8,128)S(1)} custom-call(f32[32,80,128]{2,1,0:T(8,128)S(1)} %all_to_all.24.points, f32[8,512]{1,0:T(8,128)S(1)} %get-tuple-element.93.turn_own, f32[24]{0:T(128)S(1)} %get-tuple-element.94.refraction, f32[864]{0:T(1024)S(1)} %get-tuple-element.95.growth, f32[864]{0:T(1024)S(1)} %get-tuple-element.96.dissipation, ...), custom_call_target="tpu_custom_call" | custom-call | flops 1146617856 | bytes 6000000 | tf_op jit(solution)/shard_map/cond/branch_0_fun/sources/pallas_call | solution.py:457
  51.4 23.7 %all_to_all.25.result = f32[32,80,128]{2,1,0:T(8,128)S(1)} all-to-all(f32[32,80,128]{2,1,0:T(8,128)S(1)} %sources.3), channel_id=1, replica_groups=mesh['comp'=32,'tile'=8] {'comp'}, dimensions={0} | all-to-all | bytes 2621440 | tf_op jit(solution)/shard_map/cond/branch_0_fun/all_to_all | solution.py:562
  75.1 3.1 %expand.3 = f32[32,32,512]{2,1,0:T(8,128)S(1)} custom-call(f32[32,80,128]{2,1,0:T(8,128)S(1)} %all_to_all.25.result, s32[32,512]{1,0:T(8,128)S(1)} %get-tuple-element.99.rank), custom_call_target="tpu_custom_call" | custom-call | flops 5000000 | bytes 4000000 | tf_op jit(solution)/shard_map/cond/branch_0_fun/expand/pallas_call | solution.py:516
  78.4 1.4 %finish.1 = f32[27,32,512]{2,1,0:T(8,128)} custom-call(f32[32,32,512]{2,1,0:T(8,128)S(1)} %get-tuple-element.144.mixed), custom_call_target="tpu_custom_call" | custom-call | flops 5000000 | bytes 4000000 | tf_op jit(solution)/shard_map/finish/pallas_call | solution.py:546
  (2 shorter events, 0.0 us)
Async XLA Ops:
  0.0 1.5 %copy-start = (f32[27,32,512]{2,1,0:T(8,128)S(1)}, f32[27,32,512]{2,1,0:T(8,128)}, u32[]{:S(2)}) copy-start(f32[27,32,512]{2,1,0:T(8,128)} %spec.1) | copy-start | bytes 5308420
  1.5 7.2 %copy-start.3 = (f32[27]{0:T(128)S(1)}, f32[27]{0:T(128)}, u32[]{:S(2)}) copy-start(f32[27]{0:T(128)} %speed.1) | copy-start | bytes 328
  1.5 11.2 %copy-start.1 = (f32[32,512]{1,0:T(8,128)S(1)}, f32[32,512]{1,0:T(8,128)}, u32[]{:S(2)}) copy-start(f32[32,512]{1,0:T(8,128)} %turn.1) | copy-start | bytes 196612
  1.5 11.2 %copy-start.2 = (s32[32,512]{1,0:T(8,128)S(1)}, s32[32,512]{1,0:T(8,128)}, u32[]{:S(2)}) copy-start(s32[32,512]{1,0:T(8,128)} %mask.1) | copy-start | bytes 196612
  1.5 14.3 %copy-start.4 = (bf16[864,864]{1,0:T(8,128)(2,1)S(1)}, bf16[864,864]{1,0:T(8,128)(2,1)}, u32[]{:S(2)}) copy-start(bf16[864,864]{1,0:T(8,128)(2,1)} %param.21) | copy-start | bytes 4478980
  1.5 14.3 %copy-start.5 = (bf16[864,864]{1,0:T(8,128)(2,1)S(1)}, bf16[864,864]{1,0:T(8,128)(2,1)}, u32[]{:S(2)}) copy-start(bf16[864,864]{1,0:T(8,128)(2,1)} %param.22) | copy-start | bytes 4478980
  1.5 14.3 %copy-start.6 = (f32[32,512]{1,0:T(8,128)S(1)}, f32[32,512]{1,0:T(8,128)}, u32[]{:S(2)}) copy-start(f32[32,512]{1,0:T(8,128)} %depth.1) | copy-start | bytes 196612
  1.5 14.3 %copy-start.7 = (f32[864]{0:T(1024)S(1)}, f32[864]{0:T(1024)}, u32[]{:S(2)}) copy-start(f32[864]{0:T(1024)} %param.19) | copy-start | bytes 10372
  1.5 14.3 %copy-start.8 = (f32[864]{0:T(1024)S(1)}, f32[864]{0:T(1024)}, u32[]{:S(2)}) copy-start(f32[864]{0:T(1024)} %param.20) | copy-start | bytes 10372
  1.5 14.3 %copy-start.9 = (f32[24]{0:T(128)S(1)}, f32[24]{0:T(128)}, u32[]{:S(2)}) copy-start(f32[24]{0:T(128)} %param.18) | copy-start | bytes 292
  1.9 13.9 %collective-permute-start = (f32[2,32,512]{2,1,0:T(8,128)S(1)}, f32[2,32,512]{2,1,0:T(8,128)S(1)}, u32[]{:S(2)}, u32[]{:S(2)}) collective-permute-start(f32[2,32,512]{2,1,0:T(8,128)S(1)} %get-tuple-element.139), channel_id=1, source_target_pairs={{0,1},{1,2},{2,3},{3,4},{4,5},{5,6},{6,7},{8,9},{9,10},{10,11},{11... | collective-permute-start | bytes 393224 | tf_op jit(solution)/shard_map/ppermute | solution.py:572
  6.8 9.0 %collective-permute-start.1 = (f32[2,32,512]{2,1,0:T(8,128)S(1)}, f32[2,32,512]{2,1,0:T(8,128)S(1)}, u32[]{:S(2)}, u32[]{:S(2)}) collective-permute-start(f32[2,32,512]{2,1,0:T(8,128)S(1)} %get-tuple-element.140), channel_id=1, source_target_pairs={{1,0},{2,1},{3,2},{4,3},{5,4},{6,5},{7,6},{9,8},{10,9},{11,10},{12... | collective-permute-start | bytes 393224 | tf_op jit(solution)/shard_map/ppermute | solution.py:573

commit v5 on v4

--- a/solution.py
+++ b/solution.py
@@ -90,16 +90,22 @@
     )(spectrum)
 
 
-def index_kernel(turn, mask, after, pick, rank, turn_own, most):
-    me = lax.axis_index("comp")
+def index_steps(me, turn, mask, pick, rank, turn_own, chosen):
     sea = mixed_plane(mask[...])
+    yield
     column = iota((ROWS, COLS), 1)
     count = sea
     step = 1
     while step < COLS:
         count = count + jnp.where(column >= step, pltpu.roll(count, step, axis=1), 0)
         step *= 2
-    most[0] = jnp.max(count)
+        if step <= LANES:
+            yield
+    largest = jnp.max(count)
+    kind = jnp.int32(0)
+    for whole, short in KINDS[:-1]:
+        kind += (largest > whole * LANES + short).astype(jnp.int32)
+    chosen[0] = kind
     place = count - 1
     rank[...] = jnp.where(sea > 0, place, -1)
     entry = jnp.where(sea > 0, column * COLS + (column - place), -1)
@@ -110,9 +116,10 @@
         stays = (entry >= 0) & ((entry & step) == 0)
         entry = jnp.where(arrives, other, jnp.where(stays, entry, -1))
         step *= 2
+        if step <= LANES:
+            yield
     entry = jnp.where(entry >= 0, entry >> 9, 0)
     pick[...] = entry
-
     mine = iota((ROWS, COLS), 0) == me
     own_turn = jnp.sum(jnp.where(mine, mixed_plane(turn[...]), 0.0), axis=0, keepdims=True)
     own_pick = jnp.sum(jnp.where(mine, entry, 0), axis=0, keepdims=True)
@@ -124,24 +131,7 @@
             value = lane_gather(own, index & (LANES - 1))
             total = jnp.where(index >> 7 == source, value, total)
         turn_own[:, t * LANES : (t + 1) * LANES] = total
-
-
-def make_index(turn, mask, after):
-    plane = jax.ShapeDtypeStruct((ROWS, COLS), jnp.int32)
-    return pl.pallas_call(
-        index_kernel,
-        out_shape=[
-            plane,
-            plane,
-            jax.ShapeDtypeStruct((8, COLS), jnp.float32),
-            jax.ShapeDtypeStruct((1,), jnp.int32),
-        ],
-        in_specs=[VMEM, VMEM, ANY],
-        out_specs=[VMEM] * 3 + [SMEM],
-        compiler_params=PARAMS,
-        cost_estimate=pl.CostEstimate(flops=2000000, bytes_accessed=200000, transcendentals=0),
-        name="index",
-    )(turn, mask, after)
+    yield
 
 
 def shifted(tiles, lane):
@@ -160,8 +150,11 @@
     ]
 
 
-def propagate_kernel(grid, depth, speed, moved, halo_coef):
+def propagate_kernel(
+    grid, depth, turn, mask, speed, mixed, halo_coef, pick, rank, turn_own, chosen
+):
     me = lax.axis_index("comp")
+    beside = index_steps(me, turn, mask, pick, rank, turn_own, chosen)
     sub = iota((PAD, LANES), 0)
     speeds = jnp.zeros((PAD, LANES), jnp.float32)
     for k in range(HELD):
@@ -196,6 +189,7 @@
         ]
 
         def row_step(r, rows, depth_row):
+            results = []
             centre = [grid[r, part, t * LANES : (t + 1) * LANES] for t in range(TILES)]
 
             def near(i, t):
@@ -209,35 +203,38 @@
                 total += ya * near(1, t) + yb * near(-1, t)
                 total += yf * jnp.where(yu, near(-2, t), near(2, t))
                 lanes = slice(t * LANES, (t + 1) * LANES)
-                moved[r, part, lanes] = centre[t] - depth_row[:, lanes] * total
-
-        def group(rb, first):
-            depths = depth[pl.ds(pl.multiple_of(rb * 8, 8), 8), :]
-            for i in range(8):
-                row_step(rb * 8 + i, first + i, depths[i : i + 1, :])
-
-        group(0, 0)
-
-        @pl.loop(1, 3)
-        def _(rb):
-            group(rb, 8)
-
-        group(3, 24)
-
-
-def propagate(grid, depth, speed):
+                results.append(centre[t] - depth_row[:, lanes] * total)
+            return results
+
+        for rb in range(ROWS // 8):
+            depths = depth[rb * 8 : rb * 8 + 8, :]
+            group = [row_step(rb * 8 + i, rb * 8 + i, depths[i : i + 1, :]) for i in range(8)]
+            for t in range(TILES):
+                for j, value in enumerate(butterfly([row[t] for row in group], lane)):
+                    mixed[(rb ^ t) * 8 + j, part, t * LANES : (t + 1) * LANES] = value
+            next(beside, None)
+    for _ in beside:
+        pass
+
+
+def propagate(grid, depth, turn, mask, speed):
+    plane = jax.ShapeDtypeStruct((ROWS, COLS), jnp.int32)
     return pl.pallas_call(
         propagate_kernel,
         out_shape=[
             jax.ShapeDtypeStruct((ROWS, PAD, COLS), jnp.float32),
             jax.ShapeDtypeStruct((4, PAD, LANES), jnp.float32),
+            plane,
+            plane,
+            jax.ShapeDtypeStruct((8, COLS), jnp.float32),
+            jax.ShapeDtypeStruct((1,), jnp.int32),
         ],
-        in_specs=[VMEM, VMEM, SMEM],
-        out_specs=[VMEM, VMEM],
+        in_specs=[VMEM, VMEM, VMEM, VMEM, SMEM],
+        out_specs=[VMEM] * 5 + [SMEM],
         compiler_params=PARAMS,
         cost_estimate=pl.CostEstimate(flops=20000000, bytes_accessed=4000000, transcendentals=0),
         name="propagate",
-    )(grid, depth, speed)
+    )(grid, depth, turn, mask, speed)
 
 
 SHORT = 112
@@ -266,79 +263,84 @@
     return value
 
 
-def compact_kernel(kind, moved, low, high, depth, halo_coef, pick, out, mixed, edge):
+def compact_kernel(kind, mixed, low, high, depth, halo_coef, pick, out, terms, fixed, spare, tails):
     lane = iota((8, LANES), 1)
+    strip = lane >> 4
     back, back_two, ahead, ahead_two = [wide(halo_coef[i]) for i in range(4)]
-    terms = {
-        0: back * low[1] + back_two * low[0],
-        1: back_two * low[1],
-        ROWS - 2: ahead_two * high[0],
-        ROWS - 1: ahead * high[0] + ahead_two * high[1],
-    }
-    edge_of = {}
-    for r, term in terms.items():
-        edge_of[r] = len(edge_of)
-        edge[edge_of[r]] = moved[r] - depth[r : r + 1, :] * term
-
-    def load(r, cb, t):
-        rows, lanes = slice(cb * 8, cb * 8 + 8), slice(t * LANES, (t + 1) * LANES)
-        return edge[edge_of[r], rows, lanes] if r in edge_of else moved[r, rows, lanes]
-
-    for cb in range(4):
-        for g in range(4):
-            for t in range(TILES):
-                rows = [load((g ^ t) * 8 + j, cb, t) for j in range(8)]
-                for j, value in enumerate(butterfly(rows, lane)):
-                    mixed[g * 8 + j, cb * 8 : cb * 8 + 8, t * LANES : (t + 1) * LANES] = value
-
-    def owner_group(g, carry):
-        picks = pick[pl.ds(pl.multiple_of(g * 8, 8), 8), :]
-        for i in range(8):
-            owner_step(g * 8 + i, picks[i : i + 1, :])
-        return carry
+    terms[0] = depth[0:1, :] * (back * low[1] + back_two * low[0])
+    terms[1] = depth[1:2, :] * (back_two * low[1])
+    terms[2] = depth[ROWS - 2 : ROWS - 1, :] * (ahead_two * high[0])
+    terms[3] = depth[ROWS - 1 : ROWS, :] * (ahead * high[0] + ahead_two * high[1])
+
+    for g in range(4):
+        for first, row, t in ((0, 0, g), (2, 6, 3 - g)):
+            lanes = slice(t * LANES, (t + 1) * LANES)
+            for cb in range(4):
+                part = slice(cb * 8, cb * 8 + 8)
+                one, two = terms[first, part, lanes], terms[first + 1, part, lanes]
+                for j in range(8):
+                    term = jnp.where(strip == (row + 1) ^ j, two, 0.0)
+                    term = jnp.where(strip == row ^ j, one, term)
+                    fixed[g * 8 + j, first // 2, part, :] = mixed[g * 8 + j, part, lanes] - term
 
     whole, short = kind
 
-    def owner_step(d, pick_row):
+    def load(d, cb, t):
+        part = slice(cb * 8, cb * 8 + 8)
+        if t == d // 8:
+            return fixed[d, 0, part, :]
+        if t == 3 - d // 8:
+            return fixed[d, 1, part, :]
+        return mixed[d, part, t * LANES : (t + 1) * LANES]
+
+    def index_of(d, slot):
+        index = jnp.broadcast_to(pick[d : d + 1, slot * LANES : (slot + 1) * LANES], (8, LANES))
+        return index & (LANES - 1), [index >> 7 == t for t in range(TILES)]
+
+    def picked(d, cb, slot, index, among):
+        total = lane_gather(load(d, cb, slot), index)
+        for source in range(slot + 1, TILES):
+            value = lane_gather(load(d, cb, source), index)
+            total = jnp.where(among[source], value, total)
+        return total
+
+    if short:
+        for d in range(OWNERS):
+            tails[d] = picked(d, 3, whole, *index_of(d, whole))
+        for d in range(OWNERS):
+            for cb in range(3):
+                spare[d, cb] = tuck(tails[d, cb : cb + 1, :])
+
+    for d in range(OWNERS):
         for slot in range(slots_of(kind)):
-            index = jnp.broadcast_to(pick_row[:, slot * LANES : (slot + 1) * LANES], (8, LANES))
-            tile_of = index >> 7
-            index = index & (LANES - 1)
-            values = []
-            for cb in range(4):
-                total = lane_gather(
-                    mixed[d, cb * 8 : cb * 8 + 8, slot * LANES : (slot + 1) * LANES], index
-                )
-                for source in range(slot + 1, TILES):
-                    value = mixed[d, cb * 8 : cb * 8 + 8, source * LANES : (source + 1) * LANES]
-                    total = jnp.where(tile_of == source, lane_gather(value, index), total)
-                values.append(total)
-            for cb in range(3):
-                value = values[cb]
+            index = index_of(d, slot)
+            for cb in range(4 if slot < whole else 3):
+                value = picked(d, cb, slot, *index)
                 if slot >= whole:
-                    value = jnp.where(lane < SHORT, value, tuck(values[3][cb : cb + 1]))
-                out[d, slot * 24 + cb * 8 : slot * 24 + cb * 8 + 8, :] = value
-            if slot < whole:
-                row = 24 * slots_of(kind) + 3 * slot
-                out[d, row : row + 3, :] = values[3][0:3]
-
-    lax.fori_loop(0, OWNERS // 8, owner_group, 0)
-
-
-def compact(kind, moved, low, high, depth, halo_coef, pick):
+                    value = jnp.where(lane < SHORT, value, spare[d, cb])
+                if cb < 3:
+                    out[d, slot * 24 + cb * 8 : slot * 24 + cb * 8 + 8, :] = value
+                else:
+                    row = 24 * slots_of(kind) + 3 * slot
+                    out[d, row : row + 3, :] = value[0:3]
+
+
+def compact(kind, mixed, low, high, depth, halo_coef, pick):
     return pl.pallas_call(
         functools.partial(compact_kernel, kind),
         out_shape=jax.ShapeDtypeStruct((OWNERS, block_rows(kind), LANES), jnp.float32),
         in_specs=[VMEM] * 6,
         out_specs=VMEM,
         scratch_shapes=[
-            pltpu.VMEM((OWNERS, PAD, COLS), jnp.float32),
             pltpu.VMEM((4, PAD, COLS), jnp.float32),
+            pltpu.VMEM((OWNERS, 2, PAD, LANES), jnp.float32),
+            pltpu.VMEM((OWNERS, 3, 8, LANES), jnp.float32),
+            pltpu.VMEM((OWNERS, 8, LANES), jnp.float32),
         ],
         compiler_params=PARAMS,
         cost_estimate=pl.CostEstimate(flops=5000000, bytes_accessed=4000000, transcendentals=0),
         name="compact",
-    )(moved, low, high, depth, halo_coef, pick)
+    )(mixed, low, high, depth, halo_coef, pick)
 
 
 def runs():
@@ -473,17 +475,17 @@
     )(points, turn_own, refraction, growth, dissipation, first, second)
 
 
-def expand_kernel(kind, result, rank, mixed):
+def expand_kernel(kind, result, rank, mixed, last):
     whole, short = kind
     slots = slots_of(kind)
     tail_rows = (3 * whole + 7) // 8 * 8
     row_at = iota((8, LANES), 0)
 
-    def owner_group(g, carry):
-        ranks = rank[pl.ds(pl.multiple_of(g * 8, 8), 8), :]
-        for i in range(8):
-            owner_step(g * 8 + i, ranks[i : i + 1, :])
-        return carry
+    def short_step(d):
+        row = whole * 24
+        parts = [untuck(result[d, row + cb * 8 : row + cb * 8 + 8, :]) for cb in range(3)]
+        value = jnp.where(row_at == 1, parts[1], parts[0])
+        last[d] = jnp.where(row_at == 2, parts[2], value)
 
     def owner_step(d, rank_row):
         tail = result[d, 24 * slots : 24 * slots + tail_rows, :]
@@ -491,11 +493,10 @@
         for slot in range(slots):
             parts = [result[d, slot * 24 + cb * 8 : slot * 24 + cb * 8 + 8, :] for cb in range(3)]
             if slot < whole:
-                last = pltpu.roll(tail, (tail_rows - 3 * slot) % tail_rows, axis=0)[0:8]
+                parts.append(pltpu.roll(tail, (tail_rows - 3 * slot) % tail_rows, axis=0)[0:8])
             else:
-                last = jnp.where(row_at == 1, untuck(parts[1]), untuck(parts[0]))
-                last = jnp.where(row_at == 2, untuck(parts[2]), last)
-            values.append(parts + [last])
+                parts.append(last[d])
+            values.append(parts)
         for t in range(TILES):
             index = jnp.broadcast_to(rank_row[:, t * LANES : (t + 1) * LANES], (8, LANES))
             slot_of = index >> 7
@@ -509,7 +510,11 @@
                     land, 0.0, total
                 )
 
-    lax.fori_loop(0, OWNERS // 8, owner_group, 0)
+    if short:
+        for d in range(OWNERS):
+            short_step(d)
+    for d in range(OWNERS):
+        owner_step(d, rank[d : d + 1, :])
 
 
 def expand(kind, result, rank):
@@ -518,6 +523,7 @@
         out_shape=jax.ShapeDtypeStruct((OWNERS, PAD, COLS), jnp.float32),
         in_specs=[VMEM] * 2,
         out_specs=VMEM,
+        scratch_shapes=[pltpu.VMEM((OWNERS, 8, LANES), jnp.float32)],
         compiler_params=PARAMS,
         cost_estimate=pl.CostEstimate(flops=5000000, bytes_accessed=4000000, transcendentals=0),
         name="expand",
@@ -571,12 +577,13 @@
     grid, first, last = prepare(spectrum)
     low = lax.ppermute(last, "tile", forward)
     high = lax.ppermute(first, "tile", backward)
-    moved, halo_coef = propagate(grid, depth, speed)
-    pick, rank, turn_own, most = make_index(turn, sea_mask, halo_coef)
+    mixed, halo_coef, pick, rank, turn_own, chosen = propagate(
+        grid, depth, turn, sea_mask, speed
+    )
 
     def rest(kind):
-        def run(moved, low, high):
-            sent = compact(kind, moved, low, high, depth, halo_coef, pick)
+        def run(mixed, low, high):
+            sent = compact(kind, mixed, low, high, depth, halo_coef, pick)
             points = exchange(sent)
             result = sources(
                 kind, points, turn_own, refraction, growth, dissipation, quad_first, quad_second
@@ -585,9 +592,7 @@
 
         return run
 
-    limits = [whole * LANES + short for whole, short in KINDS[:-1]]
-    chosen = sum((most[0] > limit).astype(jnp.int32) for limit in limits)
-    return finish(lax.switch(chosen, [rest(kind) for kind in KINDS], moved, low, high))
+    return finish(lax.switch(chosen[0], [rest(kind) for kind in KINDS], mixed, low, high))
 
 
 def solution(mesh):

time: 80.4 us -> 75.7 us (0.942)
  Pallas kernels: 18 us -> 12.5 us
  blocking collectives: 51.7 us -> 52.9 us
    pallas_call x1, Pallas kernels: 4.05 us -> 1.82 us  [compact(): pl.pallas_call(functools.partial(compact_kernel, kind), out_shape=jax.Sha...]
    pallas_call x1 -> x0, Pallas kernels: 1.76 us -> none  [make_index(): pl.pallas_call(index_kernel, out_shape=[plane, plane, jax.ShapeDtypeStruc...]
    pallas_call x1, Pallas kernels: 3.14 us -> 1.79 us  [expand(): pl.pallas_call(functools.partial(expand_kernel, kind), out_shape=jax.Shap...]
    all_to_all x2, blocking collectives: 51.7 us -> 52.9 us  [exchange(): lax.all_to_all(blocks, 'comp', split_axis=0, concat_axis=0, tiled=True)]
  transfers between devices with their start and end apart: 2 -> 2, of which waited for: 0 -> 1; matrix products, arithmetic and copies ran while one was open for 0% -> 0% of each run, Pallas kernels for 7% -> 5%
where the time goes in v5:
time: 75.7 us; the launch traced here: 75.5 us
  blocking collectives  52.9 us (70%)
  Pallas kernels  12.5 us (17%)
  starting transfers between devices  6.81 us (9%)
  local copies, waits for them, and re-layouts  1.51 us (2%)
  between operations  0.97 us (1%)
    all_to_all x2, blocking collectives, exchange(): lax.all_to_all(blocks, 'comp', split_axis=0, concat_axis=0, tiled=True)  52.9 us
    ppermute x1, starting transfers between devices, shards(): low = lax.ppermute(last, 'tile', forward)  4.89 us
    pallas_call x1, Pallas kernels, propagate(): pl.pallas_call(propagate_kernel, out_shape=[jax.ShapeDtypeStruct((ROWS, P...  3.77 us
    pallas_call x1, Pallas kernels, sources(): pl.pallas_call(functools.partial(source_kernel, kind), out_shape=jax.Shap...  3.4 us
    ppermute x1, starting transfers between devices, shards(): high = lax.ppermute(first, 'tile', backward)  1.92 us
    pallas_call x1, Pallas kernels, compact(): pl.pallas_call(functools.partial(compact_kernel, kind), out_shape=jax.Sha...  1.82 us
    pallas_call x1, Pallas kernels, expand(): pl.pallas_call(functools.partial(expand_kernel, kind), out_shape=jax.Shap...  1.79 us
  transfers between devices with their start and end apart: 2, of which 1 were waited for; matrix products, arithmetic and copies ran while one was open for 0% of the time, Pallas kernels for 5%

profile of v5, /device:TPU:97, one launch (start us, length us, event | category | flops | bytes accessed | tf_op | source)
XLA Modules:
  0.0 75.5 jit_solution(7060238940824394342)
XLA Ops:
  0.0 0.0 copy-start
  0.0 1.5 %copy-done = f32[27,32,512]{2,1,0:T(8,128)S(1)} copy-done((f32[27,32,512]{2,1,0:T(8,128)S(1)}, f32[27,32,512]{2,1,0:T(8,128)}, u32[]{:S(2)}) %copy-start) | copy-done | bytes 1769496
  1.5 0.0 copy-start.1
  1.5 0.0 copy-start.2
  1.5 0.0 copy-start.3
  1.5 0.0 copy-start.5
  1.5 0.0 copy-start.6
  1.5 0.0 copy-start.7
  1.5 0.0 copy-start.8
  1.5 0.0 copy-start.9
  1.5 0.3 prepare.1
  1.9 4.9 %collective-permute-start = (f32[2,32,512]{2,1,0:T(8,128)S(1)}, f32[2,32,512]{2,1,0:T(8,128)S(1)}, u32[]{:S(2)}, u32[]{:S(2)}) collective-permute-start(f32[2,32,512]{2,1,0:T(8,128)S(1)} %get-tuple-element.138), channel_id=1, source_target_pairs={{0,1},{1,2},{2,3},{3,4},{4,5},{5,6},{6,7},{8,9},{9,10},{10,11},{11... | collective-permute-start | bytes 393224 | tf_op jit(solution)/shard_map/ppermute | solution.py:578
  6.8 1.9 %collective-permute-start.1 = (f32[2,32,512]{2,1,0:T(8,128)S(1)}, f32[2,32,512]{2,1,0:T(8,128)S(1)}, u32[]{:S(2)}, u32[]{:S(2)}) collective-permute-start(f32[2,32,512]{2,1,0:T(8,128)S(1)} %get-tuple-element.139), channel_id=1, source_target_pairs={{1,0},{2,1},{3,2},{4,3},{5,4},{6,5},{7,6},{9,8},{10,9},{11,10},{12... | collective-permute-start | bytes 393224 | tf_op jit(solution)/shard_map/ppermute | solution.py:579
  8.7 0.0 copy-done.1
  8.7 0.0 copy-done.2
  8.7 0.0 copy-done.3
  8.7 3.8 %propagate.1 = (f32[32,32,512]{2,1,0:T(8,128)S(1)}, f32[4,32,128]{2,1,0:T(8,128)S(1)}, s32[32,512]{1,0:T(8,128)S(1)}, s32[32,512]{1,0:T(8,128)S(1)}, f32[8,512]{1,0:T(8,128)S(1)}, /*index=5*/s32[1]{0:T(128)}) custom-call(f32[32,32,512]{2,1,0:T(8,128)S(1)} %get-tuple-element.135.grid, f32[32,512]{1,0:T(8,128)} %depth.1, f32[32,512]{1,0:T(8,128)S(1)} %copy-done.1, ...), custom_call_target="tpu_custom_call" | custom-call | flops 20000000 | bytes 4000000 | tf_op jit(solution)/shard_map/propagate/pallas_call | solution.py:222
  13.2 0.0 collective-permute-done
  13.2 0.5 collective-permute-done.1
  13.7 0.0 copy-done.4
  13.7 0.0 copy-done.5
  13.7 0.0 copy-done.6
  13.7 0.0 copy-done.7
  13.7 0.0 copy-done.8
  13.7 0.0 copy-done.9
  13.8 60.1 %conditional.1 = (f32[32,32,512]{2,1,0:T(8,128)S(1)}) conditional(s32[]{:T(128)} %bitcast, (f32[32,32,512]{2,1,0:T(8,128)S(1)}, f32[2,32,512]{2,1,0:T(8,128)S(1)}, f32[2,32,512]{2,1,0:T(8,128)S(1)}, f32[32,512]{1,0:T(8,128)S(1)}, f32[4,32,128]{2,1,0:T(8,128)S(1)}, /*index=5*/s32[32,512]{1,0:T(8,128)S(1)}, f32[8,512]{1,0:T(8,128)S(1)}, ...), branch_computations={%region_0.0_spmd, %region_1.0_spmd, %region_2.0_spmd} | conditional | flops 1538823680 | bytes 21340040 | solution.py:595
  13.8 1.8 %compact.3 = f32[32,80,128]{2,1,0:T(8,128)S(1)} custom-call(f32[32,32,512]{2,1,0:T(8,128)S(1)} %get-tuple-element.86.mixed, f32[2,32,512]{2,1,0:T(8,128)S(1)} %get-tuple-element.88.low, f32[2,32,512]{2,1,0:T(8,128)S(1)} %get-tuple-element.89.high, f32[32,512]{1,0:T(8,128)S(1)} %get-tuple-element.90.depth, f32[4,32,128]{2,1,0:T(8,128)S(1)} %get-tuple-element.91.halo_coef, ...), custom_call_target="tpu_custom_call" | custom-call | flops 5000000 | bytes 4000000 | tf_op jit(solution)/shard_map/cond/branch_0_fun/compact/pallas_call | solution.py:329
  15.6 29.2 %all_to_all.24.points = f32[32,80,128]{2,1,0:T(8,128)S(1)} all-to-all(f32[32,80,128]{2,1,0:T(8,128)S(1)} %compact.3), channel_id=1, replica_groups=mesh['comp'=32,'tile'=8] {'comp'}, dimensions={0} | all-to-all | bytes 2621440 | tf_op jit(solution)/shard_map/cond/branch_0_fun/all_to_all | solution.py:568
  44.8 3.4 %sources.3 = f32[32,80,128]{2,1,0:T(8,128)S(1)} custom-call(f32[32,80,128]{2,1,0:T(8,128)S(1)} %all_to_all.24.points, f32[8,512]{1,0:T(8,128)S(1)} %get-tuple-element.93.turn_own, f32[24]{0:T(128)S(1)} %get-tuple-element.94.refraction, f32[864]{0:T(1024)S(1)} %get-tuple-element.95.growth, f32[864]{0:T(1024)S(1)} %get-tuple-element.96.dissipation, ...), custom_call_target="tpu_custom_call" | custom-call | flops 1146617856 | bytes 6000000 | tf_op jit(solution)/shard_map/cond/branch_0_fun/sources/pallas_call | solution.py:459
  48.2 23.7 %all_to_all.25.result = f32[32,80,128]{2,1,0:T(8,128)S(1)} all-to-all(f32[32,80,128]{2,1,0:T(8,128)S(1)} %sources.3), channel_id=1, replica_groups=mesh['comp'=32,'tile'=8] {'comp'}, dimensions={0} | all-to-all | bytes 2621440 | tf_op jit(solution)/shard_map/cond/branch_0_fun/all_to_all | solution.py:568
  71.9 1.8 %expand.3 = f32[32,32,512]{2,1,0:T(8,128)S(1)} custom-call(f32[32,80,128]{2,1,0:T(8,128)S(1)} %all_to_all.25.result, s32[32,512]{1,0:T(8,128)S(1)} %get-tuple-element.99.rank), custom_call_target="tpu_custom_call" | custom-call | flops 5000000 | bytes 4000000 | tf_op jit(solution)/shard_map/cond/branch_0_fun/expand/pallas_call | solution.py:521
  73.9 1.4 %finish.1 = f32[27,32,512]{2,1,0:T(8,128)} custom-call(f32[32,32,512]{2,1,0:T(8,128)S(1)} %get-tuple-element.144.mixed), custom_call_target="tpu_custom_call" | custom-call | flops 5000000 | bytes 4000000 | tf_op jit(solution)/shard_map/finish/pallas_call | solution.py:552
  (1 shorter events, 0.0 us)
Async XLA Ops:
  0.0 1.5 %copy-start = (f32[27,32,512]{2,1,0:T(8,128)S(1)}, f32[27,32,512]{2,1,0:T(8,128)}, u32[]{:S(2)}) copy-start(f32[27,32,512]{2,1,0:T(8,128)} %spec.1) | copy-start | bytes 5308420
  1.5 7.2 %copy-start.1 = (f32[32,512]{1,0:T(8,128)S(1)}, f32[32,512]{1,0:T(8,128)}, u32[]{:S(2)}) copy-start(f32[32,512]{1,0:T(8,128)} %turn.1) | copy-start | bytes 196612
  1.5 7.2 %copy-start.2 = (s32[32,512]{1,0:T(8,128)S(1)}, s32[32,512]{1,0:T(8,128)}, u32[]{:S(2)}) copy-start(s32[32,512]{1,0:T(8,128)} %mask.1) | copy-start | bytes 196612
  1.5 7.3 %copy-start.3 = (f32[27]{0:T(128)S(1)}, f32[27]{0:T(128)}, u32[]{:S(2)}) copy-start(f32[27]{0:T(128)} %speed.1) | copy-start | bytes 328
  1.5 12.2 %copy-start.4 = (bf16[864,864]{1,0:T(8,128)(2,1)S(1)}, bf16[864,864]{1,0:T(8,128)(2,1)}, u32[]{:S(2)}) copy-start(bf16[864,864]{1,0:T(8,128)(2,1)} %param.21) | copy-start | bytes 4478980
  1.5 12.2 %copy-start.5 = (bf16[864,864]{1,0:T(8,128)(2,1)S(1)}, bf16[864,864]{1,0:T(8,128)(2,1)}, u32[]{:S(2)}) copy-start(bf16[864,864]{1,0:T(8,128)(2,1)} %param.22) | copy-start | bytes 4478980
  1.5 12.2 %copy-start.6 = (f32[32,512]{1,0:T(8,128)S(1)}, f32[32,512]{1,0:T(8,128)}, u32[]{:S(2)}) copy-start(f32[32,512]{1,0:T(8,128)} %depth.1) | copy-start | bytes 196612
  1.5 12.2 %copy-start.7 = (f32[864]{0:T(1024)S(1)}, f32[864]{0:T(1024)}, u32[]{:S(2)}) copy-start(f32[864]{0:T(1024)} %param.19) | copy-start | bytes 10372
  1.5 12.2 %copy-start.8 = (f32[864]{0:T(1024)S(1)}, f32[864]{0:T(1024)}, u32[]{:S(2)}) copy-start(f32[864]{0:T(1024)} %param.20) | copy-start | bytes 10372
  1.5 12.2 %copy-start.9 = (f32[24]{0:T(128)S(1)}, f32[24]{0:T(128)}, u32[]{:S(2)}) copy-start(f32[24]{0:T(128)} %param.18) | copy-start | bytes 292
  1.9 11.3 %collective-permute-start = (f32[2,32,512]{2,1,0:T(8,128)S(1)}, f32[2,32,512]{2,1,0:T(8,128)S(1)}, u32[]{:S(2)}, u32[]{:S(2)}) collective-permute-start(f32[2,32,512]{2,1,0:T(8,128)S(1)} %get-tuple-element.138), channel_id=1, source_target_pairs={{0,1},{1,2},{2,3},{3,4},{4,5},{5,6},{6,7},{8,9},{9,10},{10,11},{11... | collective-permute-start | bytes 393224 | tf_op jit(solution)/shard_map/ppermute | solution.py:578
  6.8 6.9 %collective-permute-start.1 = (f32[2,32,512]{2,1,0:T(8,128)S(1)}, f32[2,32,512]{2,1,0:T(8,128)S(1)}, u32[]{:S(2)}, u32[]{:S(2)}) collective-permute-start(f32[2,32,512]{2,1,0:T(8,128)S(1)} %get-tuple-element.139), channel_id=1, source_target_pairs={{1,0},{2,1},{3,2},{4,3},{5,4},{6,5},{7,6},{9,8},{10,9},{11,10},{12... | collective-permute-start | bytes 393224 | tf_op jit(solution)/shard_map/ppermute | solution.py:579

commit v6 on v5

--- a/solution.py
+++ b/solution.py
@@ -59,7 +59,7 @@
     return jnp.concatenate(pieces, axis=1)
 
 
-def prepare_kernel(spec, grid, low, high):
+def prepare_kernel(spec, grid, to_pair, to_other):
     for cb in range(4):
         part = slice(cb * 8, cb * 8 + 8)
         size = min(8, HELD - cb * 8)
@@ -69,12 +69,10 @@
                 block = jnp.concatenate(
                     [block, jnp.zeros((8 - size, 8, COLS), jnp.float32)], axis=0
                 )
-            block = jnp.swapaxes(block, 0, 1)
-            grid[rb * 8 : rb * 8 + 8, part, :] = block
-            if rb == 0:
-                low[:, part, :] = block[0:2]
-            if rb == 3:
-                high[:, part, :] = block[6:8]
+            grid[rb * 8 : rb * 8 + 8, part, :] = jnp.swapaxes(block, 0, 1)
+    odd = lax.rem(lax.axis_index("tile"), 2)
+    to_pair[...] = grid[pl.ds((1 - odd) * (ROWS - 2), 2), :, :]
+    to_other[...] = grid[pl.ds(odd * (ROWS - 2), 2), :, :]
 
 
 def prepare(spectrum):
@@ -134,17 +132,15 @@
     yield
 
 
-def shifted(tiles, lane):
+def shifted(tiles, lane, far_lane, take_back, take_ahead):
     ahead = [pltpu.roll(v, LANES - 1, axis=1) for v in tiles] + [0.0]
     back = [0.0] + [pltpu.roll(v, 1, axis=1) for v in tiles]
-    ahead_two = [pltpu.roll(v, LANES - 2, axis=1) for v in tiles] + [0.0]
-    back_two = [0.0] + [pltpu.roll(v, 2, axis=1) for v in tiles]
+    far = [0.0] + [lane_gather(v, far_lane) for v in tiles] + [0.0]
     return [
         (
             jnp.where(lane < LANES - 1, ahead[t], ahead[t + 1]),
             jnp.where(lane >= 1, back[t + 1], back[t]),
-            jnp.where(lane < LANES - 2, ahead_two[t], ahead_two[t + 1]),
-            jnp.where(lane >= 2, back_two[t + 1], back_two[t]),
+            jnp.where(take_back, far[t], jnp.where(take_ahead, far[t + 2], far[t + 1])),
         )
         for t in range(TILES)
     ]
@@ -188,6 +184,12 @@
             for c in (centre_coef, x_ahead, x_back, x_far, x_up, y_ahead, y_back, y_far, y_up)
         ]
 
+        far_from = (
+            (lane + jnp.where(xu, LANES - 2, 2)) & (LANES - 1),
+            xu & (lane < 2),
+            jnp.logical_not(xu) & (lane >= LANES - 2),
+        )
+
         def row_step(r, rows, depth_row):
             results = []
             centre = [grid[r, part, t * LANES : (t + 1) * LANES] for t in range(TILES)]
@@ -197,9 +199,9 @@
                     return jnp.zeros((8, LANES), jnp.float32)
                 return grid[r + i, part, t * LANES : (t + 1) * LANES]
 
-            for t, (ahead, back, ahead_two, back_two) in enumerate(shifted(centre, lane)):
+            for t, (ahead, back, far) in enumerate(shifted(centre, lane, *far_from)):
                 total = c0 * centre[t] + xa * ahead + xb * back
-                total += xf * jnp.where(xu, back_two, ahead_two)
+                total += xf * far
                 total += ya * near(1, t) + yb * near(-1, t)
                 total += yf * jnp.where(yu, near(-2, t), near(2, t))
                 lanes = slice(t * LANES, (t + 1) * LANES)
@@ -263,10 +265,13 @@
     return value
 
 
-def compact_kernel(kind, mixed, low, high, depth, halo_coef, pick, out, terms, fixed, spare, tails):
+def compact_kernel(kind, mixed, from_pair, from_other, depth, halo_coef, pick, out, terms, fixed, spare, tails):
     lane = iota((8, LANES), 1)
     strip = lane >> 4
     back, back_two, ahead, ahead_two = [wide(halo_coef[i]) for i in range(4)]
+    odd = lax.rem(lax.axis_index("tile"), 2) == 1
+    low = [jnp.where(odd, from_pair[i], from_other[i]) for i in range(2)]
+    high = [jnp.where(odd, from_other[i], from_pair[i]) for i in range(2)]
     terms[0] = depth[0:1, :] * (back * low[1] + back_two * low[0])
     terms[1] = depth[1:2, :] * (back_two * low[1])
     terms[2] = depth[ROWS - 2 : ROWS - 1, :] * (ahead_two * high[0])
@@ -325,7 +330,7 @@
                     out[d, row : row + 3, :] = value[0:3]
 
 
-def compact(kind, mixed, low, high, depth, halo_coef, pick):
+def compact(kind, mixed, from_pair, from_other, depth, halo_coef, pick):
     return pl.pallas_call(
         functools.partial(compact_kernel, kind),
         out_shape=jax.ShapeDtypeStruct((OWNERS, block_rows(kind), LANES), jnp.float32),
@@ -340,7 +345,7 @@
         compiler_params=PARAMS,
         cost_estimate=pl.CostEstimate(flops=5000000, bytes_accessed=4000000, transcendentals=0),
         name="compact",
-    )(mixed, low, high, depth, halo_coef, pick)
+    )(mixed, from_pair, from_other, depth, halo_coef, pick)
 
 
 def runs():
@@ -572,18 +577,21 @@
     spectrum, speed, depth, turn, sea_mask, refraction, growth, dissipation, quad_first, quad_second
 ):
     count = lax.axis_size("tile")
-    forward = [(i, i + 1) for i in range(count - 1)]
-    backward = [(i + 1, i) for i in range(count - 1)]
-    grid, first, last = prepare(spectrum)
-    low = lax.ppermute(last, "tile", forward)
-    high = lax.ppermute(first, "tile", backward)
+
+    def swap(rows, begin):
+        pairs = [(i, i + 1) for i in range(begin, count - 1, 2)]
+        return lax.ppermute(rows, "tile", pairs + [(j, i) for i, j in pairs])
+
+    grid, to_pair, to_other = prepare(spectrum)
+    from_pair = swap(to_pair, 0)
+    from_other = swap(to_other, 1)
     mixed, halo_coef, pick, rank, turn_own, chosen = propagate(
         grid, depth, turn, sea_mask, speed
     )
 
     def rest(kind):
-        def run(mixed, low, high):
-            sent = compact(kind, mixed, low, high, depth, halo_coef, pick)
+        def run(mixed, from_pair, from_other):
+            sent = compact(kind, mixed, from_pair, from_other, depth, halo_coef, pick)
             points = exchange(sent)
             result = sources(
                 kind, points, turn_own, refraction, growth, dissipation, quad_first, quad_second
@@ -592,7 +600,7 @@
 
         return run
 
-    return finish(lax.switch(chosen[0], [rest(kind) for kind in KINDS], mixed, low, high))
+    return finish(lax.switch(chosen[0], [rest(kind) for kind in KINDS], mixed, from_pair, from_other))
 
 
 def solution(mesh):

time: 75.7 us -> 73.1 us (0.966)
  starting transfers between devices: 6.81 us -> 5.56 us
  blocking collectives: 52.9 us -> 52 us
    ppermute x2, starting transfers between devices: 6.81 us -> 5.56 us  [swap(): return lax.ppermute(rows, 'tile', pairs + [(j, i) for i, j in pairs])]
    all_to_all x2, blocking collectives: 52.9 us -> 52 us  [exchange(): lax.all_to_all(blocks, 'comp', split_axis=0, concat_axis=0, tiled=True)]
  transfers between devices with their start and end apart: 2 -> 2, of which waited for: 1 -> 0; matrix products, arithmetic and copies ran while one was open for 0% -> 0% of each run, Pallas kernels for 5% -> 5%
where the time goes in v6:
time: 73.1 us; the launch traced here: 72.8 us
  blocking collectives  52 us (71%)
  Pallas kernels  12.5 us (17%)
  starting transfers between devices  5.56 us (8%)
  local copies, waits for them, and re-layouts  1.51 us (2%)
  between operations  1 us (1%)
    all_to_all x2, blocking collectives, exchange(): lax.all_to_all(blocks, 'comp', split_axis=0, concat_axis=0, tiled=True)  52 us
    ppermute x2, starting transfers between devices, swap(): return lax.ppermute(rows, 'tile', pairs + [(j, i) for i, j in pairs])  5.56 us
    pallas_call x1, Pallas kernels, propagate(): pl.pallas_call(propagate_kernel, out_shape=[jax.ShapeDtypeStruct((ROWS, P...  3.7 us
    pallas_call x1, Pallas kernels, sources(): pl.pallas_call(functools.partial(source_kernel, kind), out_shape=jax.Shap...  3.4 us
    pallas_call x1, Pallas kernels, compact(): pl.pallas_call(functools.partial(compact_kernel, kind), out_shape=jax.Sha...  1.83 us
    pallas_call x1, Pallas kernels, expand(): pl.pallas_call(functools.partial(expand_kernel, kind), out_shape=jax.Shap...  1.79 us
    unnamed x20, local copies, waits for them, and re-layouts  1.51 us
  transfers between devices with their start and end apart: 2, of which 0 were waited for; matrix products, arithmetic and copies ran while one was open for 0% of the time, Pallas kernels for 5%

profile of v6, /device:TPU:97, one launch (start us, length us, event | category | flops | bytes accessed | tf_op | source)
XLA Modules:
  0.0 72.8 jit_solution(13207619005360413111)
XLA Ops:
  0.0 0.0 copy-start
  0.0 1.5 %copy-done = f32[27,32,512]{2,1,0:T(8,128)S(1)} copy-done((f32[27,32,512]{2,1,0:T(8,128)S(1)}, f32[27,32,512]{2,1,0:T(8,128)}, u32[]{:S(2)}) %copy-start) | copy-done | bytes 1769496
  1.5 0.0 copy-start.1
  1.5 0.0 copy-start.2
  1.5 0.0 copy-start.3
  1.5 0.0 copy-start.5
  1.5 0.0 copy-start.6
  1.5 0.0 copy-start.7
  1.5 0.0 copy-start.8
  1.5 0.0 copy-start.9
  1.5 0.4 prepare.1
  1.9 0.1 collective-permute-start
  2.0 5.5 %collective-permute-start.1 = (f32[2,32,512]{2,1,0:T(8,128)S(1)}, f32[2,32,512]{2,1,0:T(8,128)S(1)}, u32[]{:S(2)}, u32[]{:S(2)}) collective-permute-start(f32[2,32,512]{2,1,0:T(8,128)S(1)} %get-tuple-element.139), channel_id=1, source_target_pairs={{1,2},{3,4},{5,6},{2,1},{4,3},{6,5},{9,10},{11,12},{13,14},{10,9},... | collective-permute-start | bytes 393224 | tf_op jit(solution)/shard_map/ppermute | solution.py:583
  7.5 0.0 copy-done.1
  7.5 0.0 copy-done.2
  7.5 0.0 copy-done.3
  7.5 3.7 %propagate.1 = (f32[32,32,512]{2,1,0:T(8,128)S(1)}, f32[4,32,128]{2,1,0:T(8,128)S(1)}, s32[32,512]{1,0:T(8,128)S(1)}, s32[32,512]{1,0:T(8,128)S(1)}, f32[8,512]{1,0:T(8,128)S(1)}, /*index=5*/s32[1]{0:T(128)}) custom-call(f32[32,32,512]{2,1,0:T(8,128)S(1)} %get-tuple-element.135.grid, f32[32,512]{1,0:T(8,128)} %depth.1, f32[32,512]{1,0:T(8,128)S(1)} %copy-done.1, ...), custom_call_target="tpu_custom_call" | custom-call | flops 20000000 | bytes 4000000 | tf_op jit(solution)/shard_map/propagate/pallas_call | solution.py:224
  11.9 0.0 collective-permute-done
  11.9 0.0 collective-permute-done.1
  11.9 0.0 copy-done.4
  11.9 0.0 copy-done.5
  11.9 0.0 copy-done.6
  11.9 0.0 copy-done.7
  11.9 0.0 copy-done.8
  12.0 0.0 copy-done.9
  12.0 59.3 %conditional.1 = (f32[32,32,512]{2,1,0:T(8,128)S(1)}) conditional(s32[]{:T(128)} %bitcast, (f32[32,32,512]{2,1,0:T(8,128)S(1)}, f32[2,32,512]{2,1,0:T(8,128)S(1)}, f32[2,32,512]{2,1,0:T(8,128)S(1)}, f32[32,512]{1,0:T(8,128)S(1)}, f32[4,32,128]{2,1,0:T(8,128)S(1)}, /*index=5*/s32[32,512]{1,0:T(8,128)S(1)}, f32[8,512]{1,0:T(8,128)S(1)}, ...), branch_computations={%region_0.0_spmd, %region_1.0_spmd, %region_2.0_spmd} | conditional | flops 1538823680 | bytes 21340040 | solution.py:603
  12.0 1.8 %compact.3 = f32[32,80,128]{2,1,0:T(8,128)S(1)} custom-call(f32[32,32,512]{2,1,0:T(8,128)S(1)} %get-tuple-element.86.mixed, f32[2,32,512]{2,1,0:T(8,128)S(1)} %get-tuple-element.88.from_pair, f32[2,32,512]{2,1,0:T(8,128)S(1)} %get-tuple-element.89.from_other, f32[32,512]{1,0:T(8,128)S(1)} %get-tuple-element.90.depth, ...), custom_call_target="tpu_custom_call" | custom-call | flops 5000000 | bytes 4000000 | tf_op jit(solution)/shard_map/cond/branch_0_fun/compact/pallas_call | solution.py:334
  13.8 28.3 %all_to_all.24.points = f32[32,80,128]{2,1,0:T(8,128)S(1)} all-to-all(f32[32,80,128]{2,1,0:T(8,128)S(1)} %compact.3), channel_id=1, replica_groups=mesh['comp'=32,'tile'=8] {'comp'}, dimensions={0} | all-to-all | bytes 2621440 | tf_op jit(solution)/shard_map/cond/branch_0_fun/all_to_all | solution.py:573
  42.1 3.4 %sources.3 = f32[32,80,128]{2,1,0:T(8,128)S(1)} custom-call(f32[32,80,128]{2,1,0:T(8,128)S(1)} %all_to_all.24.points, f32[8,512]{1,0:T(8,128)S(1)} %get-tuple-element.93.turn_own, f32[24]{0:T(128)S(1)} %get-tuple-element.94.refraction, f32[864]{0:T(1024)S(1)} %get-tuple-element.95.growth, f32[864]{0:T(1024)S(1)} %get-tuple-element.96.dissipation, ...), custom_call_target="tpu_custom_call" | custom-call | flops 1146617856 | bytes 6000000 | tf_op jit(solution)/shard_map/cond/branch_0_fun/sources/pallas_call | solution.py:464
  45.5 23.7 %all_to_all.25.result = f32[32,80,128]{2,1,0:T(8,128)S(1)} all-to-all(f32[32,80,128]{2,1,0:T(8,128)S(1)} %sources.3), channel_id=1, replica_groups=mesh['comp'=32,'tile'=8] {'comp'}, dimensions={0} | all-to-all | bytes 2621440 | tf_op jit(solution)/shard_map/cond/branch_0_fun/all_to_all | solution.py:573
  69.2 1.8 %expand.3 = f32[32,32,512]{2,1,0:T(8,128)S(1)} custom-call(f32[32,80,128]{2,1,0:T(8,128)S(1)} %all_to_all.25.result, s32[32,512]{1,0:T(8,128)S(1)} %get-tuple-element.99.rank), custom_call_target="tpu_custom_call" | custom-call | flops 5000000 | bytes 4000000 | tf_op jit(solution)/shard_map/cond/branch_0_fun/expand/pallas_call | solution.py:526
  71.2 1.4 %finish.1 = f32[27,32,512]{2,1,0:T(8,128)} custom-call(f32[32,32,512]{2,1,0:T(8,128)S(1)} %get-tuple-element.144.mixed), custom_call_target="tpu_custom_call" | custom-call | flops 5000000 | bytes 4000000 | tf_op jit(solution)/shard_map/finish/pallas_call | solution.py:557
  (1 shorter events, 0.0 us)
Async XLA Ops:
  0.0 1.5 %copy-start = (f32[27,32,512]{2,1,0:T(8,128)S(1)}, f32[27,32,512]{2,1,0:T(8,128)}, u32[]{:S(2)}) copy-start(f32[27,32,512]{2,1,0:T(8,128)} %spec.1) | copy-start | bytes 5308420
  1.5 6.0 %copy-start.1 = (f32[32,512]{1,0:T(8,128)S(1)}, f32[32,512]{1,0:T(8,128)}, u32[]{:S(2)}) copy-start(f32[32,512]{1,0:T(8,128)} %turn.1) | copy-start | bytes 196612
  1.5 6.0 %copy-start.2 = (s32[32,512]{1,0:T(8,128)S(1)}, s32[32,512]{1,0:T(8,128)}, u32[]{:S(2)}) copy-start(s32[32,512]{1,0:T(8,128)} %mask.1) | copy-start | bytes 196612
  1.5 6.0 %copy-start.3 = (f32[27]{0:T(128)S(1)}, f32[27]{0:T(128)}, u32[]{:S(2)}) copy-start(f32[27]{0:T(128)} %speed.1) | copy-start | bytes 328
  1.5 10.4 %copy-start.4 = (bf16[864,864]{1,0:T(8,128)(2,1)S(1)}, bf16[864,864]{1,0:T(8,128)(2,1)}, u32[]{:S(2)}) copy-start(bf16[864,864]{1,0:T(8,128)(2,1)} %param.21) | copy-start | bytes 4478980
  1.5 10.4 %copy-start.5 = (bf16[864,864]{1,0:T(8,128)(2,1)S(1)}, bf16[864,864]{1,0:T(8,128)(2,1)}, u32[]{:S(2)}) copy-start(bf16[864,864]{1,0:T(8,128)(2,1)} %param.22) | copy-start | bytes 4478980
  1.5 10.4 %copy-start.6 = (f32[32,512]{1,0:T(8,128)S(1)}, f32[32,512]{1,0:T(8,128)}, u32[]{:S(2)}) copy-start(f32[32,512]{1,0:T(8,128)} %depth.1) | copy-start | bytes 196612
  1.5 10.4 %copy-start.7 = (f32[864]{0:T(1024)S(1)}, f32[864]{0:T(1024)}, u32[]{:S(2)}) copy-start(f32[864]{0:T(1024)} %param.19) | copy-start | bytes 10372
  1.5 10.4 %copy-start.8 = (f32[864]{0:T(1024)S(1)}, f32[864]{0:T(1024)}, u32[]{:S(2)}) copy-start(f32[864]{0:T(1024)} %param.20) | copy-start | bytes 10372
  1.5 10.4 %copy-start.9 = (f32[24]{0:T(128)S(1)}, f32[24]{0:T(128)}, u32[]{:S(2)}) copy-start(f32[24]{0:T(128)} %param.18) | copy-start | bytes 292
  1.9 10.0 %collective-permute-start = (f32[2,32,512]{2,1,0:T(8,128)S(1)}, f32[2,32,512]{2,1,0:T(8,128)S(1)}, u32[]{:S(2)}, u32[]{:S(2)}) collective-permute-start(f32[2,32,512]{2,1,0:T(8,128)S(1)} %get-tuple-element.138), channel_id=1, source_target_pairs={{0,1},{2,3},{4,5},{6,7},{1,0},{3,2},{5,4},{7,6},{8,9},{10,11},{12,... | collective-permute-start | bytes 393224 | tf_op jit(solution)/shard_map/ppermute | solution.py:583
  2.0 9.9 %collective-permute-start.1 = (f32[2,32,512]{2,1,0:T(8,128)S(1)}, f32[2,32,512]{2,1,0:T(8,128)S(1)}, u32[]{:S(2)}, u32[]{:S(2)}) collective-permute-start(f32[2,32,512]{2,1,0:T(8,128)S(1)} %get-tuple-element.139), channel_id=1, source_target_pairs={{1,2},{3,4},{5,6},{2,1},{4,3},{6,5},{9,10},{11,12},{13,14},{10,9},... | collective-permute-start | bytes 393224 | tf_op jit(solution)/shard_map/ppermute | solution.py:583

commit v7 on v6

--- a/solution.py
+++ b/solution.py
@@ -147,7 +147,7 @@
 
 
 def propagate_kernel(
-    grid, depth, turn, mask, speed, mixed, halo_coef, pick, rank, turn_own, chosen
+    grid, depth, turn, mask, speed, mixed, halo_coef, edge_depth, pick, rank, turn_own, chosen
 ):
     me = lax.axis_index("comp")
     beside = index_steps(me, turn, mask, pick, rank, turn_own, chosen)
@@ -170,6 +170,8 @@
 
     x_centre, x_ahead, x_back, x_far, x_up = taps(speeds * jnp.cos(theta))
     y_centre, y_ahead, y_back, y_far, y_up = taps(speeds * jnp.sin(theta))
+    edge_depth[0:2, :] = depth[0:2, :]
+    edge_depth[2:4, :] = depth[ROWS - 2 : ROWS, :]
     halo_coef[0] = y_back
     halo_coef[1] = jnp.where(y_up, y_far, 0.0)
     halo_coef[2] = y_ahead
@@ -226,13 +228,14 @@
         out_shape=[
             jax.ShapeDtypeStruct((ROWS, PAD, COLS), jnp.float32),
             jax.ShapeDtypeStruct((4, PAD, LANES), jnp.float32),
+            jax.ShapeDtypeStruct((4, COLS), jnp.float32),
             plane,
             plane,
             jax.ShapeDtypeStruct((8, COLS), jnp.float32),
             jax.ShapeDtypeStruct((1,), jnp.int32),
         ],
         in_specs=[VMEM, VMEM, VMEM, VMEM, SMEM],
-        out_specs=[VMEM] * 5 + [SMEM],
+        out_specs=[VMEM] * 6 + [SMEM],
         compiler_params=PARAMS,
         cost_estimate=pl.CostEstimate(flops=20000000, bytes_accessed=4000000, transcendentals=0),
         name="propagate",
@@ -265,17 +268,17 @@
     return value
 
 
-def compact_kernel(kind, mixed, from_pair, from_other, depth, halo_coef, pick, out, terms, fixed, spare, tails):
+def compact_kernel(kind, mixed, from_pair, from_other, edge_depth, halo_coef, pick, out, terms, fixed, spare, tails):
     lane = iota((8, LANES), 1)
     strip = lane >> 4
     back, back_two, ahead, ahead_two = [wide(halo_coef[i]) for i in range(4)]
     odd = lax.rem(lax.axis_index("tile"), 2) == 1
     low = [jnp.where(odd, from_pair[i], from_other[i]) for i in range(2)]
     high = [jnp.where(odd, from_other[i], from_pair[i]) for i in range(2)]
-    terms[0] = depth[0:1, :] * (back * low[1] + back_two * low[0])
-    terms[1] = depth[1:2, :] * (back_two * low[1])
-    terms[2] = depth[ROWS - 2 : ROWS - 1, :] * (ahead_two * high[0])
-    terms[3] = depth[ROWS - 1 : ROWS, :] * (ahead * high[0] + ahead_two * high[1])
+    terms[0] = edge_depth[0:1, :] * (back * low[1] + back_two * low[0])
+    terms[1] = edge_depth[1:2, :] * (back_two * low[1])
+    terms[2] = edge_depth[2:3, :] * (ahead_two * high[0])
+    terms[3] = edge_depth[3:4, :] * (ahead * high[0] + ahead_two * high[1])
 
     for g in range(4):
         for first, row, t in ((0, 0, g), (2, 6, 3 - g)):
@@ -330,7 +333,7 @@
                     out[d, row : row + 3, :] = value[0:3]
 
 
-def compact(kind, mixed, from_pair, from_other, depth, halo_coef, pick):
+def compact(kind, mixed, from_pair, from_other, edge_depth, halo_coef, pick):
     return pl.pallas_call(
         functools.partial(compact_kernel, kind),
         out_shape=jax.ShapeDtypeStruct((OWNERS, block_rows(kind), LANES), jnp.float32),
@@ -345,7 +348,7 @@
         compiler_params=PARAMS,
         cost_estimate=pl.CostEstimate(flops=5000000, bytes_accessed=4000000, transcendentals=0),
         name="compact",
-    )(mixed, from_pair, from_other, depth, halo_coef, pick)
+    )(mixed, from_pair, from_other, edge_depth, halo_coef, pick)
 
 
 def runs():
@@ -480,7 +483,7 @@
     )(points, turn_own, refraction, growth, dissipation, first, second)
 
 
-def expand_kernel(kind, result, rank, mixed, last):
+def expand_kernel(kind, result, rank, field, last):
     whole, short = kind
     slots = slots_of(kind)
     tail_rows = (3 * whole + 7) // 8 * 8
@@ -492,40 +495,46 @@
         value = jnp.where(row_at == 1, parts[1], parts[0])
         last[d] = jnp.where(row_at == 2, parts[2], value)
 
-    def owner_step(d, rank_row):
+    def value_of(d, cb, slot):
+        if cb < 3:
+            return result[d, slot * 24 + cb * 8 : slot * 24 + cb * 8 + 8, :]
+        if slot >= whole:
+            return last[d]
         tail = result[d, 24 * slots : 24 * slots + tail_rows, :]
-        values = []
-        for slot in range(slots):
-            parts = [result[d, slot * 24 + cb * 8 : slot * 24 + cb * 8 + 8, :] for cb in range(3)]
-            if slot < whole:
-                parts.append(pltpu.roll(tail, (tail_rows - 3 * slot) % tail_rows, axis=0)[0:8])
-            else:
-                parts.append(last[d])
-            values.append(parts)
-        for t in range(TILES):
-            index = jnp.broadcast_to(rank_row[:, t * LANES : (t + 1) * LANES], (8, LANES))
-            slot_of = index >> 7
-            land = index < 0
-            index = index & (LANES - 1)
-            for cb in range(4):
-                total = lane_gather(values[0][cb], index)
-                for slot in range(1, min(t + 1, slots)):
-                    total = jnp.where(slot_of == slot, lane_gather(values[slot][cb], index), total)
-                mixed[d, cb * 8 : cb * 8 + 8, t * LANES : (t + 1) * LANES] = jnp.where(
-                    land, 0.0, total
-                )
+        return pltpu.roll(tail, (tail_rows - 3 * slot) % tail_rows, axis=0)[0:8]
+
+    def owner_cells(d, t):
+        index = jnp.broadcast_to(rank[d : d + 1, t * LANES : (t + 1) * LANES], (8, LANES))
+        land = index < 0
+        among = [index >> 7 == slot for slot in range(slots)]
+        index = index & (LANES - 1)
+        cells = []
+        for cb in range(4):
+            total = lane_gather(value_of(d, cb, 0), index)
+            for slot in range(1, min(t + 1, slots)):
+                total = jnp.where(among[slot], lane_gather(value_of(d, cb, slot), index), total)
+            cells.append(jnp.where(land, 0.0, total))
+        return cells
 
     if short:
         for d in range(OWNERS):
             short_step(d)
-    for d in range(OWNERS):
-        owner_step(d, rank[d : d + 1, :])
+    lane = iota((8, LANES), 1)
+    for g in range(4):
+        for t in range(TILES):
+            cells = [owner_cells(g * 8 + j, t) for j in range(8)]
+            rows = slice((g ^ t) * 8, (g ^ t) * 8 + 8)
+            for cb in range(4):
+                size = min(8, HELD - cb * 8)
+                block = butterfly([cell[cb] for cell in cells], lane)
+                block = jnp.swapaxes(jnp.stack(block), 0, 1)
+                field[cb * 8 : cb * 8 + size, rows, t * LANES : (t + 1) * LANES] = block[0:size]
 
 
 def expand(kind, result, rank):
     return pl.pallas_call(
         functools.partial(expand_kernel, kind),
-        out_shape=jax.ShapeDtypeStruct((OWNERS, PAD, COLS), jnp.float32),
+        out_shape=jax.ShapeDtypeStruct((HELD, ROWS, COLS), jnp.float32),
         in_specs=[VMEM] * 2,
         out_specs=VMEM,
         scratch_shapes=[pltpu.VMEM((OWNERS, 8, LANES), jnp.float32)],
@@ -535,38 +544,27 @@
     )(result, rank)
 
 
-def finish_kernel(mixed, out, done, leaving):
-    lane = iota((8, LANES), 1)
+def finish_kernel(field, out, leaving):
     copies = []
     for cb in range(4):
-        size = min(8, HELD - cb * 8)
-        for g in range(4):
-            for t in range(TILES):
-                lanes = slice(t * LANES, (t + 1) * LANES)
-                rows = [mixed[(g ^ t) * 8 + j, cb * 8 : cb * 8 + 8, lanes] for j in range(8)]
-                block = jnp.swapaxes(jnp.stack(butterfly(rows, lane)), 0, 1)
-                done[cb * 8 : cb * 8 + size, g * 8 : g * 8 + 8, lanes] = block[0:size]
-        part = slice(cb * 8, cb * 8 + size)
-        copies.append(pltpu.make_async_copy(done.at[part], out.at[part], leaving.at[cb]))
+        part = slice(cb * 8, min(cb * 8 + 8, HELD))
+        copies.append(pltpu.make_async_copy(field.at[part], out.at[part], leaving.at[cb]))
         copies[cb].start()
     for copy in copies:
         copy.wait()
 
 
-def finish(mixed):
+def finish(field):
     return pl.pallas_call(
         finish_kernel,
         out_shape=jax.ShapeDtypeStruct((HELD, ROWS, COLS), jnp.float32),
         in_specs=[VMEM],
         out_specs=ANY,
-        scratch_shapes=[
-            pltpu.VMEM((HELD, ROWS, COLS), jnp.float32),
-            pltpu.SemaphoreType.DMA((4,)),
-        ],
+        scratch_shapes=[pltpu.SemaphoreType.DMA((4,))],
         compiler_params=PARAMS,
-        cost_estimate=pl.CostEstimate(flops=5000000, bytes_accessed=4000000, transcendentals=0),
+        cost_estimate=pl.CostEstimate(flops=0, bytes_accessed=4000000, transcendentals=0),
         name="finish",
-    )(mixed)
+    )(field)
 
 
 def exchange(blocks):
@@ -585,13 +583,13 @@
     grid, to_pair, to_other = prepare(spectrum)
     from_pair = swap(to_pair, 0)
     from_other = swap(to_other, 1)
-    mixed, halo_coef, pick, rank, turn_own, chosen = propagate(
+    mixed, halo_coef, edge_depth, pick, rank, turn_own, chosen = propagate(
         grid, depth, turn, sea_mask, speed
     )
 
     def rest(kind):
         def run(mixed, from_pair, from_other):
-            sent = compact(kind, mixed, from_pair, from_other, depth, halo_coef, pick)
+            sent = compact(kind, mixed, from_pair, from_other, edge_depth, halo_coef, pick)
             points = exchange(sent)
             result = sources(
                 kind, points, turn_own, refraction, growth, dissipation, quad_first, quad_second

time: 73.1 us -> 72.2 us (0.988)
  Pallas kernels: 12.5 us -> 11.7 us
  transfers between devices with their start and end apart: 2 -> 2, of which waited for: 0 -> 0; matrix products, arithmetic and copies ran while one was open for 0% -> 0% of each run, Pallas kernels for 5% -> 4%
where the time goes in v7:
time: 72.2 us; the launch traced here: 72 us
  blocking collectives  52 us (72%)
  Pallas kernels  11.7 us (16%)
  starting transfers between devices  5.56 us (8%)
  local copies, waits for them, and re-layouts  1.51 us (2%)
  between operations  1 us (1%)
    all_to_all x2, blocking collectives, exchange(): lax.all_to_all(blocks, 'comp', split_axis=0, concat_axis=0, tiled=True)  52 us
    ppermute x2, starting transfers between devices, swap(): return lax.ppermute(rows, 'tile', pairs + [(j, i) for i, j in pairs])  5.56 us
    pallas_call x1, Pallas kernels, sources(): pl.pallas_call(functools.partial(source_kernel, kind), out_shape=jax.Shap...  3.4 us
    pallas_call x1, Pallas kernels, propagate(): pl.pallas_call(propagate_kernel, out_shape=[jax.ShapeDtypeStruct((ROWS, P...  3.01 us
    pallas_call x1, Pallas kernels, expand(): pl.pallas_call(functools.partial(expand_kernel, kind), out_shape=jax.Shap...  1.84 us
    pallas_call x1, Pallas kernels, compact(): pl.pallas_call(functools.partial(compact_kernel, kind), out_shape=jax.Sha...  1.83 us
    unnamed x20, local copies, waits for them, and re-layouts  1.51 us
  transfers between devices with their start and end apart: 2, of which 0 were waited for; matrix products, arithmetic and copies ran while one was open for 0% of the time, Pallas kernels for 4%

profile of v7, /device:TPU:97, one launch (start us, length us, event | category | flops | bytes accessed | tf_op | source)
XLA Modules:
  0.0 72.0 jit_solution(15033051937484501201)
XLA Ops:
  0.0 0.0 copy-start
  0.0 1.5 %copy-done = f32[27,32,512]{2,1,0:T(8,128)S(1)} copy-done((f32[27,32,512]{2,1,0:T(8,128)S(1)}, f32[27,32,512]{2,1,0:T(8,128)}, u32[]{:S(2)}) %copy-start) | copy-done | bytes 1769496
  1.5 0.0 copy-start.1
  1.5 0.0 copy-start.2
  1.5 0.0 copy-start.3
  1.5 0.0 copy-start.5
  1.5 0.0 copy-start.6
  1.5 0.0 copy-start.7
  1.5 0.0 copy-start.8
  1.5 0.0 copy-start.9
  1.5 0.4 prepare.1
  1.9 0.1 collective-permute-start
  2.0 5.5 %collective-permute-start.1 = (f32[2,32,512]{2,1,0:T(8,128)S(1)}, f32[2,32,512]{2,1,0:T(8,128)S(1)}, u32[]{:S(2)}, u32[]{:S(2)}) collective-permute-start(f32[2,32,512]{2,1,0:T(8,128)S(1)} %get-tuple-element.140), channel_id=1, source_target_pairs={{1,2},{3,4},{5,6},{2,1},{4,3},{6,5},{9,10},{11,12},{13,14},{10,9},... | collective-permute-start | bytes 393224 | tf_op jit(solution)/shard_map/ppermute | solution.py:581
  7.5 0.0 copy-done.1
  7.5 0.0 copy-done.2
  7.5 0.0 copy-done.3
  7.5 0.0 copy-done.4
  7.5 3.0 %propagate.1 = (f32[32,32,512]{2,1,0:T(8,128)S(1)}, f32[4,32,128]{2,1,0:T(8,128)S(1)}, f32[4,512]{1,0:T(4,128)S(1)}, s32[32,512]{1,0:T(8,128)S(1)}, s32[32,512]{...) custom-call(f32[32,32,512]{2,1,0:T(8,128)S(1)} %get-tuple-element.136.grid, f32[32,512]{1,0:T(8,128)S(1)} %copy-done.1, ...), custom_call_target="tpu_custom_call" | custom-call | flops 20000000 | bytes 4000000 | tf_op jit(solution)/shard_map/propagate/pallas_call | solution.py:226
  11.2 0.0 collective-permute-done
  11.2 0.0 collective-permute-done.1
  11.2 0.0 copy-done.5
  11.2 0.0 copy-done.6
  11.2 0.0 copy-done.7
  11.2 0.0 copy-done.8
  11.3 0.0 copy-done.9
  11.3 59.3 %conditional.1 = (f32[27,32,512]{2,1,0:T(8,128)S(1)}) conditional(s32[]{:T(128)} %bitcast, (f32[32,32,512]{2,1,0:T(8,128)S(1)}, f32[2,32,512]{2,1,0:T(8,128)S(1)}, f32[2,32,512]{2,1,0:T(8,128)S(1)}, f32[4,512]{1,0:T(4,128)S(1)}, f32[4,32,128]{2,1,0:T(8,128)S(1)}, /*index=5*/s32[32,512]{1,0:T(8,128)S(1)}, f32[8,512]{1,0:T(8,128)S(1)}, ...), branch_computations={%region_0.0_spmd, %region_1.0_spmd, %region_2.0_spmd} | conditional | flops 1538823680 | bytes 21340040 | solution.py:601
  11.3 1.8 %compact.3 = f32[32,80,128]{2,1,0:T(8,128)S(1)} custom-call(f32[32,32,512]{2,1,0:T(8,128)S(1)} %get-tuple-element.86.mixed, f32[2,32,512]{2,1,0:T(8,128)S(1)} %get-tuple-element.88.from_pair, f32[2,32,512]{2,1,0:T(8,128)S(1)} %get-tuple-element.89.from_other, f32[4,512]{1,0:T(4,128)S(1)} %get-tuple-element.90.edge_depth, ...), custom_call_target="tpu_custom_call" | custom-call | flops 5000000 | bytes 4000000 | tf_op jit(solution)/shard_map/cond/branch_0_fun/compact/pallas_call | solution.py:337
  13.1 28.3 %all_to_all.24.points = f32[32,80,128]{2,1,0:T(8,128)S(1)} all-to-all(f32[32,80,128]{2,1,0:T(8,128)S(1)} %compact.3), channel_id=1, replica_groups=mesh['comp'=32,'tile'=8] {'comp'}, dimensions={0} | all-to-all | bytes 2621440 | tf_op jit(solution)/shard_map/cond/branch_0_fun/all_to_all | solution.py:571
  41.4 3.4 %sources.3 = f32[32,80,128]{2,1,0:T(8,128)S(1)} custom-call(f32[32,80,128]{2,1,0:T(8,128)S(1)} %all_to_all.24.points, f32[8,512]{1,0:T(8,128)S(1)} %get-tuple-element.93.turn_own, f32[24]{0:T(128)S(1)} %get-tuple-element.94.refraction, f32[864]{0:T(1024)S(1)} %get-tuple-element.95.growth, f32[864]{0:T(1024)S(1)} %get-tuple-element.96.dissipation, ...), custom_call_target="tpu_custom_call" | custom-call | flops 1146617856 | bytes 6000000 | tf_op jit(solution)/shard_map/cond/branch_0_fun/sources/pallas_call | solution.py:467
  44.8 23.7 %all_to_all.25.result = f32[32,80,128]{2,1,0:T(8,128)S(1)} all-to-all(f32[32,80,128]{2,1,0:T(8,128)S(1)} %sources.3), channel_id=1, replica_groups=mesh['comp'=32,'tile'=8] {'comp'}, dimensions={0} | all-to-all | bytes 2621440 | tf_op jit(solution)/shard_map/cond/branch_0_fun/all_to_all | solution.py:571
  68.5 1.8 %expand.3 = f32[27,32,512]{2,1,0:T(8,128)S(1)} custom-call(f32[32,80,128]{2,1,0:T(8,128)S(1)} %all_to_all.25.result, s32[32,512]{1,0:T(8,128)S(1)} %get-tuple-element.99.rank), custom_call_target="tpu_custom_call" | custom-call | flops 5000000 | bytes 4000000 | tf_op jit(solution)/shard_map/cond/branch_0_fun/expand/pallas_call | solution.py:535
  70.6 1.2 %finish.1 = f32[27,32,512]{2,1,0:T(8,128)} custom-call(f32[27,32,512]{2,1,0:T(8,128)S(1)} %get-tuple-element.146.field), custom_call_target="tpu_custom_call" | custom-call | bytes 4000000 | tf_op jit(solution)/shard_map/finish/pallas_call | solution.py:558
  (1 shorter events, 0.0 us)
Async XLA Ops:
  0.0 1.5 %copy-start = (f32[27,32,512]{2,1,0:T(8,128)S(1)}, f32[27,32,512]{2,1,0:T(8,128)}, u32[]{:S(2)}) copy-start(f32[27,32,512]{2,1,0:T(8,128)} %spec.1) | copy-start | bytes 5308420
  1.5 6.0 %copy-start.1 = (f32[32,512]{1,0:T(8,128)S(1)}, f32[32,512]{1,0:T(8,128)}, u32[]{:S(2)}) copy-start(f32[32,512]{1,0:T(8,128)} %depth.1) | copy-start | bytes 196612
  1.5 6.0 %copy-start.2 = (f32[32,512]{1,0:T(8,128)S(1)}, f32[32,512]{1,0:T(8,128)}, u32[]{:S(2)}) copy-start(f32[32,512]{1,0:T(8,128)} %turn.1) | copy-start | bytes 196612
  1.5 6.0 %copy-start.3 = (s32[32,512]{1,0:T(8,128)S(1)}, s32[32,512]{1,0:T(8,128)}, u32[]{:S(2)}) copy-start(s32[32,512]{1,0:T(8,128)} %mask.1) | copy-start | bytes 196612
  1.5 6.0 %copy-start.4 = (f32[27]{0:T(128)S(1)}, f32[27]{0:T(128)}, u32[]{:S(2)}) copy-start(f32[27]{0:T(128)} %speed.1) | copy-start | bytes 328
  1.5 9.7 %copy-start.5 = (bf16[864,864]{1,0:T(8,128)(2,1)S(1)}, bf16[864,864]{1,0:T(8,128)(2,1)}, u32[]{:S(2)}) copy-start(bf16[864,864]{1,0:T(8,128)(2,1)} %param.21) | copy-start | bytes 4478980
  1.5 9.7 %copy-start.6 = (bf16[864,864]{1,0:T(8,128)(2,1)S(1)}, bf16[864,864]{1,0:T(8,128)(2,1)}, u32[]{:S(2)}) copy-start(bf16[864,864]{1,0:T(8,128)(2,1)} %param.22) | copy-start | bytes 4478980
  1.5 9.7 %copy-start.7 = (f32[864]{0:T(1024)S(1)}, f32[864]{0:T(1024)}, u32[]{:S(2)}) copy-start(f32[864]{0:T(1024)} %param.19) | copy-start | bytes 10372
  1.5 9.7 %copy-start.8 = (f32[864]{0:T(1024)S(1)}, f32[864]{0:T(1024)}, u32[]{:S(2)}) copy-start(f32[864]{0:T(1024)} %param.20) | copy-start | bytes 10372
  1.5 9.7 %copy-start.9 = (f32[24]{0:T(128)S(1)}, f32[24]{0:T(128)}, u32[]{:S(2)}) copy-start(f32[24]{0:T(128)} %param.18) | copy-start | bytes 292
  1.9 9.3 %collective-permute-start = (f32[2,32,512]{2,1,0:T(8,128)S(1)}, f32[2,32,512]{2,1,0:T(8,128)S(1)}, u32[]{:S(2)}, u32[]{:S(2)}) collective-permute-start(f32[2,32,512]{2,1,0:T(8,128)S(1)} %get-tuple-element.139), channel_id=1, source_target_pairs={{0,1},{2,3},{4,5},{6,7},{1,0},{3,2},{5,4},{7,6},{8,9},{10,11},{12,... | collective-permute-start | bytes 393224 | tf_op jit(solution)/shard_map/ppermute | solution.py:581
  2.0 9.2 %collective-permute-start.1 = (f32[2,32,512]{2,1,0:T(8,128)S(1)}, f32[2,32,512]{2,1,0:T(8,128)S(1)}, u32[]{:S(2)}, u32[]{:S(2)}) collective-permute-start(f32[2,32,512]{2,1,0:T(8,128)S(1)} %get-tuple-element.140), channel_id=1, source_target_pairs={{1,2},{3,4},{5,6},{2,1},{4,3},{6,5},{9,10},{11,12},{13,14},{10,9},... | collective-permute-start | bytes 393224 | tf_op jit(solution)/shard_map/ppermute | solution.py:581

commit v8 on v7

--- a/solution.py
+++ b/solution.py
@@ -545,13 +545,9 @@
 
 
 def finish_kernel(field, out, leaving):
-    copies = []
-    for cb in range(4):
-        part = slice(cb * 8, min(cb * 8 + 8, HELD))
-        copies.append(pltpu.make_async_copy(field.at[part], out.at[part], leaving.at[cb]))
-        copies[cb].start()
-    for copy in copies:
-        copy.wait()
+    copy = pltpu.make_async_copy(field, out, leaving)
+    copy.start()
+    copy.wait()
 
 
 def finish(field):
@@ -560,7 +556,7 @@
         out_shape=jax.ShapeDtypeStruct((HELD, ROWS, COLS), jnp.float32),
         in_specs=[VMEM],
         out_specs=ANY,
-        scratch_shapes=[pltpu.SemaphoreType.DMA((4,))],
+        scratch_shapes=[pltpu.SemaphoreType.DMA],
         compiler_params=PARAMS,
         cost_estimate=pl.CostEstimate(flops=0, bytes_accessed=4000000, transcendentals=0),
         name="finish",

time: 72.2 us -> 72.2 us (level)
  no operation moved by 1% of the time
where the time goes in v8:
time: 72.2 us; the launch traced here: 72 us
  blocking collectives  52 us (72%)
  Pallas kernels  11.7 us (16%)
  starting transfers between devices  5.56 us (8%)
  local copies, waits for them, and re-layouts  1.51 us (2%)
  between operations  1 us (1%)
    all_to_all x2, blocking collectives, exchange(): lax.all_to_all(blocks, 'comp', split_axis=0, concat_axis=0, tiled=True)  52 us
    ppermute x2, starting transfers between devices, swap(): return lax.ppermute(rows, 'tile', pairs + [(j, i) for i, j in pairs])  5.56 us
    pallas_call x1, Pallas kernels, sources(): pl.pallas_call(functools.partial(source_kernel, kind), out_shape=jax.Shap...  3.4 us
    pallas_call x1, Pallas kernels, propagate(): pl.pallas_call(propagate_kernel, out_shape=[jax.ShapeDtypeStruct((ROWS, P...  3.01 us
    pallas_call x1, Pallas kernels, expand(): pl.pallas_call(functools.partial(expand_kernel, kind), out_shape=jax.Shap...  1.84 us
    pallas_call x1, Pallas kernels, compact(): pl.pallas_call(functools.partial(compact_kernel, kind), out_shape=jax.Sha...  1.83 us
    unnamed x20, local copies, waits for them, and re-layouts  1.51 us
  transfers between devices with their start and end apart: 2, of which 0 were waited for; matrix products, arithmetic and copies ran while one was open for 0% of the time, Pallas kernels for 4%

profile of v8, /device:TPU:97, one launch (start us, length us, event | category | flops | bytes accessed | tf_op | source)
XLA Modules:
  0.0 72.0 jit_solution(6509908527583112484)
XLA Ops:
  0.0 0.0 copy-start
  0.0 1.5 %copy-done = f32[27,32,512]{2,1,0:T(8,128)S(1)} copy-done((f32[27,32,512]{2,1,0:T(8,128)S(1)}, f32[27,32,512]{2,1,0:T(8,128)}, u32[]{:S(2)}) %copy-start) | copy-done | bytes 1769496
  1.5 0.0 copy-start.1
  1.5 0.0 copy-start.2
  1.5 0.0 copy-start.3
  1.5 0.0 copy-start.5
  1.5 0.0 copy-start.6
  1.5 0.0 copy-start.7
  1.5 0.0 copy-start.8
  1.5 0.0 copy-start.9
  1.5 0.4 prepare.1
  1.9 0.1 collective-permute-start
  2.0 5.5 %collective-permute-start.1 = (f32[2,32,512]{2,1,0:T(8,128)S(1)}, f32[2,32,512]{2,1,0:T(8,128)S(1)}, u32[]{:S(2)}, u32[]{:S(2)}) collective-permute-start(f32[2,32,512]{2,1,0:T(8,128)S(1)} %get-tuple-element.140), channel_id=1, source_target_pairs={{1,2},{3,4},{5,6},{2,1},{4,3},{6,5},{9,10},{11,12},{13,14},{10,9},... | collective-permute-start | bytes 393224 | tf_op jit(solution)/shard_map/ppermute | solution.py:577
  7.5 0.0 copy-done.1
  7.5 0.0 copy-done.2
  7.5 0.0 copy-done.3
  7.5 0.0 copy-done.4
  7.5 3.0 %propagate.1 = (f32[32,32,512]{2,1,0:T(8,128)S(1)}, f32[4,32,128]{2,1,0:T(8,128)S(1)}, f32[4,512]{1,0:T(4,128)S(1)}, s32[32,512]{1,0:T(8,128)S(1)}, s32[32,512]{...) custom-call(f32[32,32,512]{2,1,0:T(8,128)S(1)} %get-tuple-element.136.grid, f32[32,512]{1,0:T(8,128)S(1)} %copy-done.1, ...), custom_call_target="tpu_custom_call" | custom-call | flops 20000000 | bytes 4000000 | tf_op jit(solution)/shard_map/propagate/pallas_call | solution.py:226
  11.2 0.0 collective-permute-done
  11.2 0.0 collective-permute-done.1
  11.2 0.0 copy-done.5
  11.2 0.0 copy-done.6
  11.2 0.0 copy-done.7
  11.2 0.0 copy-done.8
  11.3 0.0 copy-done.9
  11.3 59.3 %conditional.1 = (f32[27,32,512]{2,1,0:T(8,128)S(1)}) conditional(s32[]{:T(128)} %bitcast, (f32[32,32,512]{2,1,0:T(8,128)S(1)}, f32[2,32,512]{2,1,0:T(8,128)S(1)}, f32[2,32,512]{2,1,0:T(8,128)S(1)}, f32[4,512]{1,0:T(4,128)S(1)}, f32[4,32,128]{2,1,0:T(8,128)S(1)}, /*index=5*/s32[32,512]{1,0:T(8,128)S(1)}, f32[8,512]{1,0:T(8,128)S(1)}, ...), branch_computations={%region_0.0_spmd, %region_1.0_spmd, %region_2.0_spmd} | conditional | flops 1538823680 | bytes 21340040 | solution.py:597
  11.3 1.8 %compact.3 = f32[32,80,128]{2,1,0:T(8,128)S(1)} custom-call(f32[32,32,512]{2,1,0:T(8,128)S(1)} %get-tuple-element.86.mixed, f32[2,32,512]{2,1,0:T(8,128)S(1)} %get-tuple-element.88.from_pair, f32[2,32,512]{2,1,0:T(8,128)S(1)} %get-tuple-element.89.from_other, f32[4,512]{1,0:T(4,128)S(1)} %get-tuple-element.90.edge_depth, ...), custom_call_target="tpu_custom_call" | custom-call | flops 5000000 | bytes 4000000 | tf_op jit(solution)/shard_map/cond/branch_0_fun/compact/pallas_call | solution.py:337
  13.1 28.3 %all_to_all.24.points = f32[32,80,128]{2,1,0:T(8,128)S(1)} all-to-all(f32[32,80,128]{2,1,0:T(8,128)S(1)} %compact.3), channel_id=1, replica_groups=mesh['comp'=32,'tile'=8] {'comp'}, dimensions={0} | all-to-all | bytes 2621440 | tf_op jit(solution)/shard_map/cond/branch_0_fun/all_to_all | solution.py:567
  41.4 3.4 %sources.3 = f32[32,80,128]{2,1,0:T(8,128)S(1)} custom-call(f32[32,80,128]{2,1,0:T(8,128)S(1)} %all_to_all.24.points, f32[8,512]{1,0:T(8,128)S(1)} %get-tuple-element.93.turn_own, f32[24]{0:T(128)S(1)} %get-tuple-element.94.refraction, f32[864]{0:T(1024)S(1)} %get-tuple-element.95.growth, f32[864]{0:T(1024)S(1)} %get-tuple-element.96.dissipation, ...), custom_call_target="tpu_custom_call" | custom-call | flops 1146617856 | bytes 6000000 | tf_op jit(solution)/shard_map/cond/branch_0_fun/sources/pallas_call | solution.py:467
  44.8 23.7 %all_to_all.25.result = f32[32,80,128]{2,1,0:T(8,128)S(1)} all-to-all(f32[32,80,128]{2,1,0:T(8,128)S(1)} %sources.3), channel_id=1, replica_groups=mesh['comp'=32,'tile'=8] {'comp'}, dimensions={0} | all-to-all | bytes 2621440 | tf_op jit(solution)/shard_map/cond/branch_0_fun/all_to_all | solution.py:567
  68.5 1.8 %expand.3 = f32[27,32,512]{2,1,0:T(8,128)S(1)} custom-call(f32[32,80,128]{2,1,0:T(8,128)S(1)} %all_to_all.25.result, s32[32,512]{1,0:T(8,128)S(1)} %get-tuple-element.99.rank), custom_call_target="tpu_custom_call" | custom-call | flops 5000000 | bytes 4000000 | tf_op jit(solution)/shard_map/cond/branch_0_fun/expand/pallas_call | solution.py:535
  70.6 1.2 %finish.1 = f32[27,32,512]{2,1,0:T(8,128)} custom-call(f32[27,32,512]{2,1,0:T(8,128)S(1)} %get-tuple-element.146.field), custom_call_target="tpu_custom_call" | custom-call | bytes 4000000 | tf_op jit(solution)/shard_map/finish/pallas_call | solution.py:554
  (1 shorter events, 0.0 us)
Async XLA Ops:
  0.0 1.5 %copy-start = (f32[27,32,512]{2,1,0:T(8,128)S(1)}, f32[27,32,512]{2,1,0:T(8,128)}, u32[]{:S(2)}) copy-start(f32[27,32,512]{2,1,0:T(8,128)} %spec.1) | copy-start | bytes 5308420
  1.5 6.0 %copy-start.1 = (f32[32,512]{1,0:T(8,128)S(1)}, f32[32,512]{1,0:T(8,128)}, u32[]{:S(2)}) copy-start(f32[32,512]{1,0:T(8,128)} %depth.1) | copy-start | bytes 196612
  1.5 6.0 %copy-start.2 = (f32[32,512]{1,0:T(8,128)S(1)}, f32[32,512]{1,0:T(8,128)}, u32[]{:S(2)}) copy-start(f32[32,512]{1,0:T(8,128)} %turn.1) | copy-start | bytes 196612
  1.5 6.0 %copy-start.3 = (s32[32,512]{1,0:T(8,128)S(1)}, s32[32,512]{1,0:T(8,128)}, u32[]{:S(2)}) copy-start(s32[32,512]{1,0:T(8,128)} %mask.1) | copy-start | bytes 196612
  1.5 6.0 %copy-start.4 = (f32[27]{0:T(128)S(1)}, f32[27]{0:T(128)}, u32[]{:S(2)}) copy-start(f32[27]{0:T(128)} %speed.1) | copy-start | bytes 328
  1.5 9.7 %copy-start.5 = (bf16[864,864]{1,0:T(8,128)(2,1)S(1)}, bf16[864,864]{1,0:T(8,128)(2,1)}, u32[]{:S(2)}) copy-start(bf16[864,864]{1,0:T(8,128)(2,1)} %param.21) | copy-start | bytes 4478980
  1.5 9.7 %copy-start.6 = (bf16[864,864]{1,0:T(8,128)(2,1)S(1)}, bf16[864,864]{1,0:T(8,128)(2,1)}, u32[]{:S(2)}) copy-start(bf16[864,864]{1,0:T(8,128)(2,1)} %param.22) | copy-start | bytes 4478980
  1.5 9.7 %copy-start.7 = (f32[864]{0:T(1024)S(1)}, f32[864]{0:T(1024)}, u32[]{:S(2)}) copy-start(f32[864]{0:T(1024)} %param.19) | copy-start | bytes 10372
  1.5 9.7 %copy-start.8 = (f32[864]{0:T(1024)S(1)}, f32[864]{0:T(1024)}, u32[]{:S(2)}) copy-start(f32[864]{0:T(1024)} %param.20) | copy-start | bytes 10372
  1.5 9.7 %copy-start.9 = (f32[24]{0:T(128)S(1)}, f32[24]{0:T(128)}, u32[]{:S(2)}) copy-start(f32[24]{0:T(128)} %param.18) | copy-start | bytes 292
  1.9 9.3 %collective-permute-start = (f32[2,32,512]{2,1,0:T(8,128)S(1)}, f32[2,32,512]{2,1,0:T(8,128)S(1)}, u32[]{:S(2)}, u32[]{:S(2)}) collective-permute-start(f32[2,32,512]{2,1,0:T(8,128)S(1)} %get-tuple-element.139), channel_id=1, source_target_pairs={{0,1},{2,3},{4,5},{6,7},{1,0},{3,2},{5,4},{7,6},{8,9},{10,11},{12,... | collective-permute-start | bytes 393224 | tf_op jit(solution)/shard_map/ppermute | solution.py:577
  2.0 9.2 %collective-permute-start.1 = (f32[2,32,512]{2,1,0:T(8,128)S(1)}, f32[2,32,512]{2,1,0:T(8,128)S(1)}, u32[]{:S(2)}, u32[]{:S(2)}) collective-permute-start(f32[2,32,512]{2,1,0:T(8,128)S(1)} %get-tuple-element.140), channel_id=1, source_target_pairs={{1,2},{3,4},{5,6},{2,1},{4,3},{6,5},{9,10},{11,12},{13,14},{10,9},... | collective-permute-start | bytes 393224 | tf_op jit(solution)/shard_map/ppermute | solution.py:577
